TPU v7x, 32 devices: a whole 2x2x4 slice. The times are simulated.
32 devices in a mesh: ctx: 8 (over z, y), head: 4 (over x, core).
Axes of the slice: x: 2, y: 2, z: 4, core: 2. Of those that a mesh axis runs over, the one named last changes fastest.
Arguments:
- queries: bfloat16 [16384, 4, 128], P('ctx', 'head'), may hold values from -4 to 4
- keys: bfloat16 [16384, 128], P('ctx'), may hold values from -5 to 5
- values: bfloat16 [16384, 128], P('ctx'), may hold values from -6 to 6
- dout: bfloat16 [16384, 4, 128], P('ctx', 'head'), may hold values from -6 to 6
- selected: int32 [32, 3], P('ctx'), may hold values from 0 to 30, as said below
Outputs:
- grad_queries: bfloat16 [16384, 4, 128], P('ctx', 'head')
- grad_keys: bfloat16 [16384, 128], P('ctx')
- grad_values: bfloat16 [16384, 128], P('ctx')
Inputs may be any that keep to these rules, and one draw needn't show every extreme that they name: `selected`: each entry of row g is either g itself, meaning no block, or an earlier block (below g); the entries of a row that are not g differ; g itself appears only in rows that have fewer than 3 earlier blocks to choose from. Over the 4 rows of one index of ctx, all entries that lie on one other index of ctx (block // 4) name the same block, so one index of ctx reads at most one block from each other index. Every row from 4 on names exactly one block among the first 4. The last row names block 30.
All inputs are finite; a program needn't handle non-finite values.
Results may differ from a plain program's by a relative error of at most 0.015.
Values may be sent and summed in bfloat16 or wider, within the bound.
No kernel may reach another device: no remote copies, remote signals or barrier semaphores. Data moves between devices by JAX's collectives and lax.ppermute only.
A program may use at most 192 MiB of HBM per device.

v0:
```python
import functools
import math

import jax
import jax.numpy as jnp
from jax import lax
from jax.experimental import pallas as pl
from jax.experimental.pallas import tpu as pltpu
from jax.sharding import PartitionSpec as P

F32 = jnp.float32
BF16 = jnp.bfloat16
VMEM_LIMIT = 56 * 1024 * 1024


def dot_nt(a, b):
    return lax.dot_general(a, b, (((1,), (1,)), ((), ())), preferred_element_type=F32)


def dot_nn(a, b):
    return lax.dot_general(a, b, (((1,), (0,)), ((), ())), preferred_element_type=F32)


def slot_of(chosen, blocks_here, row, t):
    ctx_self = lax.axis_index("ctx")
    entry = chosen[row, t]
    owner = lax.div(entry, jnp.int32(blocks_here))
    apart = ctx_self - owner
    slot = jnp.where(apart == 0, entry - owner * blocks_here, blocks_here + apart - 1)
    return jnp.where(entry != ctx_self * blocks_here + row, slot, -1)


def pick_kernel(blocks_here, count, chips, far, piece, chosen, keys, values, asked, *refs):
    outs, sems = refs[:-1], refs[-1]
    ctx_self = lax.axis_index("ctx")
    place = lax.axis_index("head")
    core, chip = lax.rem(place, 2), lax.div(place, 2)
    first = ctx_self * blocks_here
    span = pl.ds(pl.multiple_of(chip * piece, piece), piece)

    def copy(source, s, slot):
        rows = source.at[slot, span, :] if s in far else source.at[slot]
        return pltpu.make_async_copy(rows, outs[s], sems.at[s])

    for s in range(count - 1):
        peer = ctx_self + s + 1
        near = jnp.minimum(peer, count - 1)
        found = jnp.int32(0)
        for row in range(blocks_here):
            for t in range(3):
                entry = chosen[near, row * 3 + t]
                hit = (entry >= first) & (entry < first + blocks_here)
                found = jnp.where(hit, entry - first + 1, found)
        found = jnp.where(peer < count, found, 0)
        asked[s] = found
        slot = jnp.maximum(found - 1, 0)

        @pl.when(core == 0)
        def _():
            copy(keys, s, slot).start()

        @pl.when(core != 0)
        def _():
            copy(values, s, slot).start()

    for s in range(count - 1):
        copy(keys, s, 0).wait()


def chip_sum_kernel(chips, piece, far, near, mine, theirs, *outs):
    chip = lax.div(lax.axis_index("head"), 2)
    for d in range(chips):
        target = lax.rem(chip + d, chips)
        span = pl.ds(pl.multiple_of(target * piece, piece), piece)
        for i, s in enumerate(far):
            total = mine[s, span, :].astype(F32) + theirs[s, span, :].astype(F32)
            outs[d][i] = total.astype(outs[d].dtype)
    for i, s in enumerate(near):
        outs[chips + i][...] = (mine[s].astype(F32) + theirs[s].astype(F32)).astype(BF16)


def own_sum_kernel(chips, piece, near, asked, mine, theirs, *refs):
    back, outs, acc = refs[: len(near)], refs[len(near) : -1], refs[-1]
    chip = lax.div(lax.axis_index("head"), 2)
    acc[...] = mine[...].astype(F32) + theirs[...].astype(F32)
    for i, s in enumerate(near):
        slot = asked[s] - 1

        @pl.when(slot >= 0)
        def _():
            acc[slot] += back[i][...].astype(F32)

    for d in range(chips):
        target = lax.rem(chip + d, chips)
        span = pl.ds(pl.multiple_of(target * piece, piece), piece)
        outs[d][...] = acc[:, span, :].astype(outs[d].dtype)


def head_sum_kernel(count, mine, *refs):
    parts, outs = refs[: len(refs) - count], refs[len(refs) - count :]
    for i in range(count):
        total = mine[i]
        for part in parts:
            total = total + part[i].astype(F32)
        outs[i][...] = total.astype(BF16)


def fold(array, reduce):
    rows, lanes = array.shape
    return reduce(array.reshape(rows // 8, 8, lanes), axis=0)


def causal(array, first_col, first_pos, other):
    col = lax.broadcasted_iota(jnp.int32, array.shape, 0) + first_col
    pos = lax.broadcasted_iota(jnp.int32, array.shape, 1) + first_pos
    return jnp.where(col <= pos, array, other)


def row_sums(s_ref, dp_ref, factor):
    block_len = s_ref.shape[0]
    step = min(64, block_len)
    spans = [pl.ds(c, step) for c in range(0, block_len, step)]
    top = fold(s_ref[spans[0], :], jnp.max)
    for span in spans[1:]:
        top = jnp.maximum(top, fold(s_ref[span, :], jnp.max))
    top = jnp.max(top, axis=0, keepdims=True) * factor
    total = weighted = jnp.zeros((8, block_len), F32)
    for span in spans:
        terms = jnp.exp2(s_ref[span, :] * factor - top)
        total = total + fold(terms, jnp.sum)
        weighted = weighted + fold(terms * dp_ref[span, :], jnp.sum)
    total = jnp.sum(total, axis=0, keepdims=True)
    return top, total, jnp.sum(weighted, axis=0, keepdims=True)


def local_stats_kernel(factor, blocks_here, chosen, q, do, keys, values, stats, s_buf, dp_buf):
    block_len = keys.shape[1]
    half = block_len // 2

    def per_row(row, _):
        start = row * block_len
        span = pl.ds(start, block_len)
        late = pl.ds(start + half, half)

        s_buf[:half, :] = causal(dot_nt(keys[row, :half], q[span, :]), 0, 0, -jnp.inf)
        s_buf[half:, :half] = jnp.full((half, half), -jnp.inf, F32)
        s_buf[half:, half:] = causal(dot_nt(keys[row, half:], q[late, :]), 0, 0, -jnp.inf)
        dp_buf[:half, :] = dot_nt(values[row, :half], do[span, :])
        dp_buf[half:, :half] = jnp.zeros((half, half), F32)
        dp_buf[half:, half:] = dot_nt(values[row, half:], do[late, :])
        top, total, weighted = row_sums(s_buf, dp_buf, factor)
        stats[row, 0:1, :] = top
        stats[row, 1:2, :] = total
        stats[row, 2:3, :] = weighted
        for t in range(3):
            slot = slot_of(chosen, blocks_here, row, t)

            @pl.when((slot >= 0) & (slot < blocks_here))
            def _():
                s_buf[...] = dot_nt(keys[slot], q[span, :])
                dp_buf[...] = dot_nt(values[slot], do[span, :])
                more_top, more, more_weighted = row_sums(s_buf, dp_buf, factor)
                old = stats[row, 0:1, :]
                top = jnp.maximum(old, more_top)
                scale_old = jnp.exp2(old - top)
                scale_new = jnp.exp2(more_top - top)
                stats[row, 0:1, :] = top
                stats[row, 1:2, :] = stats[row, 1:2, :] * scale_old + more * scale_new
                stats[row, 2:3, :] = stats[row, 2:3, :] * scale_old + more_weighted * scale_new

        return 0

    lax.fori_loop(0, blocks_here, per_row, 0)


def remote_kernel(
    factor, scaling, blocks_here, chips, far, near, piece, chosen, q, do, stats, *refs
):
    near_refs, far_refs, refs = refs[:2], refs[2 : 2 + 2 * chips], refs[2 + 2 * chips :]
    keep, send, final, grad_qt, rows, acc, s_buf, dp_buf, parts = refs
    place = lax.axis_index("head")
    core, chip = lax.rem(place, 2), lax.div(place, 2)
    block_len = rows.shape[2]

    def lay(kind, which):
        for i, s in enumerate(near):
            rows[kind, s] = near_refs[which][i]
        for d in range(chips):
            source = lax.rem(chip + chips - d, chips)
            span = pl.ds(pl.multiple_of(source * piece, piece), piece)
            for i, s in enumerate(far):
                rows[kind, s, span, :] = far_refs[2 * d + which][i]

    @pl.when(core == 0)
    def _():
        lay(0, 0)
        lay(1, 1)

    @pl.when(core != 0)
    def _():
        lay(0, 1)
        lay(1, 0)

    acc[...] = jnp.zeros_like(acc)

    def per_row(row, _):
        span = pl.ds(row * block_len, block_len)
        parts[0, 0:3, :] = stats[row, 0:3, :]
        for t in range(3):
            slot = slot_of(chosen, blocks_here, row, t) - blocks_here

            @pl.when(slot >= 0)
            def _():
                s_buf[t] = dot_nt(rows[0, slot], q[span, :])
                dp_buf[t] = dot_nt(rows[1, slot], do[span, :])
                top, total, weighted = row_sums(s_buf.at[t], dp_buf.at[t], factor)
                parts[t + 1, 0:1, :] = top
                parts[t + 1, 1:2, :] = total
                parts[t + 1, 2:3, :] = weighted

            @pl.when(slot < 0)
            def _():
                parts[t + 1, 0:1, :] = jnp.full((1, block_len), -jnp.inf, F32)
                parts[t + 1, 1:3, :] = jnp.zeros((2, block_len), F32)

        top = parts[0, 0:1, :]
        for t in range(3):
            top = jnp.maximum(top, parts[t + 1, 0:1, :])
        total = jnp.zeros_like(top)
        weighted = jnp.zeros_like(top)
        for t in range(4):
            scale = jnp.exp2(parts[t, 0:1, :] - top)
            total = total + scale * parts[t, 1:2, :]
            weighted = weighted + scale * parts[t, 2:3, :]
        final[row, 0:1, :] = top + jnp.log2(total)
        final[row, 1:2, :] = weighted / total
        grad_qt[row] = jnp.zeros_like(grad_qt[row])
        for t in range(3):
            slot = slot_of(chosen, blocks_here, row, t) - blocks_here

            @pl.when(slot >= 0)
            def _():
                level = final[row, 0:1, :]
                delta = final[row, 1:2, :]
                weights = jnp.exp2(s_buf[t] * factor - level)
                dscores = (weights * (dp_buf[t] - delta)).astype(BF16)
                acc[1, slot] += dot_nn(weights.astype(BF16), do[span, :])
                acc[0, slot] += dot_nn(dscores, q[span, :])
                grad_qt[row] += dot_nn(rows[0, slot].T, dscores)

        return 0

    lax.fori_loop(0, blocks_here, per_row, 0)
    keep_scale = jnp.where(core == 0, scaling, 1.0)
    send_scale = jnp.where(core == 0, 1.0, scaling)
    keep[...] = (acc[core] * keep_scale).astype(BF16)
    send[...] = (acc[1 - core] * send_scale).astype(BF16)


def local_kernel(
    factor, scaling, blocks_here, chosen, q, do, keys, values, final, grad_qt,
    keep, send, grad_q,
    acc, total_qt,
):
    core = lax.rem(lax.axis_index("head"), 2)
    block_len = keys.shape[1]
    half = block_len // 2
    acc[...] = jnp.zeros_like(acc)

    def per_row(row, _):
        start = row * block_len
        span = pl.ds(start, block_len)

        def rows_from(ref, first):
            return ref[pl.ds(start + first, block_len - first), :]

        def products(slot, c, first):
            cut = pl.ds(c, half)
            scores = dot_nt(keys[slot, cut, :], rows_from(q, first))
            return scores, dot_nt(values[slot, cut, :], rows_from(do, first))

        def pair(slot, seconds, masked):
            parts = ((0, 0), (half, seconds))
            ready = [products(slot, c, first) for c, first in parts]
            sides = []
            for (c, first), (scores, dprobs) in zip(parts, ready):
                weights = jnp.exp2(scores * factor - final[row, 0:1, first:])
                if masked:
                    weights = causal(weights, c, first, 0.0)
                dscores = (weights * (dprobs - final[row, 1:2, first:])).astype(BF16)
                sides.append((weights.astype(BF16), dscores))
            for (c, first), (weights, dscores) in zip(parts, sides):
                cut = pl.ds(c, half)
                acc[1, slot, cut, :] += dot_nn(weights, rows_from(do, first))
                acc[0, slot, cut, :] += dot_nn(dscores, rows_from(q, first))
                total_qt[:, first:] += dot_nn(keys[slot, cut, :].T, dscores)

        total_qt[...] = grad_qt[row]
        pair(row, half, True)
        for t in range(3):
            slot = slot_of(chosen, blocks_here, row, t)

            @pl.when((slot >= 0) & (slot < blocks_here))
            def _():
                pair(slot, 0, False)

        grad_q[span, :] = (total_qt[...].T * scaling).astype(BF16)
        return 0

    lax.fori_loop(0, blocks_here, per_row, 0)
    keep_scale = jnp.where(core == 0, scaling, 1.0)
    send_scale = jnp.where(core == 0, 1.0, scaling)
    keep[...] = (acc[core] * keep_scale).astype(BF16)
    send[...] = (acc[1 - core] * send_scale).astype(BF16)


def owner_kernel(chips, far, asked, mine, *refs):
    others, back, (out, acc) = refs[: chips - 1], refs[chips - 1 : -2], refs[-2:]
    total = mine[...]
    for part in others:
        total = total + part[...].astype(F32)
    acc[...] = total
    for i, s in enumerate(far):
        slot = asked[s] - 1

        @pl.when(slot >= 0)
        def _():
            acc[slot] += back[i][...].astype(F32)

    out[...] = acc[...].astype(BF16)


def spread_kernel(chips, piece, *refs):
    pieces, (grad_k, grad_v) = refs[: 2 * chips], refs[2 * chips :]
    place = lax.axis_index("head")
    core, chip = lax.rem(place, 2), lax.div(place, 2)

    def lay(out, which):
        for d in range(chips):
            source = lax.rem(chip + chips - d, chips)
            span = pl.ds(pl.multiple_of(source * piece, piece), piece)
            out[:, span, :] = pieces[2 * d + which][...]

    @pl.when(core == 0)
    def _():
        lay(grad_k, 0)
        lay(grad_v, 1)

    @pl.when(core != 0)
    def _():
        lay(grad_k, 1)
        lay(grad_v, 0)


def params(size):
    return pltpu.CompilerParams(vmem_limit_bytes=min(size + 12 * 1024 * 1024, VMEM_LIMIT))


def body(queries, keys, values, dout, selected):
    tok_rows, head_count, feature = queries.shape
    blocks_here = selected.shape[0]
    block_len = tok_rows // blocks_here
    ctx_count = lax.axis_size("ctx")
    heads = lax.axis_size("head")
    chips = heads // 2
    piece = block_len // chips
    scaling = 1.0 / math.sqrt(feature)
    factor = scaling * math.log2(math.e)
    shifts = ctx_count - 1
    far = [s for s in range(shifts) if 2 * (s + 1) >= ctx_count]
    near = [s for s in range(shifts) if 2 * (s + 1) < ctx_count]

    q2 = queries.reshape(tok_rows, feature)
    do2 = dout.reshape(tok_rows, feature)
    key_blocks = keys.reshape(blocks_here, block_len, feature)
    value_blocks = values.reshape(blocks_here, block_len, feature)
    remote_shape = (shifts, block_len, feature)
    local_shape = (blocks_here, block_len, feature)

    smem = pl.BlockSpec(memory_space=pltpu.SMEM)
    whole = pl.BlockSpec(memory_space=pltpu.VMEM)
    hbm = pl.BlockSpec(memory_space=pltpu.HBM)
    stat_type = jax.ShapeDtypeStruct((blocks_here, 8, block_len), F32)
    far_type = jax.ShapeDtypeStruct(remote_shape, BF16)
    own_type = jax.ShapeDtypeStruct(local_shape, BF16)
    block_type = jax.ShapeDtypeStruct((block_len, feature), BF16)
    piece_type = jax.ShapeDtypeStruct((piece, feature), BF16)
    qt_type = jax.ShapeDtypeStruct((blocks_here, feature, block_len), F32)
    pair_flops = 2 * block_len * block_len * feature
    block_bytes = block_len * feature * 2
    pair_bytes = block_len * block_len * 4

    def pieces_type(count, dtype):
        return jax.ShapeDtypeStruct((count, piece, feature), dtype)

    def cost(matmuls, size):
        return pl.CostEstimate(
            flops=matmuls * pair_flops, bytes_accessed=size, transcendentals=matmuls * block_len**2
        )

    def swap(array):
        return lax.ppermute(array, "head", [(h, h ^ 1) for h in range(heads)])

    def to_chip(array, d):
        return lax.ppermute(array, "head", [(h, (h + 2 * d) % heads) for h in range(heads)])

    def to_owner(array, s):
        return lax.ppermute(array, "ctx", [(c, c - s - 1) for c in range(s + 1, ctx_count)])

    def to_reader(array, s):
        return lax.ppermute(array, "ctx", [(c - s - 1, c) for c in range(s + 1, ctx_count)])

    everyone = lax.all_to_all(
        jnp.broadcast_to(selected.reshape(1, 3 * blocks_here), (ctx_count, 3 * blocks_here)),
        "ctx", split_axis=0, concat_axis=0, tiled=True,
    )
    asked, *sent = pl.pallas_call(
        functools.partial(pick_kernel, blocks_here, ctx_count, chips, far, piece),
        in_specs=[smem, hbm, hbm],
        out_specs=[smem] + [whole] * shifts,
        out_shape=[jax.ShapeDtypeStruct((shifts,), jnp.int32)]
        + [piece_type if s in far else block_type for s in range(shifts)],
        scratch_shapes=[pltpu.SemaphoreType.DMA((shifts,))],
        name="pick_rows",
    )(everyone, key_blocks, value_blocks)

    far_mine = jnp.stack([to_reader(sent[s], s) for s in far])
    near_parts = [to_reader(sent[s], s) for s in near]
    far_mine, chosen = lax.optimization_barrier((far_mine, selected))
    far_more = [to_chip(far_mine, d) for d in range(1, chips)]
    stats = pl.pallas_call(
        functools.partial(local_stats_kernel, factor, blocks_here),
        in_specs=[smem] + [whole] * 4,
        out_specs=whole,
        out_shape=stat_type,
        scratch_shapes=[pltpu.VMEM((block_len, block_len), F32)] * 2,
        compiler_params=params(4 * blocks_here * block_bytes + 2 * pair_bytes),
        cost_estimate=cost(30, 4 * tok_rows * feature * 2),
        name="local_stats",
    )(chosen, q2, do2, key_blocks, value_blocks)
    near_parts, far_held, stats = lax.optimization_barrier((near_parts, far_mine, stats))
    near_mine = jnp.stack(near_parts)
    row_sets = [near_mine, swap(near_mine), far_held, swap(far_held)]
    for part in far_more:
        row_sets += [part, swap(part)]

    keep_far, send_far, final, grad_qt = pl.pallas_call(
        functools.partial(remote_kernel, factor, scaling, blocks_here, chips, far, near, piece),
        in_specs=[smem] + [whole] * (3 + len(row_sets)),
        out_specs=[whole] * 4,
        out_shape=[far_type, far_type, stat_type, qt_type],
        scratch_shapes=[
            pltpu.VMEM((2,) + remote_shape, BF16),
            pltpu.VMEM((2,) + remote_shape, F32),
            pltpu.VMEM((3, block_len, block_len), F32),
            pltpu.VMEM((3, block_len, block_len), F32),
            pltpu.VMEM((4, 8, block_len), F32),
        ],
        compiler_params=params((10 * shifts + 4 * blocks_here) * block_bytes + 6 * pair_bytes),
        cost_estimate=cost(60, 8 * tok_rows * feature * 2),
        name="remote_pairs",
    )(chosen, q2, do2, stats, *row_sets)

    def head_sums(mine, parts, count):
        return pl.pallas_call(
            functools.partial(head_sum_kernel, count),
            in_specs=[whole] * (1 + len(parts)),
            out_specs=[whole] * count,
            out_shape=[piece_type] * count,
            compiler_params=params(4 * count * block_bytes),
            name="head_sum",
        )(mine, *parts)

    chip_far = pl.pallas_call(
        functools.partial(chip_sum_kernel, chips, piece, far, near),
        in_specs=[whole, whole],
        out_specs=[whole] * (chips + len(near)),
        out_shape=[pieces_type(len(far), F32)]
        + [pieces_type(len(far), BF16)] * (chips - 1)
        + [block_type] * len(near),
        compiler_params=params(4 * shifts * block_bytes),
        name="chip_sum",
    )(keep_far, swap(send_far))
    chip_far, final = lax.optimization_barrier((chip_far, final))
    far_sums, near_sums = chip_far[:chips], chip_far[chips:]
    far_parts = [to_chip(far_sums[d], d) for d in range(1, chips)]
    near_back = [to_owner(near_sums[i], s) for i, s in enumerate(near)]
    keep_own, send_own, grad_q = pl.pallas_call(
        functools.partial(local_kernel, factor, scaling, blocks_here),
        in_specs=[smem] + [whole] * 6,
        out_specs=[whole] * 3,
        out_shape=[own_type, own_type, jax.ShapeDtypeStruct((tok_rows, feature), BF16)],
        scratch_shapes=[
            pltpu.VMEM((2,) + local_shape, F32),
            pltpu.VMEM((feature, block_len), F32),
        ],
        compiler_params=params(14 * blocks_here * block_bytes),
        cost_estimate=cost(60, 8 * tok_rows * feature * 2),
        name="local_pairs",
    )(chosen, q2, do2, key_blocks, value_blocks, final, grad_qt)
    far_parts, near_back, keep_own, send_own = lax.optimization_barrier(
        (far_parts, near_back, keep_own, send_own)
    )
    own_sums = pl.pallas_call(
        functools.partial(own_sum_kernel, chips, piece, near),
        in_specs=[smem] + [whole] * (2 + len(near)),
        out_specs=[whole] * chips,
        out_shape=[pieces_type(blocks_here, F32)]
        + [pieces_type(blocks_here, BF16)] * (chips - 1),
        scratch_shapes=[pltpu.VMEM(local_shape, F32)],
        compiler_params=params((8 * blocks_here + len(near)) * block_bytes),
        name="own_sum",
    )(asked, keep_own, swap(send_own), *near_back)
    own_parts = [to_chip(own_sums[d], d) for d in range(1, chips)]
    far_out = head_sums(far_sums[0], far_parts, len(far))
    far_back = [to_owner(far_out[i], s) for i, s in enumerate(far)]
    mine = pl.pallas_call(
        functools.partial(owner_kernel, chips, far),
        in_specs=[smem] + [whole] * (chips + len(far)),
        out_specs=whole,
        out_shape=pieces_type(blocks_here, BF16),
        scratch_shapes=[pltpu.VMEM((blocks_here, piece, feature), F32)],
        compiler_params=params((5 * blocks_here + shifts) * block_bytes),
        name="owner_sum",
    )(asked, own_sums[0], *own_parts, *far_back)
    spread = [mine, swap(mine)]
    for d in range(1, chips):
        part = to_chip(mine, d)
        spread += [part, swap(part)]
    grad_keys, grad_values = pl.pallas_call(
        functools.partial(spread_kernel, chips, piece),
        in_specs=[whole] * len(spread),
        out_specs=[whole] * 2,
        out_shape=[own_type] * 2,
        compiler_params=params(4 * blocks_here * block_bytes),
        name="spread",
    )(*spread)
    return (
        grad_q.reshape(tok_rows, head_count, feature),
        grad_keys.reshape(tok_rows, feature),
        grad_values.reshape(tok_rows, feature),
    )


def solution(mesh):
    return jax.shard_map(
        body,
        mesh=mesh,
        in_specs=(
            P("ctx", "head", None),
            P("ctx", None),
            P("ctx", None),
            P("ctx", "head", None),
            P("ctx", None),
        ),
        out_specs=(P("ctx", "head", None), P("ctx", None), P("ctx", None)),
        check_vma=False,
    )
```

profile of v0, /device:TPU:0, one launch (start us, length us, event | category | flops | bytes accessed | tf_op | source)
XLA Modules:
  0.0 101.2 jit_solution(408227548360430289)
XLA Ops:
  0.6 0.8 broadcast_in_dim.7
  1.4 13.6 %all_to_all.8 = s32[8,1,12]{2,1,0:T(1,128)} all-to-all(s32[8,1,12]{2,1,0:T(1,128)S(1)} %broadcast_in_dim.8), channel_id=1, replica_groups=mesh['ctx'=8,'head'=4] {'ctx'}, dimensions={0} | all-to-all | bytes 768 | tf_op jit(solution)/shard_map/all_to_all | solution.py:413
  15.0 2.9 %pick_rows.1 = (s32[7]{0:T(128)}, bf16[512,128]{1,0:T(8,128)(2,1)}, bf16[512,128]{1,0:T(8,128)(2,1)}, bf16[512,128]{1,0:T(8,128)(2,1)}, bf16[256,128]{1,0:T(8,12...) custom-call(s32[8,12]{1,0:T(8,128)} %bitcast.34, ...), custom_call_target="tpu_custom_call" | custom-call | tf_op jit(solution)/shard_map/pick_rows/pallas_call | solution.py:417
  18.0 0.0 copy-start
  18.0 2.6 %collective-permute-start = (bf16[256,128]{1,0:T(8,128)(2,1)}, bf16[256,128]{1,0:T(8,128)(2,1)S(1)}, u32[]{:S(2)}, u32[]{:S(2)}) collective-permute-start(bf16[256,128]{1,0:T(8,128)(2,1)} %get-tuple-element.50), channel_id=1, source_target_pairs={{0,16},{4,20},{8,24},{12,28},{1,17},{5,21},{9,25},{13,29},{2,18},{... | collective-permute-start | bytes 196616 | tf_op jit(solution)/shard_map/ppermute | solution.py:411
  20.6 1.3 %collective-permute-start.1 = (bf16[256,128]{1,0:T(8,128)(2,1)}, bf16[256,128]{1,0:T(8,128)(2,1)S(1)}, u32[]{:S(2)}, u32[]{:S(2)}) collective-permute-start(bf16[256,128]{1,0:T(8,128)(2,1)} %get-tuple-element.51), channel_id=1, source_target_pairs={{0,20},{4,24},{8,28},{1,21},{5,25},{9,29},{2,22},{6,26},{10,30},{3... | collective-permute-start | bytes 196616 | tf_op jit(solution)/shard_map/ppermute | solution.py:411
  22.0 1.4 %collective-permute-start.2 = (bf16[256,128]{1,0:T(8,128)(2,1)}, bf16[256,128]{1,0:T(8,128)(2,1)S(1)}, u32[]{:S(2)}, u32[]{:S(2)}) collective-permute-start(bf16[256,128]{1,0:T(8,128)(2,1)} %get-tuple-element.52), channel_id=1, source_target_pairs={{0,24},{4,28},{1,25},{5,29},{2,26},{6,30},{3,27},{7,31}} | collective-permute-start | bytes 196616 | tf_op jit(solution)/shard_map/ppermute | solution.py:411
  23.3 1.3 %collective-permute-start.3 = (bf16[256,128]{1,0:T(8,128)(2,1)}, bf16[256,128]{1,0:T(8,128)(2,1)S(1)}, u32[]{:S(2)}, u32[]{:S(2)}) collective-permute-start(bf16[256,128]{1,0:T(8,128)(2,1)} %get-tuple-element.53), channel_id=1, source_target_pairs={{0,28},{1,29},{2,30},{3,31}} | collective-permute-start | bytes 196616 | tf_op jit(solution)/shard_map/ppermute | solution.py:411
  24.6 2.7 %collective-permute-start.4 = (bf16[512,128]{1,0:T(8,128)(2,1)}, bf16[512,128]{1,0:T(8,128)(2,1)S(1)}, u32[]{:S(2)}, u32[]{:S(2)}) collective-permute-start(bf16[512,128]{1,0:T(8,128)(2,1)} %get-tuple-element.55), channel_id=1, source_target_pairs={{0,4},{4,8},{8,12},{12,16},{16,20},{20,24},{24,28},{1,5},{5,9},{9,... | collective-permute-start | bytes 393224 | tf_op jit(solution)/shard_map/ppermute | solution.py:411
  27.4 0.0 collective-permute-done
  27.4 1.3 %collective-permute-start.5 = (bf16[512,128]{1,0:T(8,128)(2,1)}, bf16[512,128]{1,0:T(8,128)(2,1)S(1)}, u32[]{:S(2)}, u32[]{:S(2)}) collective-permute-start(bf16[512,128]{1,0:T(8,128)(2,1)} %get-tuple-element.56), channel_id=1, source_target_pairs={{0,8},{4,12},{8,16},{12,20},{16,24},{20,28},{1,9},{5,13},{9,17},{1... | collective-permute-start | bytes 393224 | tf_op jit(solution)/shard_map/ppermute | solution.py:411
  28.7 0.0 collective-permute-done.1
  28.7 2.5 %collective-permute-start.6 = (bf16[512,128]{1,0:T(8,128)(2,1)}, bf16[512,128]{1,0:T(8,128)(2,1)S(1)}, u32[]{:S(2)}, u32[]{:S(2)}) collective-permute-start(bf16[512,128]{1,0:T(8,128)(2,1)} %get-tuple-element.57), channel_id=1, source_target_pairs={{0,12},{4,16},{8,20},{12,24},{16,28},{1,13},{5,17},{9,21},{13,25},... | collective-permute-start | bytes 393224 | tf_op jit(solution)/shard_map/ppermute | solution.py:411
  31.2 0.0 collective-permute-done.2
  31.2 0.0 collective-permute-done.3
  31.2 0.0 copy-start.3
  31.2 1.5 %collective-permute-start.9 = (bf16[4,256,128]{2,1,0:T(8,128)(2,1)S(1)}, bf16[4,256,128]{2,1,0:T(8,128)(2,1)S(1)}, u32[]{:S(2)}, u32[]{:S(2)}) collective-permute-start(bf16[4,256,128]{2,1,0:T(8,128)(2,1)S(1)} %pad_maximum_fusion.1.refs_2_), channel_id=1, source_target_pairs={{0,2},{1,3},{2,0},{3,1},{4,6},{5,7},{6,4},{7,5},{8,10},{9,11},{10,... | collective-permute-start | bytes 786440 | tf_op jit(solution)/shard_map/ppermute | solution.py:405
  32.8 0.0 copy-start.5
  32.8 1.0 %copy-done.5 = bf16[2048,1,128]{2,0,1:T(8,128)(2,1)S(1)} copy-done((bf16[2048,1,128]{2,0,1:T(8,128)(2,1)S(1)}, bf16[2048,1,128]{2,0,1:T(8,128)(2,1)}, u32[]{:S(2)}) %copy-start.5) | copy-done | bytes 524312
  33.9 5.7 %local_stats.1.stats = f32[4,8,512]{2,1,0:T(8,128)S(1)} custom-call(s32[4,3]{1,0:T(4,128)S(1)} %copy-done.3, bf16[2048,128]{1,0:T(8,128)(2,1)S(1)} %bitcast.21, bf16[2048,128]{1,0:T(8,128)(2,1)S(1)} %bitcast.24, bf16[4,512,128]{2,1,0:T(8,128)(2,1)S(1)} %bitcast.16, bf16[4,512,128]{2,1,0:T(8,128)(2,1)S(1)} %bitcast.19), custom_call_target="tpu_custom_call" | custom-call | flops 2013265920 | bytes 2097152 | tf_op jit(solution)/shard_map/local_stats/pallas_call | solution.py:431
  39.6 0.0 copy-start.6
  39.6 0.0 collective-permute-done.4
  39.6 0.0 collective-permute-done.5
  39.6 0.0 collective-permute-done.6
  39.7 0.1 collective-permute-start.7
  39.8 0.5 collective-permute-start.8
  40.3 0.0 collective-permute-done.9.refs_4_
  40.3 0.1 collective-permute-start.10
  40.4 1.5 %collective-permute-done.8.refs_3_ = bf16[4,256,128]{2,1,0:T(8,128)(2,1)S(1)} collective-permute-done((bf16[4,256,128]{2,1,0:T(8,128)(2,1)S(1)}, bf16[4,256,128]{2,1,0:T(8,128)(2,1)S(1)}, u32[]{:S(2)}, u32[]{:S(2)}) %collective-permute-start.8) | collective-permute-done | bytes 262176 | tf_op jit(solution)/shard_map/ppermute | solution.py:402
  41.9 0.0 collective-permute-done.7.refs_1_
  41.9 0.4 collective-permute-done.10.refs_5_
  42.2 1.6 %remote_pairs.1 = (bf16[7,512,128]{2,1,0:T(8,128)(2,1)S(1)}, bf16[7,512,128]{2,1,0:T(8,128)(2,1)S(1)}, f32[4,8,512]{2,1,0:T(8,128)S(1)}, f32[4,128,512]{2,1,0:T(8,128)S(1)}) custom-call(s32[4,3]{1,0:T(4,128)S(1)} %copy-done.3, bf16[2048,128]{1,0:T(8,128)(2,1)S(1)} %bitcast.22, bf16[2048,128]{1,0:T(8,128)(2,1)S(1)} %bitcast.25, ...), custom_call_target="tpu_custom_call" | custom-call | flops 4026531840 | bytes 4194304 | tf_op jit(solution)/shard_map/remote_pairs/pallas_call | solution.py:447
  43.8 0.2 collective-permute-start.11
  44.0 2.3 %collective-permute-done.11.theirs = bf16[7,512,128]{2,1,0:T(8,128)(2,1)S(1)} collective-permute-done((bf16[7,512,128]{2,1,0:T(8,128)(2,1)S(1)}, bf16[7,512,128]{2,1,0:T(8,128)(2,1)S(1)}, u32[]{:S(2)}, u32[]{:S(2)}) %collective-permute-start.11) | collective-permute-done | bytes 917536 | tf_op jit(solution)/shard_map/ppermute | solution.py:402
  46.3 0.2 chip_sum.1
  46.5 1.3 %collective-permute-start.13 = (bf16[512,128]{1,0:T(8,128)(2,1)S(1)}, bf16[512,128]{1,0:T(8,128)(2,1)S(1)}, u32[]{:S(2)}, u32[]{:S(2)}) collective-permute-start(bf16[512,128]{1,0:T(8,128)(2,1)S(1)} %get-tuple-element.77), channel_id=1, source_target_pairs={{4,0},{8,4},{12,8},{16,12},{20,16},{24,20},{28,24},{5,1},{9,5},{13... | collective-permute-start | bytes 393224 | tf_op jit(solution)/shard_map/ppermute | solution.py:408
  47.8 1.3 %collective-permute-start.14 = (bf16[512,128]{1,0:T(8,128)(2,1)S(1)}, bf16[512,128]{1,0:T(8,128)(2,1)S(1)}, u32[]{:S(2)}, u32[]{:S(2)}) collective-permute-start(bf16[512,128]{1,0:T(8,128)(2,1)S(1)} %get-tuple-element.78), channel_id=1, source_target_pairs={{8,0},{12,4},{16,8},{20,12},{24,16},{28,20},{9,1},{13,5},{17,9},{2... | collective-permute-start | bytes 393224 | tf_op jit(solution)/shard_map/ppermute | solution.py:408
  49.1 1.3 %collective-permute-start.15 = (bf16[512,128]{1,0:T(8,128)(2,1)S(1)}, bf16[512,128]{1,0:T(8,128)(2,1)S(1)}, u32[]{:S(2)}, u32[]{:S(2)}) collective-permute-start(bf16[512,128]{1,0:T(8,128)(2,1)S(1)} %get-tuple-element.79), channel_id=1, source_target_pairs={{12,0},{16,4},{20,8},{24,12},{28,16},{13,1},{17,5},{21,9},{25,13},... | collective-permute-start | bytes 393224 | tf_op jit(solution)/shard_map/ppermute | solution.py:408
  50.4 0.7 collective-permute-start.12
  51.1 9.4 %local_pairs.1 = (bf16[4,512,128]{2,1,0:T(8,128)(2,1)S(1)}, bf16[4,512,128]{2,1,0:T(8,128)(2,1)S(1)}, bf16[2048,128]{1,0:T(8,128)(2,1)}) custom-call(s32[4,3]{1,0:T(4,128)S(1)} %copy-done.3, bf16[2048,128]{1,0:T(8,128)(2,1)S(1)} %bitcast.23, bf16[2048,128]{1,0:T(8,128)(2,1)S(1)} %bitcast.26, bf16[4,512,128]{2,1,0:T(8,128)(2,1)S(1)} %bitcast.17, ...), custom_call_target="tpu_custom_call" | custom-call | flops 4026531840 | bytes 4194304 | tf_op jit(solution)/shard_map/local_pairs/pallas_call | solution.py:488
  60.5 0.1 collective-permute-done.13.refs_0_
  60.6 4.0 %collective-permute-done.14.refs_1_ = bf16[512,128]{1,0:T(8,128)(2,1)S(1)} collective-permute-done((bf16[512,128]{1,0:T(8,128)(2,1)S(1)}, bf16[512,128]{1,0:T(8,128)(2,1)S(1)}, u32[]{:S(2)}, u32[]{:S(2)}) %collective-permute-start.14) | collective-permute-done | bytes 131104 | tf_op jit(solution)/shard_map/ppermute | solution.py:408
  64.6 4.3 %collective-permute-done.15.refs_2_ = bf16[512,128]{1,0:T(8,128)(2,1)S(1)} collective-permute-done((bf16[512,128]{1,0:T(8,128)(2,1)S(1)}, bf16[512,128]{1,0:T(8,128)(2,1)S(1)}, u32[]{:S(2)}, u32[]{:S(2)}) %collective-permute-start.15) | collective-permute-done | bytes 131104 | tf_op jit(solution)/shard_map/ppermute | solution.py:408
  68.9 0.0 collective-permute-done.12.refs_0_
  68.9 1.9 %collective-permute-done.16.theirs = bf16[4,512,128]{2,1,0:T(8,128)(2,1)S(1)} collective-permute-done((bf16[4,512,128]{2,1,0:T(8,128)(2,1)S(1)}, bf16[4,512,128]{2,1,0:T(8,128)(2,1)S(1)}, u32[]{:S(2)}, u32[]{:S(2)}) %collective-permute-start.16) | collective-permute-done | bytes 524320 | tf_op jit(solution)/shard_map/ppermute | solution.py:402
  70.8 0.8 own_sum.1
  71.6 0.8 collective-permute-start.17
  72.4 1.3 %collective-permute-start.18 = (bf16[256,128]{1,0:T(8,128)(2,1)S(1)}, bf16[256,128]{1,0:T(8,128)(2,1)S(1)}, u32[]{:S(2)}, u32[]{:S(2)}) collective-permute-start(bf16[256,128]{1,0:T(8,128)(2,1)S(1)} %get-tuple-element.91), channel_id=1, source_target_pairs={{16,0},{20,4},{24,8},{28,12},{17,1},{21,5},{25,9},{29,13},{18,2},{... | collective-permute-start | bytes 196616 | tf_op jit(solution)/shard_map/ppermute | solution.py:408
  73.7 1.3 %collective-permute-start.19 = (bf16[256,128]{1,0:T(8,128)(2,1)S(1)}, bf16[256,128]{1,0:T(8,128)(2,1)S(1)}, u32[]{:S(2)}, u32[]{:S(2)}) collective-permute-start(bf16[256,128]{1,0:T(8,128)(2,1)S(1)} %get-tuple-element.92), channel_id=1, source_target_pairs={{20,0},{24,4},{28,8},{21,1},{25,5},{29,9},{22,2},{26,6},{30,10},{2... | collective-permute-start | bytes 196616 | tf_op jit(solution)/shard_map/ppermute | solution.py:408
  75.0 1.3 %collective-permute-start.20 = (bf16[256,128]{1,0:T(8,128)(2,1)S(1)}, bf16[256,128]{1,0:T(8,128)(2,1)S(1)}, u32[]{:S(2)}, u32[]{:S(2)}) collective-permute-start(bf16[256,128]{1,0:T(8,128)(2,1)S(1)} %get-tuple-element.93), channel_id=1, source_target_pairs={{24,0},{28,4},{25,1},{29,5},{26,2},{30,6},{27,3},{31,7}} | collective-permute-start | bytes 196616 | tf_op jit(solution)/shard_map/ppermute | solution.py:408
  76.3 1.3 %collective-permute-start.21 = (bf16[256,128]{1,0:T(8,128)(2,1)S(1)}, bf16[256,128]{1,0:T(8,128)(2,1)S(1)}, u32[]{:S(2)}, u32[]{:S(2)}) collective-permute-start(bf16[256,128]{1,0:T(8,128)(2,1)S(1)} %get-tuple-element.94), channel_id=1, source_target_pairs={{28,0},{29,1},{30,2},{31,3}} | collective-permute-start | bytes 196616 | tf_op jit(solution)/shard_map/ppermute | solution.py:408
  77.6 5.1 %collective-permute-done.18.refs_1_ = bf16[256,128]{1,0:T(8,128)(2,1)S(1)} collective-permute-done((bf16[256,128]{1,0:T(8,128)(2,1)S(1)}, bf16[256,128]{1,0:T(8,128)(2,1)S(1)}, u32[]{:S(2)}, u32[]{:S(2)}) %collective-permute-start.18) | collective-permute-done | bytes 65568 | tf_op jit(solution)/shard_map/ppermute | solution.py:408
  82.7 5.1 %collective-permute-done.19.refs_2_ = bf16[256,128]{1,0:T(8,128)(2,1)S(1)} collective-permute-done((bf16[256,128]{1,0:T(8,128)(2,1)S(1)}, bf16[256,128]{1,0:T(8,128)(2,1)S(1)}, u32[]{:S(2)}, u32[]{:S(2)}) %collective-permute-start.19) | collective-permute-done | bytes 65568 | tf_op jit(solution)/shard_map/ppermute | solution.py:408
  87.8 1.0 %collective-permute-done.20.refs_3_ = bf16[256,128]{1,0:T(8,128)(2,1)S(1)} collective-permute-done((bf16[256,128]{1,0:T(8,128)(2,1)S(1)}, bf16[256,128]{1,0:T(8,128)(2,1)S(1)}, u32[]{:S(2)}, u32[]{:S(2)}) %collective-permute-start.20) | collective-permute-done | bytes 65568 | tf_op jit(solution)/shard_map/ppermute | solution.py:408
  88.9 1.3 %collective-permute-done.21.refs_4_ = bf16[256,128]{1,0:T(8,128)(2,1)S(1)} collective-permute-done((bf16[256,128]{1,0:T(8,128)(2,1)S(1)}, bf16[256,128]{1,0:T(8,128)(2,1)S(1)}, u32[]{:S(2)}, u32[]{:S(2)}) %collective-permute-start.21) | collective-permute-done | bytes 65568 | tf_op jit(solution)/shard_map/ppermute | solution.py:408
  90.2 0.0 collective-permute-done.17.refs_0_
  90.2 0.7 owner_sum.1.refs_0_
  90.9 1.4 %collective-permute-start.23 = (bf16[4,256,128]{2,1,0:T(8,128)(2,1)S(1)}, bf16[4,256,128]{2,1,0:T(8,128)(2,1)S(1)}, u32[]{:S(2)}, u32[]{:S(2)}) collective-permute-start(bf16[4,256,128]{2,1,0:T(8,128)(2,1)S(1)} %owner_sum.1.refs_0_), channel_id=1, source_target_pairs={{0,2},{1,3},{2,0},{3,1},{4,6},{5,7},{6,4},{7,5},{8,10},{9,11},{10,... | collective-permute-start | bytes 786440 | tf_op jit(solution)/shard_map/ppermute | solution.py:405
  92.2 0.0 collective-permute-start.22
  92.2 6.4 %collective-permute-done.23.refs_2_ = bf16[4,256,128]{2,1,0:T(8,128)(2,1)S(1)} collective-permute-done((bf16[4,256,128]{2,1,0:T(8,128)(2,1)S(1)}, bf16[4,256,128]{2,1,0:T(8,128)(2,1)S(1)}, u32[]{:S(2)}, u32[]{:S(2)}) %collective-permute-start.23) | collective-permute-done | bytes 262176 | tf_op jit(solution)/shard_map/ppermute | solution.py:405
  98.6 0.0 collective-permute-start.24
  98.6 0.0 collective-permute-done.22.refs_1_
  98.6 1.5 %collective-permute-done.24.refs_3_ = bf16[4,256,128]{2,1,0:T(8,128)(2,1)S(1)} collective-permute-done((bf16[4,256,128]{2,1,0:T(8,128)(2,1)S(1)}, bf16[4,256,128]{2,1,0:T(8,128)(2,1)S(1)}, u32[]{:S(2)}, u32[]{:S(2)}) %collective-permute-start.24) | collective-permute-done | bytes 262176 | tf_op jit(solution)/shard_map/ppermute | solution.py:402
  100.2 1.0 %spread.1 = (bf16[4,512,128]{2,1,0:T(8,128)(2,1)}, bf16[4,512,128]{2,1,0:T(8,128)(2,1)}) custom-call(bf16[4,256,128]{2,1,0:T(8,128)(2,1)S(1)} %owner_sum.1.refs_0_, bf16[4,256,128]{2,1,0:T(8,128)(2,1)S(1)} %collective-permute-done.22.refs_1_, bf16[4,256,128]{2,1,0:T(8,128)(2,1)S(1)} %collective-permute-done.23.refs_2_, ...), custom_call_target="tpu_custom_call" | custom-call | tf_op jit(solution)/shard_map/spread/pallas_call | solution.py:530
  (14 shorter events, 0.2 us)
Async XLA Ops:
  15.0 17.8 %copy-start.1 = (bf16[2048,128]{1,0:T(8,128)(2,1)S(1)}, bf16[2048,128]{1,0:T(8,128)(2,1)}, u32[]{:S(2)}) copy-start(bf16[2048,128]{1,0:T(8,128)(2,1)} %param.7) | copy-start | bytes 1572868
  15.0 17.8 %copy-start.4 = (bf16[2048,1,128]{2,0,1:T(8,128)(2,1)S(1)}, bf16[2048,1,128]{2,0,1:T(8,128)(2,1)}, u32[]{:S(2)}) copy-start(bf16[2048,1,128]{2,0,1:T(8,128)(2,1)} %param.5) | copy-start | bytes 1572868
  18.0 14.8 %copy-start = (bf16[2048,128]{1,0:T(8,128)(2,1)S(1)}, bf16[2048,128]{1,0:T(8,128)(2,1)}, u32[]{:S(2)}) copy-start(bf16[2048,128]{1,0:T(8,128)(2,1)} %param.6) | copy-start | bytes 1572868
  18.0 9.4 %collective-permute-start = (bf16[256,128]{1,0:T(8,128)(2,1)}, bf16[256,128]{1,0:T(8,128)(2,1)S(1)}, u32[]{:S(2)}, u32[]{:S(2)}) collective-permute-start(bf16[256,128]{1,0:T(8,128)(2,1)} %get-tuple-element.50), channel_id=1, source_target_pairs={{0,16},{4,20},{8,24},{12,28},{1,17},{5,21},{9,25},{13,29},{2,18},{... | collective-permute-start | bytes 196616 | tf_op jit(solution)/shard_map/ppermute | solution.py:411
  20.6 8.1 %collective-permute-start.1 = (bf16[256,128]{1,0:T(8,128)(2,1)}, bf16[256,128]{1,0:T(8,128)(2,1)S(1)}, u32[]{:S(2)}, u32[]{:S(2)}) collective-permute-start(bf16[256,128]{1,0:T(8,128)(2,1)} %get-tuple-element.51), channel_id=1, source_target_pairs={{0,20},{4,24},{8,28},{1,21},{5,25},{9,29},{2,22},{6,26},{10,30},{3... | collective-permute-start | bytes 196616 | tf_op jit(solution)/shard_map/ppermute | solution.py:411
  22.0 9.2 %collective-permute-start.2 = (bf16[256,128]{1,0:T(8,128)(2,1)}, bf16[256,128]{1,0:T(8,128)(2,1)S(1)}, u32[]{:S(2)}, u32[]{:S(2)}) collective-permute-start(bf16[256,128]{1,0:T(8,128)(2,1)} %get-tuple-element.52), channel_id=1, source_target_pairs={{0,24},{4,28},{1,25},{5,29},{2,26},{6,30},{3,27},{7,31}} | collective-permute-start | bytes 196616 | tf_op jit(solution)/shard_map/ppermute | solution.py:411
  23.3 7.9 %collective-permute-start.3 = (bf16[256,128]{1,0:T(8,128)(2,1)}, bf16[256,128]{1,0:T(8,128)(2,1)S(1)}, u32[]{:S(2)}, u32[]{:S(2)}) collective-permute-start(bf16[256,128]{1,0:T(8,128)(2,1)} %get-tuple-element.53), channel_id=1, source_target_pairs={{0,28},{1,29},{2,30},{3,31}} | collective-permute-start | bytes 196616 | tf_op jit(solution)/shard_map/ppermute | solution.py:411
  24.6 15.0 %collective-permute-start.4 = (bf16[512,128]{1,0:T(8,128)(2,1)}, bf16[512,128]{1,0:T(8,128)(2,1)S(1)}, u32[]{:S(2)}, u32[]{:S(2)}) collective-permute-start(bf16[512,128]{1,0:T(8,128)(2,1)} %get-tuple-element.55), channel_id=1, source_target_pairs={{0,4},{4,8},{8,12},{12,16},{16,20},{20,24},{24,28},{1,5},{5,9},{9,... | collective-permute-start | bytes 393224 | tf_op jit(solution)/shard_map/ppermute | solution.py:411
  27.4 12.2 %collective-permute-start.5 = (bf16[512,128]{1,0:T(8,128)(2,1)}, bf16[512,128]{1,0:T(8,128)(2,1)S(1)}, u32[]{:S(2)}, u32[]{:S(2)}) collective-permute-start(bf16[512,128]{1,0:T(8,128)(2,1)} %get-tuple-element.56), channel_id=1, source_target_pairs={{0,8},{4,12},{8,16},{12,20},{16,24},{20,28},{1,9},{5,13},{9,17},{1... | collective-permute-start | bytes 393224 | tf_op jit(solution)/shard_map/ppermute | solution.py:411
  28.7 10.9 %collective-permute-start.6 = (bf16[512,128]{1,0:T(8,128)(2,1)}, bf16[512,128]{1,0:T(8,128)(2,1)S(1)}, u32[]{:S(2)}, u32[]{:S(2)}) collective-permute-start(bf16[512,128]{1,0:T(8,128)(2,1)} %get-tuple-element.57), channel_id=1, source_target_pairs={{0,12},{4,16},{8,20},{12,24},{16,28},{1,13},{5,17},{9,21},{13,25},... | collective-permute-start | bytes 393224 | tf_op jit(solution)/shard_map/ppermute | solution.py:411
  31.2 1.6 %copy-start.3 = (s32[4,3]{1,0:T(4,128)S(1)}, s32[4,3]{1,0:T(4,128)}, u32[]{:S(2)}) copy-start(s32[4,3]{1,0:T(4,128)} %chosen.2) | copy-start | bytes 148
  31.2 9.0 %collective-permute-start.9 = (bf16[4,256,128]{2,1,0:T(8,128)(2,1)S(1)}, bf16[4,256,128]{2,1,0:T(8,128)(2,1)S(1)}, u32[]{:S(2)}, u32[]{:S(2)}) collective-permute-start(bf16[4,256,128]{2,1,0:T(8,128)(2,1)S(1)} %pad_maximum_fusion.1.refs_2_), channel_id=1, source_target_pairs={{0,2},{1,3},{2,0},{3,1},{4,6},{5,7},{6,4},{7,5},{8,10},{9,11},{10,... | collective-permute-start | bytes 786440 | tf_op jit(solution)/shard_map/ppermute | solution.py:405
  32.8 1.0 %copy-start.5 = (bf16[2048,1,128]{2,0,1:T(8,128)(2,1)S(1)}, bf16[2048,1,128]{2,0,1:T(8,128)(2,1)}, u32[]{:S(2)}) copy-start(bf16[2048,1,128]{2,0,1:T(8,128)(2,1)} %param.8) | copy-start | bytes 1572868
  39.6 2.6 %copy-start.6 = (bf16[2048,1,128]{2,0,1:T(8,128)(2,1)S(1)}, bf16[2048,1,128]{2,0,1:T(8,128)(2,1)}, u32[]{:S(2)}) copy-start(bf16[2048,1,128]{2,0,1:T(8,128)(2,1)} %param.8) | copy-start | bytes 1572868
  39.7 2.2 %collective-permute-start.7 = (bf16[3,512,128]{2,1,0:T(8,128)(2,1)S(1)}, bf16[3,512,128]{2,1,0:T(8,128)(2,1)S(1)}, u32[]{:S(2)}, u32[]{:S(2)}) collective-permute-start(bf16[3,512,128]{2,1,0:T(8,128)(2,1)S(1)} %pad_maximum_fusion.refs_0_), channel_id=1, source_target_pairs={{0,1},{1,0},{2,3},{3,2},{4,5},{5,4},{6,7},{7,6},{8,9},{9,8},{10,11... | collective-permute-start | bytes 1179656 | tf_op jit(solution)/shard_map/ppermute | solution.py:402
  39.8 2.1 %collective-permute-start.8 = (bf16[4,256,128]{2,1,0:T(8,128)(2,1)S(1)}, bf16[4,256,128]{2,1,0:T(8,128)(2,1)S(1)}, u32[]{:S(2)}, u32[]{:S(2)}) collective-permute-start(bf16[4,256,128]{2,1,0:T(8,128)(2,1)S(1)} %pad_maximum_fusion.1.refs_2_), channel_id=1, source_target_pairs={{0,1},{1,0},{2,3},{3,2},{4,5},{5,4},{6,7},{7,6},{8,9},{9,8},{10,11... | collective-permute-start | bytes 786440 | tf_op jit(solution)/shard_map/ppermute | solution.py:402
  40.3 2.0 %collective-permute-start.10 = (bf16[4,256,128]{2,1,0:T(8,128)(2,1)S(1)}, bf16[4,256,128]{2,1,0:T(8,128)(2,1)S(1)}, u32[]{:S(2)}, u32[]{:S(2)}) collective-permute-start(bf16[4,256,128]{2,1,0:T(8,128)(2,1)S(1)} %collective-permute-done.9.refs_4_), channel_id=1, source_target_pairs={{0,1},{1,0},{2,3},{3,2},{4,5},{5,4},{6,7},{7,6},{8,9},{9,8},{10,11... | collective-permute-start | bytes 786440 | tf_op jit(solution)/shard_map/ppermute | solution.py:402
  43.8 2.5 %collective-permute-start.11 = (bf16[7,512,128]{2,1,0:T(8,128)(2,1)S(1)}, bf16[7,512,128]{2,1,0:T(8,128)(2,1)S(1)}, u32[]{:S(2)}, u32[]{:S(2)}) collective-permute-start(bf16[7,512,128]{2,1,0:T(8,128)(2,1)S(1)} %get-tuple-element.65), channel_id=1, source_target_pairs={{0,1},{1,0},{2,3},{3,2},{4,5},{5,4},{6,7},{7,6},{8,9},{9,8},{10,11... | collective-permute-start | bytes 2752520 | tf_op jit(solution)/shard_map/ppermute | solution.py:402
  46.5 14.1 %collective-permute-start.13 = (bf16[512,128]{1,0:T(8,128)(2,1)S(1)}, bf16[512,128]{1,0:T(8,128)(2,1)S(1)}, u32[]{:S(2)}, u32[]{:S(2)}) collective-permute-start(bf16[512,128]{1,0:T(8,128)(2,1)S(1)} %get-tuple-element.77), channel_id=1, source_target_pairs={{4,0},{8,4},{12,8},{16,12},{20,16},{24,20},{28,24},{5,1},{9,5},{13... | collective-permute-start | bytes 393224 | tf_op jit(solution)/shard_map/ppermute | solution.py:408
  47.8 16.7 %collective-permute-start.14 = (bf16[512,128]{1,0:T(8,128)(2,1)S(1)}, bf16[512,128]{1,0:T(8,128)(2,1)S(1)}, u32[]{:S(2)}, u32[]{:S(2)}) collective-permute-start(bf16[512,128]{1,0:T(8,128)(2,1)S(1)} %get-tuple-element.78), channel_id=1, source_target_pairs={{8,0},{12,4},{16,8},{20,12},{24,16},{28,20},{9,1},{13,5},{17,9},{2... | collective-permute-start | bytes 393224 | tf_op jit(solution)/shard_map/ppermute | solution.py:408
  49.1 19.8 %collective-permute-start.15 = (bf16[512,128]{1,0:T(8,128)(2,1)S(1)}, bf16[512,128]{1,0:T(8,128)(2,1)S(1)}, u32[]{:S(2)}, u32[]{:S(2)}) collective-permute-start(bf16[512,128]{1,0:T(8,128)(2,1)S(1)} %get-tuple-element.79), channel_id=1, source_target_pairs={{12,0},{16,4},{20,8},{24,12},{28,16},{13,1},{17,5},{21,9},{25,13},... | collective-permute-start | bytes 393224 | tf_op jit(solution)/shard_map/ppermute | solution.py:408
  50.4 18.5 %collective-permute-start.12 = (bf16[4,256,128]{2,1,0:T(8,128)(2,1)S(1)}, bf16[4,256,128]{2,1,0:T(8,128)(2,1)S(1)}, u32[]{:S(2)}, u32[]{:S(2)}) collective-permute-start(bf16[4,256,128]{2,1,0:T(8,128)(2,1)S(1)} %get-tuple-element.76), channel_id=1, source_target_pairs={{0,2},{1,3},{2,0},{3,1},{4,6},{5,7},{6,4},{7,5},{8,10},{9,11},{10,... | collective-permute-start | bytes 786440 | tf_op jit(solution)/shard_map/ppermute | solution.py:405
  68.9 1.9 %copy-start.2 = (s32[7]{0:T(128)S(1)}, s32[7]{0:T(128)}, u32[]{:S(2)}) copy-start(s32[7]{0:T(128)} %get-tuple-element.75.asked) | copy-start | bytes 88
  68.9 1.9 %collective-permute-start.16 = (bf16[4,512,128]{2,1,0:T(8,128)(2,1)S(1)}, bf16[4,512,128]{2,1,0:T(8,128)(2,1)S(1)}, u32[]{:S(2)}, u32[]{:S(2)}) collective-permute-start(bf16[4,512,128]{2,1,0:T(8,128)(2,1)S(1)} %get-tuple-element.83), channel_id=1, source_target_pairs={{0,1},{1,0},{2,3},{3,2},{4,5},{5,4},{6,7},{7,6},{8,9},{9,8},{10,11... | collective-permute-start | bytes 1572872 | tf_op jit(solution)/shard_map/ppermute | solution.py:402
  71.6 18.5 %collective-permute-start.17 = (bf16[4,256,128]{2,1,0:T(8,128)(2,1)S(1)}, bf16[4,256,128]{2,1,0:T(8,128)(2,1)S(1)}, u32[]{:S(2)}, u32[]{:S(2)}) collective-permute-start(bf16[4,256,128]{2,1,0:T(8,128)(2,1)S(1)} %get-tuple-element.88), channel_id=1, source_target_pairs={{0,2},{1,3},{2,0},{3,1},{4,6},{5,7},{6,4},{7,5},{8,10},{9,11},{10,... | collective-permute-start | bytes 786440 | tf_op jit(solution)/shard_map/ppermute | solution.py:405
  72.4 10.3 %collective-permute-start.18 = (bf16[256,128]{1,0:T(8,128)(2,1)S(1)}, bf16[256,128]{1,0:T(8,128)(2,1)S(1)}, u32[]{:S(2)}, u32[]{:S(2)}) collective-permute-start(bf16[256,128]{1,0:T(8,128)(2,1)S(1)} %get-tuple-element.91), channel_id=1, source_target_pairs={{16,0},{20,4},{24,8},{28,12},{17,1},{21,5},{25,9},{29,13},{18,2},{... | collective-permute-start | bytes 196616 | tf_op jit(solution)/shard_map/ppermute | solution.py:408
  73.7 14.1 %collective-permute-start.19 = (bf16[256,128]{1,0:T(8,128)(2,1)S(1)}, bf16[256,128]{1,0:T(8,128)(2,1)S(1)}, u32[]{:S(2)}, u32[]{:S(2)}) collective-permute-start(bf16[256,128]{1,0:T(8,128)(2,1)S(1)} %get-tuple-element.92), channel_id=1, source_target_pairs={{20,0},{24,4},{28,8},{21,1},{25,5},{29,9},{22,2},{26,6},{30,10},{2... | collective-permute-start | bytes 196616 | tf_op jit(solution)/shard_map/ppermute | solution.py:408
  75.0 13.8 %collective-permute-start.20 = (bf16[256,128]{1,0:T(8,128)(2,1)S(1)}, bf16[256,128]{1,0:T(8,128)(2,1)S(1)}, u32[]{:S(2)}, u32[]{:S(2)}) collective-permute-start(bf16[256,128]{1,0:T(8,128)(2,1)S(1)} %get-tuple-element.93), channel_id=1, source_target_pairs={{24,0},{28,4},{25,1},{29,5},{26,2},{30,6},{27,3},{31,7}} | collective-permute-start | bytes 196616 | tf_op jit(solution)/shard_map/ppermute | solution.py:408
  76.3 13.8 %collective-permute-start.21 = (bf16[256,128]{1,0:T(8,128)(2,1)S(1)}, bf16[256,128]{1,0:T(8,128)(2,1)S(1)}, u32[]{:S(2)}, u32[]{:S(2)}) collective-permute-start(bf16[256,128]{1,0:T(8,128)(2,1)S(1)} %get-tuple-element.94), channel_id=1, source_target_pairs={{28,0},{29,1},{30,2},{31,3}} | collective-permute-start | bytes 196616 | tf_op jit(solution)/shard_map/ppermute | solution.py:408
  90.9 7.8 %collective-permute-start.23 = (bf16[4,256,128]{2,1,0:T(8,128)(2,1)S(1)}, bf16[4,256,128]{2,1,0:T(8,128)(2,1)S(1)}, u32[]{:S(2)}, u32[]{:S(2)}) collective-permute-start(bf16[4,256,128]{2,1,0:T(8,128)(2,1)S(1)} %owner_sum.1.refs_0_), channel_id=1, source_target_pairs={{0,2},{1,3},{2,0},{3,1},{4,6},{5,7},{6,4},{7,5},{8,10},{9,11},{10,... | collective-permute-start | bytes 786440 | tf_op jit(solution)/shard_map/ppermute | solution.py:405
  92.2 6.4 %collective-permute-start.22 = (bf16[4,256,128]{2,1,0:T(8,128)(2,1)S(1)}, bf16[4,256,128]{2,1,0:T(8,128)(2,1)S(1)}, u32[]{:S(2)}, u32[]{:S(2)}) collective-permute-start(bf16[4,256,128]{2,1,0:T(8,128)(2,1)S(1)} %owner_sum.1.refs_0_), channel_id=1, source_target_pairs={{0,1},{1,0},{2,3},{3,2},{4,5},{5,4},{6,7},{7,6},{8,9},{9,8},{10,11... | collective-permute-start | bytes 786440 | tf_op jit(solution)/shard_map/ppermute | solution.py:402
  98.6 1.5 %collective-permute-start.24 = (bf16[4,256,128]{2,1,0:T(8,128)(2,1)S(1)}, bf16[4,256,128]{2,1,0:T(8,128)(2,1)S(1)}, u32[]{:S(2)}, u32[]{:S(2)}) collective-permute-start(bf16[4,256,128]{2,1,0:T(8,128)(2,1)S(1)} %collective-permute-done.23.refs_2_), channel_id=1, source_target_pairs={{0,1},{1,0},{2,3},{3,2},{4,5},{5,4},{6,7},{7,6},{8,9},{9,8},{10,11... | collective-permute-start | bytes 786440 | tf_op jit(solution)/shard_map/ppermute | solution.py:402
where the time goes:
time: 102 us; the launch traced here: 101 us
  waiting for transfers between devices  35 us (34%)
  starting transfers between devices  27.4 us (27%)
  Pallas kernels  22.4 us (22%)
  blocking collectives  13.6 us (13%)
  local copies, waits for them, and re-layouts  1.84 us (2%)
    ppermute x7, waiting for transfers between devices, to_owner(): lax.ppermute(array, 'ctx', [(c, c - s - 1) for c in range(s + 1, ctx_coun...  20.9 us
    all_to_all x1, blocking collectives, body(): lax.all_to_all(jnp.broadcast_to(selected.reshape(1, 3 * blocks_here), (ct...  13.6 us
    ppermute x7, starting transfers between devices, to_reader(): lax.ppermute(array, 'ctx', [(c - s - 1, c) for c in range(s + 1, ctx_coun...  13.1 us
    pallas_call x1, Pallas kernels, body(): pl.pallas_call(functools.partial(local_kernel, factor, scaling, blocks_he...  9.44 us
    ppermute x7, starting transfers between devices, to_owner(): lax.ppermute(array, 'ctx', [(c, c - s - 1) for c in range(s + 1, ctx_coun...  9.04 us
    ppermute x7, waiting for transfers between devices, swap(): return lax.ppermute(array, 'head', [(h, h ^ 1) for h in range(heads)])  7.65 us
    ppermute x4, waiting for transfers between devices, to_chip(): lax.ppermute(array, 'head', [(h, (h + 2 * d) % heads) for h in range(head...  6.4 us
    pallas_call x1, Pallas kernels, body(): pl.pallas_call(functools.partial(local_stats_kernel, factor, blocks_here)...  5.74 us
  transfers between devices with their start and end apart: 25, of which 13 were waited for; matrix products, arithmetic and copies ran while one was open for 0% of the time, Pallas kernels for 15%

commit v1 on v0

--- a/solution.py
+++ b/solution.py
@@ -314,12 +314,9 @@
     send[...] = (acc[1 - core] * send_scale).astype(BF16)
 
 
-def owner_kernel(chips, far, asked, mine, *refs):
-    others, back, (out, acc) = refs[: chips - 1], refs[chips - 1 : -2], refs[-2:]
-    total = mine[...]
-    for part in others:
-        total = total + part[...].astype(F32)
-    acc[...] = total
+def far_return_kernel(far, asked, *refs):
+    back, acc = refs[:-1], refs[-1]
+    acc[...] = jnp.zeros_like(acc)
     for i, s in enumerate(far):
         slot = asked[s] - 1
 
@@ -327,7 +324,13 @@
         def _():
             acc[slot] += back[i][...].astype(F32)
 
-    out[...] = acc[...].astype(BF16)
+
+def owner_kernel(returned, mine, *refs):
+    others, out = refs[:-1], refs[-1]
+    total = mine[...] + returned[...]
+    for part in others:
+        total = total + part[...].astype(F32)
+    out[...] = total.astype(BF16)
 
 
 def spread_kernel(chips, piece, *refs):
@@ -514,15 +517,23 @@
     own_parts = [to_chip(own_sums[d], d) for d in range(1, chips)]
     far_out = head_sums(far_sums[0], far_parts, len(far))
     far_back = [to_owner(far_out[i], s) for i, s in enumerate(far)]
+    returned = pl.pallas_call(
+        functools.partial(far_return_kernel, far),
+        in_specs=[smem] + [whole] * len(far),
+        out_specs=whole,
+        out_shape=pieces_type(blocks_here, F32),
+        compiler_params=params((2 * blocks_here + len(far)) * block_bytes),
+        cost_estimate=cost(600, 8 * tok_rows * feature * 2),
+        name="far_returns",
+    )(asked, *far_back)
     mine = pl.pallas_call(
-        functools.partial(owner_kernel, chips, far),
-        in_specs=[smem] + [whole] * (chips + len(far)),
+        owner_kernel,
+        in_specs=[whole] * (1 + chips),
         out_specs=whole,
         out_shape=pieces_type(blocks_here, BF16),
-        scratch_shapes=[pltpu.VMEM((blocks_here, piece, feature), F32)],
-        compiler_params=params((5 * blocks_here + shifts) * block_bytes),
+        compiler_params=params(6 * blocks_here * block_bytes),
         name="owner_sum",
-    )(asked, own_sums[0], *own_parts, *far_back)
+    )(returned, own_sums[0], *own_parts)
     spread = [mine, swap(mine)]
     for d in range(1, chips):
         part = to_chip(mine, d)

time: 102 us -> 99.1 us (0.972)
  waiting for transfers between devices: 35 us -> 31.6 us
    ppermute x7, waiting for transfers between devices: 7.65 us -> 5.75 us  [swap(): return lax.ppermute(array, 'head', [(h, h ^ 1) for h in range(heads)])]
    ppermute x7, waiting for transfers between devices: 20.9 us -> 19.3 us  [to_owner(): lax.ppermute(array, 'ctx', [(c, c - s - 1) for c in range(s + 1, ctx_coun...]
  transfers between devices with their start and end apart: 25 -> 25, of which waited for: 13 -> 12; matrix products, arithmetic and copies ran while one was open for 0% -> 0% of each run, Pallas kernels for 15% -> 17%
where the time goes in v1:
time: 99.1 us; the launch traced here: 98 us
  waiting for transfers between devices  31.6 us (32%)
  starting transfers between devices  27.4 us (28%)
  Pallas kernels  22.5 us (23%)
  blocking collectives  13.6 us (14%)
  local copies, waits for them, and re-layouts  1.84 us (2%)
    ppermute x7, waiting for transfers between devices, to_owner(): lax.ppermute(array, 'ctx', [(c, c - s - 1) for c in range(s + 1, ctx_coun...  19.3 us
    all_to_all x1, blocking collectives, body(): lax.all_to_all(jnp.broadcast_to(selected.reshape(1, 3 * blocks_here), (ct...  13.6 us
    ppermute x7, starting transfers between devices, to_reader(): lax.ppermute(array, 'ctx', [(c - s - 1, c) for c in range(s + 1, ctx_coun...  13.1 us
    pallas_call x1, Pallas kernels, body(): pl.pallas_call(functools.partial(local_kernel, factor, scaling, blocks_he...  9.44 us
    ppermute x7, starting transfers between devices, to_owner(): lax.ppermute(array, 'ctx', [(c, c - s - 1) for c in range(s + 1, ctx_coun...  9.04 us
    ppermute x4, waiting for transfers between devices, to_chip(): lax.ppermute(array, 'head', [(h, (h + 2 * d) % heads) for h in range(head...  6.55 us
    ppermute x7, waiting for transfers between devices, swap(): return lax.ppermute(array, 'head', [(h, h ^ 1) for h in range(heads)])  5.75 us
    pallas_call x1, Pallas kernels, body(): pl.pallas_call(functools.partial(local_stats_kernel, factor, blocks_here)...  5.74 us
  transfers between devices with their start and end apart: 25, of which 12 were waited for; matrix products, arithmetic and copies ran while one was open for 0% of the time, Pallas kernels for 17%

profile of v1, /device:TPU:0, one launch (start us, length us, event | category | flops | bytes accessed | tf_op | source)
XLA Modules:
  0.0 98.0 jit_solution(10783848504505012786)
XLA Ops:
  0.6 0.8 broadcast_in_dim.7
  1.4 13.6 %all_to_all.8 = s32[8,1,12]{2,1,0:T(1,128)} all-to-all(s32[8,1,12]{2,1,0:T(1,128)S(1)} %broadcast_in_dim.8), channel_id=1, replica_groups=mesh['ctx'=8,'head'=4] {'ctx'}, dimensions={0} | all-to-all | bytes 768 | tf_op jit(solution)/shard_map/all_to_all | solution.py:416
  15.0 2.9 %pick_rows.1 = (s32[7]{0:T(128)}, bf16[512,128]{1,0:T(8,128)(2,1)}, bf16[512,128]{1,0:T(8,128)(2,1)}, bf16[512,128]{1,0:T(8,128)(2,1)}, bf16[256,128]{1,0:T(8,12...) custom-call(s32[8,12]{1,0:T(8,128)} %bitcast.34, ...), custom_call_target="tpu_custom_call" | custom-call | tf_op jit(solution)/shard_map/pick_rows/pallas_call | solution.py:420
  18.0 0.0 copy-start
  18.0 2.6 %collective-permute-start = (bf16[256,128]{1,0:T(8,128)(2,1)}, bf16[256,128]{1,0:T(8,128)(2,1)S(1)}, u32[]{:S(2)}, u32[]{:S(2)}) collective-permute-start(bf16[256,128]{1,0:T(8,128)(2,1)} %get-tuple-element.50), channel_id=1, source_target_pairs={{0,16},{4,20},{8,24},{12,28},{1,17},{5,21},{9,25},{13,29},{2,18},{... | collective-permute-start | bytes 196616 | tf_op jit(solution)/shard_map/ppermute | solution.py:414
  20.6 1.3 %collective-permute-start.1 = (bf16[256,128]{1,0:T(8,128)(2,1)}, bf16[256,128]{1,0:T(8,128)(2,1)S(1)}, u32[]{:S(2)}, u32[]{:S(2)}) collective-permute-start(bf16[256,128]{1,0:T(8,128)(2,1)} %get-tuple-element.51), channel_id=1, source_target_pairs={{0,20},{4,24},{8,28},{1,21},{5,25},{9,29},{2,22},{6,26},{10,30},{3... | collective-permute-start | bytes 196616 | tf_op jit(solution)/shard_map/ppermute | solution.py:414
  22.0 1.4 %collective-permute-start.2 = (bf16[256,128]{1,0:T(8,128)(2,1)}, bf16[256,128]{1,0:T(8,128)(2,1)S(1)}, u32[]{:S(2)}, u32[]{:S(2)}) collective-permute-start(bf16[256,128]{1,0:T(8,128)(2,1)} %get-tuple-element.52), channel_id=1, source_target_pairs={{0,24},{4,28},{1,25},{5,29},{2,26},{6,30},{3,27},{7,31}} | collective-permute-start | bytes 196616 | tf_op jit(solution)/shard_map/ppermute | solution.py:414
  23.3 1.3 %collective-permute-start.3 = (bf16[256,128]{1,0:T(8,128)(2,1)}, bf16[256,128]{1,0:T(8,128)(2,1)S(1)}, u32[]{:S(2)}, u32[]{:S(2)}) collective-permute-start(bf16[256,128]{1,0:T(8,128)(2,1)} %get-tuple-element.53), channel_id=1, source_target_pairs={{0,28},{1,29},{2,30},{3,31}} | collective-permute-start | bytes 196616 | tf_op jit(solution)/shard_map/ppermute | solution.py:414
  24.6 2.7 %collective-permute-start.4 = (bf16[512,128]{1,0:T(8,128)(2,1)}, bf16[512,128]{1,0:T(8,128)(2,1)S(1)}, u32[]{:S(2)}, u32[]{:S(2)}) collective-permute-start(bf16[512,128]{1,0:T(8,128)(2,1)} %get-tuple-element.55), channel_id=1, source_target_pairs={{0,4},{4,8},{8,12},{12,16},{16,20},{20,24},{24,28},{1,5},{5,9},{9,... | collective-permute-start | bytes 393224 | tf_op jit(solution)/shard_map/ppermute | solution.py:414
  27.4 0.0 collective-permute-done
  27.4 1.3 %collective-permute-start.5 = (bf16[512,128]{1,0:T(8,128)(2,1)}, bf16[512,128]{1,0:T(8,128)(2,1)S(1)}, u32[]{:S(2)}, u32[]{:S(2)}) collective-permute-start(bf16[512,128]{1,0:T(8,128)(2,1)} %get-tuple-element.56), channel_id=1, source_target_pairs={{0,8},{4,12},{8,16},{12,20},{16,24},{20,28},{1,9},{5,13},{9,17},{1... | collective-permute-start | bytes 393224 | tf_op jit(solution)/shard_map/ppermute | solution.py:414
  28.7 0.0 collective-permute-done.1
  28.7 2.5 %collective-permute-start.6 = (bf16[512,128]{1,0:T(8,128)(2,1)}, bf16[512,128]{1,0:T(8,128)(2,1)S(1)}, u32[]{:S(2)}, u32[]{:S(2)}) collective-permute-start(bf16[512,128]{1,0:T(8,128)(2,1)} %get-tuple-element.57), channel_id=1, source_target_pairs={{0,12},{4,16},{8,20},{12,24},{16,28},{1,13},{5,17},{9,21},{13,25},... | collective-permute-start | bytes 393224 | tf_op jit(solution)/shard_map/ppermute | solution.py:414
  31.2 0.0 collective-permute-done.2
  31.2 0.0 collective-permute-done.3
  31.2 0.0 copy-start.2
  31.2 1.5 %collective-permute-start.9 = (bf16[4,256,128]{2,1,0:T(8,128)(2,1)S(1)}, bf16[4,256,128]{2,1,0:T(8,128)(2,1)S(1)}, u32[]{:S(2)}, u32[]{:S(2)}) collective-permute-start(bf16[4,256,128]{2,1,0:T(8,128)(2,1)S(1)} %pad_maximum_fusion.1.refs_2_), channel_id=1, source_target_pairs={{0,2},{1,3},{2,0},{3,1},{4,6},{5,7},{6,4},{7,5},{8,10},{9,11},{10,... | collective-permute-start | bytes 786440 | tf_op jit(solution)/shard_map/ppermute | solution.py:408
  32.8 0.0 copy-start.5
  32.8 1.0 %copy-done.5 = bf16[2048,1,128]{2,0,1:T(8,128)(2,1)S(1)} copy-done((bf16[2048,1,128]{2,0,1:T(8,128)(2,1)S(1)}, bf16[2048,1,128]{2,0,1:T(8,128)(2,1)}, u32[]{:S(2)}) %copy-start.5) | copy-done | bytes 524312
  33.9 5.7 %local_stats.1.stats = f32[4,8,512]{2,1,0:T(8,128)S(1)} custom-call(s32[4,3]{1,0:T(4,128)S(1)} %copy-done.2, bf16[2048,128]{1,0:T(8,128)(2,1)S(1)} %bitcast.21, bf16[2048,128]{1,0:T(8,128)(2,1)S(1)} %bitcast.24, bf16[4,512,128]{2,1,0:T(8,128)(2,1)S(1)} %bitcast.16, bf16[4,512,128]{2,1,0:T(8,128)(2,1)S(1)} %bitcast.19), custom_call_target="tpu_custom_call" | custom-call | flops 2013265920 | bytes 2097152 | tf_op jit(solution)/shard_map/local_stats/pallas_call | solution.py:434
  39.6 0.0 copy-start.6
  39.6 0.0 collective-permute-done.4
  39.6 0.0 collective-permute-done.5
  39.6 0.0 collective-permute-done.6
  39.7 0.1 collective-permute-start.7
  39.8 0.5 collective-permute-start.8
  40.3 0.1 collective-permute-start.10
  40.4 1.5 %collective-permute-done.8.refs_3_ = bf16[4,256,128]{2,1,0:T(8,128)(2,1)S(1)} collective-permute-done((bf16[4,256,128]{2,1,0:T(8,128)(2,1)S(1)}, bf16[4,256,128]{2,1,0:T(8,128)(2,1)S(1)}, u32[]{:S(2)}, u32[]{:S(2)}) %collective-permute-start.8) | collective-permute-done | bytes 262176 | tf_op jit(solution)/shard_map/ppermute | solution.py:405
  41.9 0.0 collective-permute-done.7.refs_1_
  41.9 0.4 collective-permute-done.10.refs_5_
  42.2 1.6 %remote_pairs.1 = (bf16[7,512,128]{2,1,0:T(8,128)(2,1)S(1)}, bf16[7,512,128]{2,1,0:T(8,128)(2,1)S(1)}, f32[4,8,512]{2,1,0:T(8,128)S(1)}, f32[4,128,512]{2,1,0:T(8,128)S(1)}) custom-call(s32[4,3]{1,0:T(4,128)S(1)} %copy-done.2, bf16[2048,128]{1,0:T(8,128)(2,1)S(1)} %bitcast.22, bf16[2048,128]{1,0:T(8,128)(2,1)S(1)} %bitcast.25, ...), custom_call_target="tpu_custom_call" | custom-call | flops 4026531840 | bytes 4194304 | tf_op jit(solution)/shard_map/remote_pairs/pallas_call | solution.py:450
  43.8 0.2 collective-permute-start.11
  44.0 2.3 %collective-permute-done.11.theirs = bf16[7,512,128]{2,1,0:T(8,128)(2,1)S(1)} collective-permute-done((bf16[7,512,128]{2,1,0:T(8,128)(2,1)S(1)}, bf16[7,512,128]{2,1,0:T(8,128)(2,1)S(1)}, u32[]{:S(2)}, u32[]{:S(2)}) %collective-permute-start.11) | collective-permute-done | bytes 917536 | tf_op jit(solution)/shard_map/ppermute | solution.py:405
  46.3 0.2 chip_sum.1
  46.5 1.3 %collective-permute-start.13 = (bf16[512,128]{1,0:T(8,128)(2,1)S(1)}, bf16[512,128]{1,0:T(8,128)(2,1)S(1)}, u32[]{:S(2)}, u32[]{:S(2)}) collective-permute-start(bf16[512,128]{1,0:T(8,128)(2,1)S(1)} %get-tuple-element.78), channel_id=1, source_target_pairs={{4,0},{8,4},{12,8},{16,12},{20,16},{24,20},{28,24},{5,1},{9,5},{13... | collective-permute-start | bytes 393224 | tf_op jit(solution)/shard_map/ppermute | solution.py:411
  47.8 1.3 %collective-permute-start.14 = (bf16[512,128]{1,0:T(8,128)(2,1)S(1)}, bf16[512,128]{1,0:T(8,128)(2,1)S(1)}, u32[]{:S(2)}, u32[]{:S(2)}) collective-permute-start(bf16[512,128]{1,0:T(8,128)(2,1)S(1)} %get-tuple-element.79), channel_id=1, source_target_pairs={{8,0},{12,4},{16,8},{20,12},{24,16},{28,20},{9,1},{13,5},{17,9},{2... | collective-permute-start | bytes 393224 | tf_op jit(solution)/shard_map/ppermute | solution.py:411
  49.1 1.3 %collective-permute-start.15 = (bf16[512,128]{1,0:T(8,128)(2,1)S(1)}, bf16[512,128]{1,0:T(8,128)(2,1)S(1)}, u32[]{:S(2)}, u32[]{:S(2)}) collective-permute-start(bf16[512,128]{1,0:T(8,128)(2,1)S(1)} %get-tuple-element.80), channel_id=1, source_target_pairs={{12,0},{16,4},{20,8},{24,12},{28,16},{13,1},{17,5},{21,9},{25,13},... | collective-permute-start | bytes 393224 | tf_op jit(solution)/shard_map/ppermute | solution.py:411
  50.4 0.7 collective-permute-start.12
  51.1 9.4 %local_pairs.1 = (bf16[4,512,128]{2,1,0:T(8,128)(2,1)S(1)}, bf16[4,512,128]{2,1,0:T(8,128)(2,1)S(1)}, bf16[2048,128]{1,0:T(8,128)(2,1)}) custom-call(s32[4,3]{1,0:T(4,128)S(1)} %copy-done.2, bf16[2048,128]{1,0:T(8,128)(2,1)S(1)} %bitcast.23, bf16[2048,128]{1,0:T(8,128)(2,1)S(1)} %bitcast.26, bf16[4,512,128]{2,1,0:T(8,128)(2,1)S(1)} %bitcast.17, ...), custom_call_target="tpu_custom_call" | custom-call | flops 4026531840 | bytes 4194304 | tf_op jit(solution)/shard_map/local_pairs/pallas_call | solution.py:491
  60.5 0.1 collective-permute-done.13.refs_0_
  60.6 4.0 %collective-permute-done.14.refs_1_ = bf16[512,128]{1,0:T(8,128)(2,1)S(1)} collective-permute-done((bf16[512,128]{1,0:T(8,128)(2,1)S(1)}, bf16[512,128]{1,0:T(8,128)(2,1)S(1)}, u32[]{:S(2)}, u32[]{:S(2)}) %collective-permute-start.14) | collective-permute-done | bytes 131104 | tf_op jit(solution)/shard_map/ppermute | solution.py:411
  64.6 3.3 %collective-permute-done.15.refs_2_ = bf16[512,128]{1,0:T(8,128)(2,1)S(1)} collective-permute-done((bf16[512,128]{1,0:T(8,128)(2,1)S(1)}, bf16[512,128]{1,0:T(8,128)(2,1)S(1)}, u32[]{:S(2)}, u32[]{:S(2)}) %collective-permute-start.15) | collective-permute-done | bytes 131104 | tf_op jit(solution)/shard_map/ppermute | solution.py:411
  67.9 0.0 collective-permute-done.12.refs_0_
  67.9 0.0 collective-permute-start.20
  67.9 1.3 %collective-permute-start.16 = (bf16[256,128]{1,0:T(8,128)(2,1)S(1)}, bf16[256,128]{1,0:T(8,128)(2,1)S(1)}, u32[]{:S(2)}, u32[]{:S(2)}) collective-permute-start(bf16[256,128]{1,0:T(8,128)(2,1)S(1)} %get-tuple-element.84), channel_id=1, source_target_pairs={{16,0},{20,4},{24,8},{28,12},{17,1},{21,5},{25,9},{29,13},{18,2},{... | collective-permute-start | bytes 196616 | tf_op jit(solution)/shard_map/ppermute | solution.py:411
  69.2 1.3 %collective-permute-start.17 = (bf16[256,128]{1,0:T(8,128)(2,1)S(1)}, bf16[256,128]{1,0:T(8,128)(2,1)S(1)}, u32[]{:S(2)}, u32[]{:S(2)}) collective-permute-start(bf16[256,128]{1,0:T(8,128)(2,1)S(1)} %get-tuple-element.85), channel_id=1, source_target_pairs={{20,0},{24,4},{28,8},{21,1},{25,5},{29,9},{22,2},{26,6},{30,10},{2... | collective-permute-start | bytes 196616 | tf_op jit(solution)/shard_map/ppermute | solution.py:411
  70.5 1.3 %collective-permute-start.18 = (bf16[256,128]{1,0:T(8,128)(2,1)S(1)}, bf16[256,128]{1,0:T(8,128)(2,1)S(1)}, u32[]{:S(2)}, u32[]{:S(2)}) collective-permute-start(bf16[256,128]{1,0:T(8,128)(2,1)S(1)} %get-tuple-element.86), channel_id=1, source_target_pairs={{24,0},{28,4},{25,1},{29,5},{26,2},{30,6},{27,3},{31,7}} | collective-permute-start | bytes 196616 | tf_op jit(solution)/shard_map/ppermute | solution.py:411
  71.8 1.3 %collective-permute-start.19 = (bf16[256,128]{1,0:T(8,128)(2,1)S(1)}, bf16[256,128]{1,0:T(8,128)(2,1)S(1)}, u32[]{:S(2)}, u32[]{:S(2)}) collective-permute-start(bf16[256,128]{1,0:T(8,128)(2,1)S(1)} %get-tuple-element.87), channel_id=1, source_target_pairs={{28,0},{29,1},{30,2},{31,3}} | collective-permute-start | bytes 196616 | tf_op jit(solution)/shard_map/ppermute | solution.py:411
  73.1 0.0 collective-permute-done.20.theirs
  73.2 0.8 own_sum.1
  74.0 0.7 collective-permute-start.21
  74.6 4.3 %collective-permute-done.16.refs_0_ = bf16[256,128]{1,0:T(8,128)(2,1)S(1)} collective-permute-done((bf16[256,128]{1,0:T(8,128)(2,1)S(1)}, bf16[256,128]{1,0:T(8,128)(2,1)S(1)}, u32[]{:S(2)}, u32[]{:S(2)}) %collective-permute-start.16) | collective-permute-done | bytes 65568 | tf_op jit(solution)/shard_map/ppermute | solution.py:411
  78.9 4.9 %collective-permute-done.17.refs_1_ = bf16[256,128]{1,0:T(8,128)(2,1)S(1)} collective-permute-done((bf16[256,128]{1,0:T(8,128)(2,1)S(1)}, bf16[256,128]{1,0:T(8,128)(2,1)S(1)}, u32[]{:S(2)}, u32[]{:S(2)}) %collective-permute-start.17) | collective-permute-done | bytes 65568 | tf_op jit(solution)/shard_map/ppermute | solution.py:411
  83.8 1.4 %collective-permute-done.18.refs_2_ = bf16[256,128]{1,0:T(8,128)(2,1)S(1)} collective-permute-done((bf16[256,128]{1,0:T(8,128)(2,1)S(1)}, bf16[256,128]{1,0:T(8,128)(2,1)S(1)}, u32[]{:S(2)}, u32[]{:S(2)}) %collective-permute-start.18) | collective-permute-done | bytes 65568 | tf_op jit(solution)/shard_map/ppermute | solution.py:411
  85.2 1.4 %collective-permute-done.19.refs_3_ = bf16[256,128]{1,0:T(8,128)(2,1)S(1)} collective-permute-done((bf16[256,128]{1,0:T(8,128)(2,1)S(1)}, bf16[256,128]{1,0:T(8,128)(2,1)S(1)}, u32[]{:S(2)}, u32[]{:S(2)}) %collective-permute-start.19) | collective-permute-done | bytes 65568 | tf_op jit(solution)/shard_map/ppermute | solution.py:411
  86.6 0.6 far_returns.1.returned
  87.2 0.0 collective-permute-done.21.refs_0_
  87.2 0.1 owner_sum.1.refs_0_
  87.3 1.5 %collective-permute-start.23 = (bf16[4,256,128]{2,1,0:T(8,128)(2,1)S(1)}, bf16[4,256,128]{2,1,0:T(8,128)(2,1)S(1)}, u32[]{:S(2)}, u32[]{:S(2)}) collective-permute-start(bf16[4,256,128]{2,1,0:T(8,128)(2,1)S(1)} %owner_sum.1.refs_0_), channel_id=1, source_target_pairs={{0,2},{1,3},{2,0},{3,1},{4,6},{5,7},{6,4},{7,5},{8,10},{9,11},{10,... | collective-permute-start | bytes 786440 | tf_op jit(solution)/shard_map/ppermute | solution.py:408
  88.8 0.0 collective-permute-start.22
  88.8 6.5 %collective-permute-done.23.refs_2_ = bf16[4,256,128]{2,1,0:T(8,128)(2,1)S(1)} collective-permute-done((bf16[4,256,128]{2,1,0:T(8,128)(2,1)S(1)}, bf16[4,256,128]{2,1,0:T(8,128)(2,1)S(1)}, u32[]{:S(2)}, u32[]{:S(2)}) %collective-permute-start.23) | collective-permute-done | bytes 262176 | tf_op jit(solution)/shard_map/ppermute | solution.py:408
  95.4 0.0 collective-permute-start.24
  95.4 1.5 %collective-permute-done.24.refs_3_ = bf16[4,256,128]{2,1,0:T(8,128)(2,1)S(1)} collective-permute-done((bf16[4,256,128]{2,1,0:T(8,128)(2,1)S(1)}, bf16[4,256,128]{2,1,0:T(8,128)(2,1)S(1)}, u32[]{:S(2)}, u32[]{:S(2)}) %collective-permute-start.24) | collective-permute-done | bytes 262176 | tf_op jit(solution)/shard_map/ppermute | solution.py:405
  96.9 1.0 %spread.1 = (bf16[4,512,128]{2,1,0:T(8,128)(2,1)}, bf16[4,512,128]{2,1,0:T(8,128)(2,1)}) custom-call(bf16[4,256,128]{2,1,0:T(8,128)(2,1)S(1)} %owner_sum.1.refs_0_, bf16[4,256,128]{2,1,0:T(8,128)(2,1)S(1)} %collective-permute-done.22.refs_1_, bf16[4,256,128]{2,1,0:T(8,128)(2,1)S(1)} %collective-permute-done.23.refs_2_, ...), custom_call_target="tpu_custom_call" | custom-call | tf_op jit(solution)/shard_map/spread/pallas_call | solution.py:541
  (15 shorter events, 0.2 us)
Async XLA Ops:
  15.0 17.8 %copy-start.1 = (bf16[2048,128]{1,0:T(8,128)(2,1)S(1)}, bf16[2048,128]{1,0:T(8,128)(2,1)}, u32[]{:S(2)}) copy-start(bf16[2048,128]{1,0:T(8,128)(2,1)} %param.7) | copy-start | bytes 1572868
  15.0 17.8 %copy-start.4 = (bf16[2048,1,128]{2,0,1:T(8,128)(2,1)S(1)}, bf16[2048,1,128]{2,0,1:T(8,128)(2,1)}, u32[]{:S(2)}) copy-start(bf16[2048,1,128]{2,0,1:T(8,128)(2,1)} %param.5) | copy-start | bytes 1572868
  18.0 14.8 %copy-start = (bf16[2048,128]{1,0:T(8,128)(2,1)S(1)}, bf16[2048,128]{1,0:T(8,128)(2,1)}, u32[]{:S(2)}) copy-start(bf16[2048,128]{1,0:T(8,128)(2,1)} %param.6) | copy-start | bytes 1572868
  18.0 9.4 %collective-permute-start = (bf16[256,128]{1,0:T(8,128)(2,1)}, bf16[256,128]{1,0:T(8,128)(2,1)S(1)}, u32[]{:S(2)}, u32[]{:S(2)}) collective-permute-start(bf16[256,128]{1,0:T(8,128)(2,1)} %get-tuple-element.50), channel_id=1, source_target_pairs={{0,16},{4,20},{8,24},{12,28},{1,17},{5,21},{9,25},{13,29},{2,18},{... | collective-permute-start | bytes 196616 | tf_op jit(solution)/shard_map/ppermute | solution.py:414
  20.6 8.1 %collective-permute-start.1 = (bf16[256,128]{1,0:T(8,128)(2,1)}, bf16[256,128]{1,0:T(8,128)(2,1)S(1)}, u32[]{:S(2)}, u32[]{:S(2)}) collective-permute-start(bf16[256,128]{1,0:T(8,128)(2,1)} %get-tuple-element.51), channel_id=1, source_target_pairs={{0,20},{4,24},{8,28},{1,21},{5,25},{9,29},{2,22},{6,26},{10,30},{3... | collective-permute-start | bytes 196616 | tf_op jit(solution)/shard_map/ppermute | solution.py:414
  22.0 9.2 %collective-permute-start.2 = (bf16[256,128]{1,0:T(8,128)(2,1)}, bf16[256,128]{1,0:T(8,128)(2,1)S(1)}, u32[]{:S(2)}, u32[]{:S(2)}) collective-permute-start(bf16[256,128]{1,0:T(8,128)(2,1)} %get-tuple-element.52), channel_id=1, source_target_pairs={{0,24},{4,28},{1,25},{5,29},{2,26},{6,30},{3,27},{7,31}} | collective-permute-start | bytes 196616 | tf_op jit(solution)/shard_map/ppermute | solution.py:414
  23.3 7.9 %collective-permute-start.3 = (bf16[256,128]{1,0:T(8,128)(2,1)}, bf16[256,128]{1,0:T(8,128)(2,1)S(1)}, u32[]{:S(2)}, u32[]{:S(2)}) collective-permute-start(bf16[256,128]{1,0:T(8,128)(2,1)} %get-tuple-element.53), channel_id=1, source_target_pairs={{0,28},{1,29},{2,30},{3,31}} | collective-permute-start | bytes 196616 | tf_op jit(solution)/shard_map/ppermute | solution.py:414
  24.6 15.0 %collective-permute-start.4 = (bf16[512,128]{1,0:T(8,128)(2,1)}, bf16[512,128]{1,0:T(8,128)(2,1)S(1)}, u32[]{:S(2)}, u32[]{:S(2)}) collective-permute-start(bf16[512,128]{1,0:T(8,128)(2,1)} %get-tuple-element.55), channel_id=1, source_target_pairs={{0,4},{4,8},{8,12},{12,16},{16,20},{20,24},{24,28},{1,5},{5,9},{9,... | collective-permute-start | bytes 393224 | tf_op jit(solution)/shard_map/ppermute | solution.py:414
  27.4 12.2 %collective-permute-start.5 = (bf16[512,128]{1,0:T(8,128)(2,1)}, bf16[512,128]{1,0:T(8,128)(2,1)S(1)}, u32[]{:S(2)}, u32[]{:S(2)}) collective-permute-start(bf16[512,128]{1,0:T(8,128)(2,1)} %get-tuple-element.56), channel_id=1, source_target_pairs={{0,8},{4,12},{8,16},{12,20},{16,24},{20,28},{1,9},{5,13},{9,17},{1... | collective-permute-start | bytes 393224 | tf_op jit(solution)/shard_map/ppermute | solution.py:414
  28.7 10.9 %collective-permute-start.6 = (bf16[512,128]{1,0:T(8,128)(2,1)}, bf16[512,128]{1,0:T(8,128)(2,1)S(1)}, u32[]{:S(2)}, u32[]{:S(2)}) collective-permute-start(bf16[512,128]{1,0:T(8,128)(2,1)} %get-tuple-element.57), channel_id=1, source_target_pairs={{0,12},{4,16},{8,20},{12,24},{16,28},{1,13},{5,17},{9,21},{13,25},... | collective-permute-start | bytes 393224 | tf_op jit(solution)/shard_map/ppermute | solution.py:414
  31.2 1.6 %copy-start.2 = (s32[4,3]{1,0:T(4,128)S(1)}, s32[4,3]{1,0:T(4,128)}, u32[]{:S(2)}) copy-start(s32[4,3]{1,0:T(4,128)} %chosen.2) | copy-start | bytes 148
  31.2 9.0 %collective-permute-start.9 = (bf16[4,256,128]{2,1,0:T(8,128)(2,1)S(1)}, bf16[4,256,128]{2,1,0:T(8,128)(2,1)S(1)}, u32[]{:S(2)}, u32[]{:S(2)}) collective-permute-start(bf16[4,256,128]{2,1,0:T(8,128)(2,1)S(1)} %pad_maximum_fusion.1.refs_2_), channel_id=1, source_target_pairs={{0,2},{1,3},{2,0},{3,1},{4,6},{5,7},{6,4},{7,5},{8,10},{9,11},{10,... | collective-permute-start | bytes 786440 | tf_op jit(solution)/shard_map/ppermute | solution.py:408
  32.8 1.0 %copy-start.5 = (bf16[2048,1,128]{2,0,1:T(8,128)(2,1)S(1)}, bf16[2048,1,128]{2,0,1:T(8,128)(2,1)}, u32[]{:S(2)}) copy-start(bf16[2048,1,128]{2,0,1:T(8,128)(2,1)} %param.8) | copy-start | bytes 1572868
  39.6 2.6 %copy-start.6 = (bf16[2048,1,128]{2,0,1:T(8,128)(2,1)S(1)}, bf16[2048,1,128]{2,0,1:T(8,128)(2,1)}, u32[]{:S(2)}) copy-start(bf16[2048,1,128]{2,0,1:T(8,128)(2,1)} %param.8) | copy-start | bytes 1572868
  39.7 2.2 %collective-permute-start.7 = (bf16[3,512,128]{2,1,0:T(8,128)(2,1)S(1)}, bf16[3,512,128]{2,1,0:T(8,128)(2,1)S(1)}, u32[]{:S(2)}, u32[]{:S(2)}) collective-permute-start(bf16[3,512,128]{2,1,0:T(8,128)(2,1)S(1)} %pad_maximum_fusion.refs_0_), channel_id=1, source_target_pairs={{0,1},{1,0},{2,3},{3,2},{4,5},{5,4},{6,7},{7,6},{8,9},{9,8},{10,11... | collective-permute-start | bytes 1179656 | tf_op jit(solution)/shard_map/ppermute | solution.py:405
  39.8 2.1 %collective-permute-start.8 = (bf16[4,256,128]{2,1,0:T(8,128)(2,1)S(1)}, bf16[4,256,128]{2,1,0:T(8,128)(2,1)S(1)}, u32[]{:S(2)}, u32[]{:S(2)}) collective-permute-start(bf16[4,256,128]{2,1,0:T(8,128)(2,1)S(1)} %pad_maximum_fusion.1.refs_2_), channel_id=1, source_target_pairs={{0,1},{1,0},{2,3},{3,2},{4,5},{5,4},{6,7},{7,6},{8,9},{9,8},{10,11... | collective-permute-start | bytes 786440 | tf_op jit(solution)/shard_map/ppermute | solution.py:405
  40.3 2.0 %collective-permute-start.10 = (bf16[4,256,128]{2,1,0:T(8,128)(2,1)S(1)}, bf16[4,256,128]{2,1,0:T(8,128)(2,1)S(1)}, u32[]{:S(2)}, u32[]{:S(2)}) collective-permute-start(bf16[4,256,128]{2,1,0:T(8,128)(2,1)S(1)} %collective-permute-done.9.refs_4_), channel_id=1, source_target_pairs={{0,1},{1,0},{2,3},{3,2},{4,5},{5,4},{6,7},{7,6},{8,9},{9,8},{10,11... | collective-permute-start | bytes 786440 | tf_op jit(solution)/shard_map/ppermute | solution.py:405
  43.8 2.5 %collective-permute-start.11 = (bf16[7,512,128]{2,1,0:T(8,128)(2,1)S(1)}, bf16[7,512,128]{2,1,0:T(8,128)(2,1)S(1)}, u32[]{:S(2)}, u32[]{:S(2)}) collective-permute-start(bf16[7,512,128]{2,1,0:T(8,128)(2,1)S(1)} %get-tuple-element.65), channel_id=1, source_target_pairs={{0,1},{1,0},{2,3},{3,2},{4,5},{5,4},{6,7},{7,6},{8,9},{9,8},{10,11... | collective-permute-start | bytes 2752520 | tf_op jit(solution)/shard_map/ppermute | solution.py:405
  46.5 14.1 %collective-permute-start.13 = (bf16[512,128]{1,0:T(8,128)(2,1)S(1)}, bf16[512,128]{1,0:T(8,128)(2,1)S(1)}, u32[]{:S(2)}, u32[]{:S(2)}) collective-permute-start(bf16[512,128]{1,0:T(8,128)(2,1)S(1)} %get-tuple-element.78), channel_id=1, source_target_pairs={{4,0},{8,4},{12,8},{16,12},{20,16},{24,20},{28,24},{5,1},{9,5},{13... | collective-permute-start | bytes 393224 | tf_op jit(solution)/shard_map/ppermute | solution.py:411
  47.8 16.7 %collective-permute-start.14 = (bf16[512,128]{1,0:T(8,128)(2,1)S(1)}, bf16[512,128]{1,0:T(8,128)(2,1)S(1)}, u32[]{:S(2)}, u32[]{:S(2)}) collective-permute-start(bf16[512,128]{1,0:T(8,128)(2,1)S(1)} %get-tuple-element.79), channel_id=1, source_target_pairs={{8,0},{12,4},{16,8},{20,12},{24,16},{28,20},{9,1},{13,5},{17,9},{2... | collective-permute-start | bytes 393224 | tf_op jit(solution)/shard_map/ppermute | solution.py:411
  49.1 18.7 %collective-permute-start.15 = (bf16[512,128]{1,0:T(8,128)(2,1)S(1)}, bf16[512,128]{1,0:T(8,128)(2,1)S(1)}, u32[]{:S(2)}, u32[]{:S(2)}) collective-permute-start(bf16[512,128]{1,0:T(8,128)(2,1)S(1)} %get-tuple-element.80), channel_id=1, source_target_pairs={{12,0},{16,4},{20,8},{24,12},{28,16},{13,1},{17,5},{21,9},{25,13},... | collective-permute-start | bytes 393224 | tf_op jit(solution)/shard_map/ppermute | solution.py:411
  50.4 17.4 %collective-permute-start.12 = (bf16[4,256,128]{2,1,0:T(8,128)(2,1)S(1)}, bf16[4,256,128]{2,1,0:T(8,128)(2,1)S(1)}, u32[]{:S(2)}, u32[]{:S(2)}) collective-permute-start(bf16[4,256,128]{2,1,0:T(8,128)(2,1)S(1)} %get-tuple-element.77), channel_id=1, source_target_pairs={{0,2},{1,3},{2,0},{3,1},{4,6},{5,7},{6,4},{7,5},{8,10},{9,11},{10,... | collective-permute-start | bytes 786440 | tf_op jit(solution)/shard_map/ppermute | solution.py:408
  67.9 5.3 %collective-permute-start.20 = (bf16[4,512,128]{2,1,0:T(8,128)(2,1)S(1)}, bf16[4,512,128]{2,1,0:T(8,128)(2,1)S(1)}, u32[]{:S(2)}, u32[]{:S(2)}) collective-permute-start(bf16[4,512,128]{2,1,0:T(8,128)(2,1)S(1)} %get-tuple-element.89), channel_id=1, source_target_pairs={{0,1},{1,0},{2,3},{3,2},{4,5},{5,4},{6,7},{7,6},{8,9},{9,8},{10,11... | collective-permute-start | bytes 1572872 | tf_op jit(solution)/shard_map/ppermute | solution.py:405
  67.9 11.0 %collective-permute-start.16 = (bf16[256,128]{1,0:T(8,128)(2,1)S(1)}, bf16[256,128]{1,0:T(8,128)(2,1)S(1)}, u32[]{:S(2)}, u32[]{:S(2)}) collective-permute-start(bf16[256,128]{1,0:T(8,128)(2,1)S(1)} %get-tuple-element.84), channel_id=1, source_target_pairs={{16,0},{20,4},{24,8},{28,12},{17,1},{21,5},{25,9},{29,13},{18,2},{... | collective-permute-start | bytes 196616 | tf_op jit(solution)/shard_map/ppermute | solution.py:411
  69.2 14.6 %collective-permute-start.17 = (bf16[256,128]{1,0:T(8,128)(2,1)S(1)}, bf16[256,128]{1,0:T(8,128)(2,1)S(1)}, u32[]{:S(2)}, u32[]{:S(2)}) collective-permute-start(bf16[256,128]{1,0:T(8,128)(2,1)S(1)} %get-tuple-element.85), channel_id=1, source_target_pairs={{20,0},{24,4},{28,8},{21,1},{25,5},{29,9},{22,2},{26,6},{30,10},{2... | collective-permute-start | bytes 196616 | tf_op jit(solution)/shard_map/ppermute | solution.py:411
  70.5 14.7 %collective-permute-start.18 = (bf16[256,128]{1,0:T(8,128)(2,1)S(1)}, bf16[256,128]{1,0:T(8,128)(2,1)S(1)}, u32[]{:S(2)}, u32[]{:S(2)}) collective-permute-start(bf16[256,128]{1,0:T(8,128)(2,1)S(1)} %get-tuple-element.86), channel_id=1, source_target_pairs={{24,0},{28,4},{25,1},{29,5},{26,2},{30,6},{27,3},{31,7}} | collective-permute-start | bytes 196616 | tf_op jit(solution)/shard_map/ppermute | solution.py:411
  71.8 1.3 %copy-start.3 = (s32[7]{0:T(128)S(1)}, s32[7]{0:T(128)}, u32[]{:S(2)}) copy-start(s32[7]{0:T(128)} %get-tuple-element.75.asked) | copy-start | bytes 88
  71.8 14.7 %collective-permute-start.19 = (bf16[256,128]{1,0:T(8,128)(2,1)S(1)}, bf16[256,128]{1,0:T(8,128)(2,1)S(1)}, u32[]{:S(2)}, u32[]{:S(2)}) collective-permute-start(bf16[256,128]{1,0:T(8,128)(2,1)S(1)} %get-tuple-element.87), channel_id=1, source_target_pairs={{28,0},{29,1},{30,2},{31,3}} | collective-permute-start | bytes 196616 | tf_op jit(solution)/shard_map/ppermute | solution.py:411
  74.0 13.3 %collective-permute-start.21 = (bf16[4,256,128]{2,1,0:T(8,128)(2,1)S(1)}, bf16[4,256,128]{2,1,0:T(8,128)(2,1)S(1)}, u32[]{:S(2)}, u32[]{:S(2)}) collective-permute-start(bf16[4,256,128]{2,1,0:T(8,128)(2,1)S(1)} %get-tuple-element.94), channel_id=1, source_target_pairs={{0,2},{1,3},{2,0},{3,1},{4,6},{5,7},{6,4},{7,5},{8,10},{9,11},{10,... | collective-permute-start | bytes 786440 | tf_op jit(solution)/shard_map/ppermute | solution.py:408
  87.3 8.1 %collective-permute-start.23 = (bf16[4,256,128]{2,1,0:T(8,128)(2,1)S(1)}, bf16[4,256,128]{2,1,0:T(8,128)(2,1)S(1)}, u32[]{:S(2)}, u32[]{:S(2)}) collective-permute-start(bf16[4,256,128]{2,1,0:T(8,128)(2,1)S(1)} %owner_sum.1.refs_0_), channel_id=1, source_target_pairs={{0,2},{1,3},{2,0},{3,1},{4,6},{5,7},{6,4},{7,5},{8,10},{9,11},{10,... | collective-permute-start | bytes 786440 | tf_op jit(solution)/shard_map/ppermute | solution.py:408
  88.8 6.5 %collective-permute-start.22 = (bf16[4,256,128]{2,1,0:T(8,128)(2,1)S(1)}, bf16[4,256,128]{2,1,0:T(8,128)(2,1)S(1)}, u32[]{:S(2)}, u32[]{:S(2)}) collective-permute-start(bf16[4,256,128]{2,1,0:T(8,128)(2,1)S(1)} %owner_sum.1.refs_0_), channel_id=1, source_target_pairs={{0,1},{1,0},{2,3},{3,2},{4,5},{5,4},{6,7},{7,6},{8,9},{9,8},{10,11... | collective-permute-start | bytes 786440 | tf_op jit(solution)/shard_map/ppermute | solution.py:405
  95.4 1.5 %collective-permute-start.24 = (bf16[4,256,128]{2,1,0:T(8,128)(2,1)S(1)}, bf16[4,256,128]{2,1,0:T(8,128)(2,1)S(1)}, u32[]{:S(2)}, u32[]{:S(2)}) collective-permute-start(bf16[4,256,128]{2,1,0:T(8,128)(2,1)S(1)} %collective-permute-done.23.refs_2_), channel_id=1, source_target_pairs={{0,1},{1,0},{2,3},{3,2},{4,5},{5,4},{6,7},{7,6},{8,9},{9,8},{10,11... | collective-permute-start | bytes 786440 | tf_op jit(solution)/shard_map/ppermute | solution.py:405

commit v2 on v1

--- a/solution.py
+++ b/solution.py
@@ -372,6 +372,8 @@
     shifts = ctx_count - 1
     far = [s for s in range(shifts) if 2 * (s + 1) >= ctx_count]
     near = [s for s in range(shifts) if 2 * (s + 1) < ctx_count]
+    far_in = [s for s in range(shifts) if 2 * (s + 2) >= ctx_count]
+    near_in = [s for s in range(shifts) if 2 * (s + 2) < ctx_count]
 
     q2 = queries.reshape(tok_rows, feature)
     do2 = dout.reshape(tok_rows, feature)
@@ -418,17 +420,17 @@
         "ctx", split_axis=0, concat_axis=0, tiled=True,
     )
     asked, *sent = pl.pallas_call(
-        functools.partial(pick_kernel, blocks_here, ctx_count, chips, far, piece),
+        functools.partial(pick_kernel, blocks_here, ctx_count, chips, far_in, piece),
         in_specs=[smem, hbm, hbm],
         out_specs=[smem] + [whole] * shifts,
         out_shape=[jax.ShapeDtypeStruct((shifts,), jnp.int32)]
-        + [piece_type if s in far else block_type for s in range(shifts)],
+        + [piece_type if s in far_in else block_type for s in range(shifts)],
         scratch_shapes=[pltpu.SemaphoreType.DMA((shifts,))],
         name="pick_rows",
     )(everyone, key_blocks, value_blocks)
 
-    far_mine = jnp.stack([to_reader(sent[s], s) for s in far])
-    near_parts = [to_reader(sent[s], s) for s in near]
+    far_mine = jnp.stack([to_reader(sent[s], s) for s in far_in])
+    near_parts = [to_reader(sent[s], s) for s in near_in]
     far_mine, chosen = lax.optimization_barrier((far_mine, selected))
     far_more = [to_chip(far_mine, d) for d in range(1, chips)]
     stats = pl.pallas_call(
@@ -448,7 +450,9 @@
         row_sets += [part, swap(part)]
 
     keep_far, send_far, final, grad_qt = pl.pallas_call(
-        functools.partial(remote_kernel, factor, scaling, blocks_here, chips, far, near, piece),
+        functools.partial(
+            remote_kernel, factor, scaling, blocks_here, chips, far_in, near_in, piece
+        ),
         in_specs=[smem] + [whole] * (3 + len(row_sets)),
         out_specs=[whole] * 4,
         out_shape=[far_type, far_type, stat_type, qt_type],

time: 99.1 us -> 104 us (1.049)
  waiting for transfers between devices: 31.6 us -> 36.6 us
    ppermute x7, waiting for transfers between devices: 0.02 us -> 2.12 us  [to_reader(): lax.ppermute(array, 'ctx', [(c - s - 1, c) for c in range(s + 1, ctx_coun...]
    ppermute x7, waiting for transfers between devices: 19.3 us -> 21.1 us  [to_owner(): lax.ppermute(array, 'ctx', [(c, c - s - 1) for c in range(s + 1, ctx_coun...]
    ppermute x7, starting transfers between devices: 13.1 us -> 14.7 us  [to_reader(): lax.ppermute(array, 'ctx', [(c - s - 1, c) for c in range(s + 1, ctx_coun...]
    ppermute x4, waiting for transfers between devices: 6.55 us -> 7.75 us  [to_chip(): lax.ppermute(array, 'head', [(h, (h + 2 * d) % heads) for h in range(head...]
  transfers between devices with their start and end apart: 25 -> 25, of which waited for: 12 -> 11; matrix products, arithmetic and copies ran while one was open for 0% -> 0% of each run, Pallas kernels for 17% -> 16%
where the time goes in v2:
time: 104 us
  waiting for transfers between devices  36.6 us (35%)
  starting transfers between devices  28 us (27%)
  Pallas kernels  22.4 us (22%)
  blocking collectives  13.6 us (13%)
  local copies, waits for them, and re-layouts  1.9 us (2%)
    ppermute x7, waiting for transfers between devices, to_owner(): lax.ppermute(array, 'ctx', [(c, c - s - 1) for c in range(s + 1, ctx_coun...  21.1 us
    ppermute x7, starting transfers between devices, to_reader(): lax.ppermute(array, 'ctx', [(c - s - 1, c) for c in range(s + 1, ctx_coun...  14.7 us
    all_to_all x1, blocking collectives, body(): lax.all_to_all(jnp.broadcast_to(selected.reshape(1, 3 * blocks_here), (ct...  13.6 us
    pallas_call x1, Pallas kernels, body(): pl.pallas_call(functools.partial(local_kernel, factor, scaling, blocks_he...  9.44 us
    ppermute x7, starting transfers between devices, to_owner(): lax.ppermute(array, 'ctx', [(c, c - s - 1) for c in range(s + 1, ctx_coun...  9.04 us
    ppermute x4, waiting for transfers between devices, to_chip(): lax.ppermute(array, 'head', [(h, (h + 2 * d) % heads) for h in range(head...  7.75 us
    pallas_call x1, Pallas kernels, body(): pl.pallas_call(functools.partial(local_stats_kernel, factor, blocks_here)...  5.74 us
    ppermute x7, waiting for transfers between devices, swap(): return lax.ppermute(array, 'head', [(h, h ^ 1) for h in range(heads)])  5.65 us
  transfers between devices with their start and end apart: 25, of which 11 were waited for; matrix products, arithmetic and copies ran while one was open for 0% of the time, Pallas kernels for 16%

profile of v2, /device:TPU:0, one launch (start us, length us, event | category | flops | bytes accessed | tf_op | source)
XLA Modules:
  0.0 103.6 jit_solution(432789520768891677)
XLA Ops:
  0.6 0.8 broadcast_in_dim.7
  1.4 13.6 %all_to_all.8 = s32[8,1,12]{2,1,0:T(1,128)} all-to-all(s32[8,1,12]{2,1,0:T(1,128)S(1)} %broadcast_in_dim.8), channel_id=1, replica_groups=mesh['ctx'=8,'head'=4] {'ctx'}, dimensions={0} | all-to-all | bytes 768 | tf_op jit(solution)/shard_map/all_to_all | solution.py:418
  15.0 2.9 %pick_rows.1 = (s32[7]{0:T(128)}, bf16[512,128]{1,0:T(8,128)(2,1)}, bf16[512,128]{1,0:T(8,128)(2,1)}, bf16[256,128]{1,0:T(8,128)(2,1)}, bf16[256,128]{1,0:T(8,12...) custom-call(s32[8,12]{1,0:T(8,128)} %bitcast.34, ...), custom_call_target="tpu_custom_call" | custom-call | tf_op jit(solution)/shard_map/pick_rows/pallas_call | solution.py:422
  17.9 0.0 copy-start
  18.0 2.6 %collective-permute-start = (bf16[256,128]{1,0:T(8,128)(2,1)}, bf16[256,128]{1,0:T(8,128)(2,1)S(1)}, u32[]{:S(2)}, u32[]{:S(2)}) collective-permute-start(bf16[256,128]{1,0:T(8,128)(2,1)} %get-tuple-element.49), channel_id=1, source_target_pairs={{0,12},{4,16},{8,20},{12,24},{16,28},{1,13},{5,17},{9,21},{13,25},... | collective-permute-start | bytes 196616 | tf_op jit(solution)/shard_map/ppermute | solution.py:416
  20.6 2.5 %collective-permute-start.1 = (bf16[256,128]{1,0:T(8,128)(2,1)}, bf16[256,128]{1,0:T(8,128)(2,1)S(1)}, u32[]{:S(2)}, u32[]{:S(2)}) collective-permute-start(bf16[256,128]{1,0:T(8,128)(2,1)} %get-tuple-element.50), channel_id=1, source_target_pairs={{0,16},{4,20},{8,24},{12,28},{1,17},{5,21},{9,25},{13,29},{2,18},{... | collective-permute-start | bytes 196616 | tf_op jit(solution)/shard_map/ppermute | solution.py:416
  23.1 1.3 %collective-permute-start.2 = (bf16[256,128]{1,0:T(8,128)(2,1)}, bf16[256,128]{1,0:T(8,128)(2,1)S(1)}, u32[]{:S(2)}, u32[]{:S(2)}) collective-permute-start(bf16[256,128]{1,0:T(8,128)(2,1)} %get-tuple-element.51), channel_id=1, source_target_pairs={{0,20},{4,24},{8,28},{1,21},{5,25},{9,29},{2,22},{6,26},{10,30},{3... | collective-permute-start | bytes 196616 | tf_op jit(solution)/shard_map/ppermute | solution.py:416
  24.4 1.3 %collective-permute-start.3 = (bf16[256,128]{1,0:T(8,128)(2,1)}, bf16[256,128]{1,0:T(8,128)(2,1)S(1)}, u32[]{:S(2)}, u32[]{:S(2)}) collective-permute-start(bf16[256,128]{1,0:T(8,128)(2,1)} %get-tuple-element.52), channel_id=1, source_target_pairs={{0,24},{4,28},{1,25},{5,29},{2,26},{6,30},{3,27},{7,31}} | collective-permute-start | bytes 196616 | tf_op jit(solution)/shard_map/ppermute | solution.py:416
  25.7 1.3 %collective-permute-start.4 = (bf16[256,128]{1,0:T(8,128)(2,1)}, bf16[256,128]{1,0:T(8,128)(2,1)S(1)}, u32[]{:S(2)}, u32[]{:S(2)}) collective-permute-start(bf16[256,128]{1,0:T(8,128)(2,1)} %get-tuple-element.53), channel_id=1, source_target_pairs={{0,28},{1,29},{2,30},{3,31}} | collective-permute-start | bytes 196616 | tf_op jit(solution)/shard_map/ppermute | solution.py:416
  27.0 0.0 collective-permute-done
  27.0 0.0 collective-permute-done.1
  27.1 0.1 collective-permute-done.2
  27.1 0.0 copy-start.7
  27.2 0.7 collective-permute-done.3
  27.9 1.3 %collective-permute-done.4 = bf16[256,128]{1,0:T(8,128)(2,1)S(1)} collective-permute-done((bf16[256,128]{1,0:T(8,128)(2,1)}, bf16[256,128]{1,0:T(8,128)(2,1)S(1)}, u32[]{:S(2)}, u32[]{:S(2)}) %collective-permute-start.4) | collective-permute-done | bytes 65568 | tf_op jit(solution)/shard_map/ppermute | solution.py:416
  29.2 1.6 %collective-permute-start.9 = (bf16[5,256,128]{2,1,0:T(8,128)(2,1)S(1)}, bf16[5,256,128]{2,1,0:T(8,128)(2,1)S(1)}, u32[]{:S(2)}, u32[]{:S(2)}) collective-permute-start(bf16[5,256,128]{2,1,0:T(8,128)(2,1)S(1)} %bitcast_dynamic-update-slice_fusion.refs_2_), channel_id=1, source_target_pairs={{0,2},{1,3},{2,0},{3,1},{4,6},{5,7},{6,4},{7,5},{8,10},{9,11},{10,... | collective-permute-start | bytes 983048 | tf_op jit(solution)/shard_map/ppermute | solution.py:410
  30.8 1.3 %collective-permute-start.5 = (bf16[512,128]{1,0:T(8,128)(2,1)}, bf16[512,128]{1,0:T(8,128)(2,1)S(1)}, u32[]{:S(2)}, u32[]{:S(2)}) collective-permute-start(bf16[512,128]{1,0:T(8,128)(2,1)} %get-tuple-element.55), channel_id=1, source_target_pairs={{0,4},{4,8},{8,12},{12,16},{16,20},{20,24},{24,28},{1,5},{5,9},{9,... | collective-permute-start | bytes 393224 | tf_op jit(solution)/shard_map/ppermute | solution.py:416
  32.1 0.0 copy-start.2
  32.1 4.4 %collective-permute-start.6 = (bf16[512,128]{1,0:T(8,128)(2,1)S(1)}, bf16[512,128]{1,0:T(8,128)(2,1)S(1)}, u32[]{:S(2)}, u32[]{:S(2)}) collective-permute-start(bf16[512,128]{1,0:T(8,128)(2,1)S(1)} %copy-done.7), channel_id=1, source_target_pairs={{0,8},{4,12},{8,16},{12,20},{16,24},{20,28},{1,9},{5,13},{9,17},{1... | collective-permute-start | bytes 393224 | tf_op jit(solution)/shard_map/ppermute | solution.py:416
  36.5 0.0 copy-start.5
  36.5 1.0 copy-done.5
  37.6 5.7 %local_stats.1.stats = f32[4,8,512]{2,1,0:T(8,128)S(1)} custom-call(s32[4,3]{1,0:T(4,128)S(1)} %copy-done.2, bf16[2048,128]{1,0:T(8,128)(2,1)S(1)} %bitcast.26, bf16[2048,128]{1,0:T(8,128)(2,1)S(1)} %bitcast.29, bf16[4,512,128]{2,1,0:T(8,128)(2,1)S(1)} %bitcast.21, bf16[4,512,128]{2,1,0:T(8,128)(2,1)S(1)} %bitcast.24), custom_call_target="tpu_custom_call" | custom-call | flops 2013265920 | bytes 2097152 | tf_op jit(solution)/shard_map/local_stats/pallas_call | solution.py:436
  43.3 0.0 copy-start.6
  43.3 0.0 collective-permute-done.5
  43.3 0.0 collective-permute-done.6
  43.3 0.1 collective-permute-start.8
  43.4 0.0 collective-permute-done.9.refs_4_
  43.4 0.5 collective-permute-start.10
  43.9 0.2 collective-permute-start.7
  44.1 1.8 %collective-permute-done.7.refs_1_ = bf16[2,512,128]{2,1,0:T(8,128)(2,1)S(1)} collective-permute-done((bf16[2,512,128]{2,1,0:T(8,128)(2,1)S(1)}, bf16[2,512,128]{2,1,0:T(8,128)(2,1)S(1)}, u32[]{:S(2)}, u32[]{:S(2)}) %collective-permute-start.7) | collective-permute-done | bytes 262176 | tf_op jit(solution)/shard_map/ppermute | solution.py:407
  45.9 1.6 %remote_pairs.1 = (bf16[7,512,128]{2,1,0:T(8,128)(2,1)S(1)}, bf16[7,512,128]{2,1,0:T(8,128)(2,1)S(1)}, f32[4,8,512]{2,1,0:T(8,128)S(1)}, f32[4,128,512]{2,1,0:T(8,128)S(1)}) custom-call(s32[4,3]{1,0:T(4,128)S(1)} %copy-done.2, bf16[2048,128]{1,0:T(8,128)(2,1)S(1)} %bitcast.27, bf16[2048,128]{1,0:T(8,128)(2,1)S(1)} %bitcast.30, ...), custom_call_target="tpu_custom_call" | custom-call | flops 4026531840 | bytes 4194304 | tf_op jit(solution)/shard_map/remote_pairs/pallas_call | solution.py:452
  47.5 0.2 collective-permute-start.11
  47.7 2.3 %collective-permute-done.11.theirs = bf16[7,512,128]{2,1,0:T(8,128)(2,1)S(1)} collective-permute-done((bf16[7,512,128]{2,1,0:T(8,128)(2,1)S(1)}, bf16[7,512,128]{2,1,0:T(8,128)(2,1)S(1)}, u32[]{:S(2)}, u32[]{:S(2)}) %collective-permute-start.11) | collective-permute-done | bytes 917536 | tf_op jit(solution)/shard_map/ppermute | solution.py:407
  50.0 0.2 chip_sum.1
  50.2 1.3 %collective-permute-start.13 = (bf16[512,128]{1,0:T(8,128)(2,1)S(1)}, bf16[512,128]{1,0:T(8,128)(2,1)S(1)}, u32[]{:S(2)}, u32[]{:S(2)}) collective-permute-start(bf16[512,128]{1,0:T(8,128)(2,1)S(1)} %get-tuple-element.76), channel_id=1, source_target_pairs={{4,0},{8,4},{12,8},{16,12},{20,16},{24,20},{28,24},{5,1},{9,5},{13... | collective-permute-start | bytes 393224 | tf_op jit(solution)/shard_map/ppermute | solution.py:413
  51.5 1.3 %collective-permute-start.14 = (bf16[512,128]{1,0:T(8,128)(2,1)S(1)}, bf16[512,128]{1,0:T(8,128)(2,1)S(1)}, u32[]{:S(2)}, u32[]{:S(2)}) collective-permute-start(bf16[512,128]{1,0:T(8,128)(2,1)S(1)} %get-tuple-element.77), channel_id=1, source_target_pairs={{8,0},{12,4},{16,8},{20,12},{24,16},{28,20},{9,1},{13,5},{17,9},{2... | collective-permute-start | bytes 393224 | tf_op jit(solution)/shard_map/ppermute | solution.py:413
  52.8 1.3 %collective-permute-start.15 = (bf16[512,128]{1,0:T(8,128)(2,1)S(1)}, bf16[512,128]{1,0:T(8,128)(2,1)S(1)}, u32[]{:S(2)}, u32[]{:S(2)}) collective-permute-start(bf16[512,128]{1,0:T(8,128)(2,1)S(1)} %get-tuple-element.78), channel_id=1, source_target_pairs={{12,0},{16,4},{20,8},{24,12},{28,16},{13,1},{17,5},{21,9},{25,13},... | collective-permute-start | bytes 393224 | tf_op jit(solution)/shard_map/ppermute | solution.py:413
  54.1 0.6 collective-permute-start.12
  54.7 9.4 %local_pairs.1 = (bf16[4,512,128]{2,1,0:T(8,128)(2,1)S(1)}, bf16[4,512,128]{2,1,0:T(8,128)(2,1)S(1)}, bf16[2048,128]{1,0:T(8,128)(2,1)}) custom-call(s32[4,3]{1,0:T(4,128)S(1)} %copy-done.2, bf16[2048,128]{1,0:T(8,128)(2,1)S(1)} %bitcast.28, bf16[2048,128]{1,0:T(8,128)(2,1)S(1)} %bitcast.31, bf16[4,512,128]{2,1,0:T(8,128)(2,1)S(1)} %bitcast.22, ...), custom_call_target="tpu_custom_call" | custom-call | flops 4026531840 | bytes 4194304 | tf_op jit(solution)/shard_map/local_pairs/pallas_call | solution.py:495
  64.2 3.0 %collective-permute-done.14.refs_1_ = bf16[512,128]{1,0:T(8,128)(2,1)S(1)} collective-permute-done((bf16[512,128]{1,0:T(8,128)(2,1)S(1)}, bf16[512,128]{1,0:T(8,128)(2,1)S(1)}, u32[]{:S(2)}, u32[]{:S(2)}) %collective-permute-start.14) | collective-permute-done | bytes 131104 | tf_op jit(solution)/shard_map/ppermute | solution.py:413
  67.1 4.8 %collective-permute-done.15.refs_2_ = bf16[512,128]{1,0:T(8,128)(2,1)S(1)} collective-permute-done((bf16[512,128]{1,0:T(8,128)(2,1)S(1)}, bf16[512,128]{1,0:T(8,128)(2,1)S(1)}, u32[]{:S(2)}, u32[]{:S(2)}) %collective-permute-start.15) | collective-permute-done | bytes 131104 | tf_op jit(solution)/shard_map/ppermute | solution.py:413
  71.9 0.0 collective-permute-done.12.refs_0_
  71.9 0.0 collective-permute-start.20
  72.0 1.3 %collective-permute-start.16 = (bf16[256,128]{1,0:T(8,128)(2,1)S(1)}, bf16[256,128]{1,0:T(8,128)(2,1)S(1)}, u32[]{:S(2)}, u32[]{:S(2)}) collective-permute-start(bf16[256,128]{1,0:T(8,128)(2,1)S(1)} %get-tuple-element.82), channel_id=1, source_target_pairs={{16,0},{20,4},{24,8},{28,12},{17,1},{21,5},{25,9},{29,13},{18,2},{... | collective-permute-start | bytes 196616 | tf_op jit(solution)/shard_map/ppermute | solution.py:413
  73.3 1.3 %collective-permute-start.17 = (bf16[256,128]{1,0:T(8,128)(2,1)S(1)}, bf16[256,128]{1,0:T(8,128)(2,1)S(1)}, u32[]{:S(2)}, u32[]{:S(2)}) collective-permute-start(bf16[256,128]{1,0:T(8,128)(2,1)S(1)} %get-tuple-element.83), channel_id=1, source_target_pairs={{20,0},{24,4},{28,8},{21,1},{25,5},{29,9},{22,2},{26,6},{30,10},{2... | collective-permute-start | bytes 196616 | tf_op jit(solution)/shard_map/ppermute | solution.py:413
  74.6 1.3 %collective-permute-start.18 = (bf16[256,128]{1,0:T(8,128)(2,1)S(1)}, bf16[256,128]{1,0:T(8,128)(2,1)S(1)}, u32[]{:S(2)}, u32[]{:S(2)}) collective-permute-start(bf16[256,128]{1,0:T(8,128)(2,1)S(1)} %get-tuple-element.84), channel_id=1, source_target_pairs={{24,0},{28,4},{25,1},{29,5},{26,2},{30,6},{27,3},{31,7}} | collective-permute-start | bytes 196616 | tf_op jit(solution)/shard_map/ppermute | solution.py:413
  75.9 1.3 %collective-permute-start.19 = (bf16[256,128]{1,0:T(8,128)(2,1)S(1)}, bf16[256,128]{1,0:T(8,128)(2,1)S(1)}, u32[]{:S(2)}, u32[]{:S(2)}) collective-permute-start(bf16[256,128]{1,0:T(8,128)(2,1)S(1)} %get-tuple-element.85), channel_id=1, source_target_pairs={{28,0},{29,1},{30,2},{31,3}} | collective-permute-start | bytes 196616 | tf_op jit(solution)/shard_map/ppermute | solution.py:413
  77.2 0.0 collective-permute-done.20.theirs
  77.2 0.8 own_sum.1
  78.0 0.6 collective-permute-start.21
  78.6 4.0 %collective-permute-done.16.refs_0_ = bf16[256,128]{1,0:T(8,128)(2,1)S(1)} collective-permute-done((bf16[256,128]{1,0:T(8,128)(2,1)S(1)}, bf16[256,128]{1,0:T(8,128)(2,1)S(1)}, u32[]{:S(2)}, u32[]{:S(2)}) %collective-permute-start.16) | collective-permute-done | bytes 65568 | tf_op jit(solution)/shard_map/ppermute | solution.py:413
  82.6 9.3 %collective-permute-done.17.refs_1_ = bf16[256,128]{1,0:T(8,128)(2,1)S(1)} collective-permute-done((bf16[256,128]{1,0:T(8,128)(2,1)S(1)}, bf16[256,128]{1,0:T(8,128)(2,1)S(1)}, u32[]{:S(2)}, u32[]{:S(2)}) %collective-permute-start.17) | collective-permute-done | bytes 65568 | tf_op jit(solution)/shard_map/ppermute | solution.py:413
  91.9 0.0 collective-permute-done.18.refs_2_
  91.9 0.0 collective-permute-done.19.refs_3_
  91.9 0.6 far_returns.1.returned
  92.6 0.0 collective-permute-done.21.refs_0_
  92.6 0.1 owner_sum.1.refs_0_
  92.7 0.6 collective-permute-start.23
  93.3 0.0 collective-permute-start.22
  93.3 7.7 %collective-permute-done.23.refs_2_ = bf16[4,256,128]{2,1,0:T(8,128)(2,1)S(1)} collective-permute-done((bf16[4,256,128]{2,1,0:T(8,128)(2,1)S(1)}, bf16[4,256,128]{2,1,0:T(8,128)(2,1)S(1)}, u32[]{:S(2)}, u32[]{:S(2)}) %collective-permute-start.23) | collective-permute-done | bytes 262176 | tf_op jit(solution)/shard_map/ppermute | solution.py:410
  101.0 0.0 collective-permute-start.24
  101.0 0.0 collective-permute-done.22.refs_1_
  101.0 1.5 %collective-permute-done.24.refs_3_ = bf16[4,256,128]{2,1,0:T(8,128)(2,1)S(1)} collective-permute-done((bf16[4,256,128]{2,1,0:T(8,128)(2,1)S(1)}, bf16[4,256,128]{2,1,0:T(8,128)(2,1)S(1)}, u32[]{:S(2)}, u32[]{:S(2)}) %collective-permute-start.24) | collective-permute-done | bytes 262176 | tf_op jit(solution)/shard_map/ppermute | solution.py:407
  102.5 1.0 %spread.1 = (bf16[4,512,128]{2,1,0:T(8,128)(2,1)}, bf16[4,512,128]{2,1,0:T(8,128)(2,1)}) custom-call(bf16[4,256,128]{2,1,0:T(8,128)(2,1)S(1)} %owner_sum.1.refs_0_, bf16[4,256,128]{2,1,0:T(8,128)(2,1)S(1)} %collective-permute-done.22.refs_1_, bf16[4,256,128]{2,1,0:T(8,128)(2,1)S(1)} %collective-permute-done.23.refs_2_, ...), custom_call_target="tpu_custom_call" | custom-call | tf_op jit(solution)/shard_map/spread/pallas_call | solution.py:545
  (21 shorter events, 0.2 us)
Async XLA Ops:
  15.0 21.4 %copy-start.1 = (bf16[2048,128]{1,0:T(8,128)(2,1)S(1)}, bf16[2048,128]{1,0:T(8,128)(2,1)}, u32[]{:S(2)}) copy-start(bf16[2048,128]{1,0:T(8,128)(2,1)} %param.7) | copy-start | bytes 1572868
  15.0 21.4 %copy-start.4 = (bf16[2048,1,128]{2,0,1:T(8,128)(2,1)S(1)}, bf16[2048,1,128]{2,0,1:T(8,128)(2,1)}, u32[]{:S(2)}) copy-start(bf16[2048,1,128]{2,0,1:T(8,128)(2,1)} %param.5) | copy-start | bytes 1572868
  17.9 18.6 %copy-start = (bf16[2048,128]{1,0:T(8,128)(2,1)S(1)}, bf16[2048,128]{1,0:T(8,128)(2,1)}, u32[]{:S(2)}) copy-start(bf16[2048,128]{1,0:T(8,128)(2,1)} %param.6) | copy-start | bytes 1572868
  18.0 9.1 %collective-permute-start = (bf16[256,128]{1,0:T(8,128)(2,1)}, bf16[256,128]{1,0:T(8,128)(2,1)S(1)}, u32[]{:S(2)}, u32[]{:S(2)}) collective-permute-start(bf16[256,128]{1,0:T(8,128)(2,1)} %get-tuple-element.49), channel_id=1, source_target_pairs={{0,12},{4,16},{8,20},{12,24},{16,28},{1,13},{5,17},{9,21},{13,25},... | collective-permute-start | bytes 196616 | tf_op jit(solution)/shard_map/ppermute | solution.py:416
  20.6 6.5 %collective-permute-start.1 = (bf16[256,128]{1,0:T(8,128)(2,1)}, bf16[256,128]{1,0:T(8,128)(2,1)S(1)}, u32[]{:S(2)}, u32[]{:S(2)}) collective-permute-start(bf16[256,128]{1,0:T(8,128)(2,1)} %get-tuple-element.50), channel_id=1, source_target_pairs={{0,16},{4,20},{8,24},{12,28},{1,17},{5,21},{9,25},{13,29},{2,18},{... | collective-permute-start | bytes 196616 | tf_op jit(solution)/shard_map/ppermute | solution.py:416
  23.1 4.0 %collective-permute-start.2 = (bf16[256,128]{1,0:T(8,128)(2,1)}, bf16[256,128]{1,0:T(8,128)(2,1)S(1)}, u32[]{:S(2)}, u32[]{:S(2)}) collective-permute-start(bf16[256,128]{1,0:T(8,128)(2,1)} %get-tuple-element.51), channel_id=1, source_target_pairs={{0,20},{4,24},{8,28},{1,21},{5,25},{9,29},{2,22},{6,26},{10,30},{3... | collective-permute-start | bytes 196616 | tf_op jit(solution)/shard_map/ppermute | solution.py:416
  24.4 3.5 %collective-permute-start.3 = (bf16[256,128]{1,0:T(8,128)(2,1)}, bf16[256,128]{1,0:T(8,128)(2,1)S(1)}, u32[]{:S(2)}, u32[]{:S(2)}) collective-permute-start(bf16[256,128]{1,0:T(8,128)(2,1)} %get-tuple-element.52), channel_id=1, source_target_pairs={{0,24},{4,28},{1,25},{5,29},{2,26},{6,30},{3,27},{7,31}} | collective-permute-start | bytes 196616 | tf_op jit(solution)/shard_map/ppermute | solution.py:416
  25.7 3.5 %collective-permute-start.4 = (bf16[256,128]{1,0:T(8,128)(2,1)}, bf16[256,128]{1,0:T(8,128)(2,1)S(1)}, u32[]{:S(2)}, u32[]{:S(2)}) collective-permute-start(bf16[256,128]{1,0:T(8,128)(2,1)} %get-tuple-element.53), channel_id=1, source_target_pairs={{0,28},{1,29},{2,30},{3,31}} | collective-permute-start | bytes 196616 | tf_op jit(solution)/shard_map/ppermute | solution.py:416
  27.1 4.9 %copy-start.7 = (bf16[512,128]{1,0:T(8,128)(2,1)S(1)}, bf16[512,128]{1,0:T(8,128)(2,1)}, u32[]{:S(2)}) copy-start(bf16[512,128]{1,0:T(8,128)(2,1)} %get-tuple-element.56) | copy-start | bytes 393220
  29.2 14.2 %collective-permute-start.9 = (bf16[5,256,128]{2,1,0:T(8,128)(2,1)S(1)}, bf16[5,256,128]{2,1,0:T(8,128)(2,1)S(1)}, u32[]{:S(2)}, u32[]{:S(2)}) collective-permute-start(bf16[5,256,128]{2,1,0:T(8,128)(2,1)S(1)} %bitcast_dynamic-update-slice_fusion.refs_2_), channel_id=1, source_target_pairs={{0,2},{1,3},{2,0},{3,1},{4,6},{5,7},{6,4},{7,5},{8,10},{9,11},{10,... | collective-permute-start | bytes 983048 | tf_op jit(solution)/shard_map/ppermute | solution.py:410
  30.8 12.5 %collective-permute-start.5 = (bf16[512,128]{1,0:T(8,128)(2,1)}, bf16[512,128]{1,0:T(8,128)(2,1)S(1)}, u32[]{:S(2)}, u32[]{:S(2)}) collective-permute-start(bf16[512,128]{1,0:T(8,128)(2,1)} %get-tuple-element.55), channel_id=1, source_target_pairs={{0,4},{4,8},{8,12},{12,16},{16,20},{20,24},{24,28},{1,5},{5,9},{9,... | collective-permute-start | bytes 393224 | tf_op jit(solution)/shard_map/ppermute | solution.py:416
  32.1 4.4 %copy-start.2 = (s32[4,3]{1,0:T(4,128)S(1)}, s32[4,3]{1,0:T(4,128)}, u32[]{:S(2)}) copy-start(s32[4,3]{1,0:T(4,128)} %chosen.2) | copy-start | bytes 148
  32.1 11.2 %collective-permute-start.6 = (bf16[512,128]{1,0:T(8,128)(2,1)S(1)}, bf16[512,128]{1,0:T(8,128)(2,1)S(1)}, u32[]{:S(2)}, u32[]{:S(2)}) collective-permute-start(bf16[512,128]{1,0:T(8,128)(2,1)S(1)} %copy-done.7), channel_id=1, source_target_pairs={{0,8},{4,12},{8,16},{12,20},{16,24},{20,28},{1,9},{5,13},{9,17},{1... | collective-permute-start | bytes 393224 | tf_op jit(solution)/shard_map/ppermute | solution.py:416
  36.5 1.0 %copy-start.5 = (bf16[2048,1,128]{2,0,1:T(8,128)(2,1)S(1)}, bf16[2048,1,128]{2,0,1:T(8,128)(2,1)}, u32[]{:S(2)}) copy-start(bf16[2048,1,128]{2,0,1:T(8,128)(2,1)} %param.8) | copy-start | bytes 1572868
  43.3 2.6 %copy-start.6 = (bf16[2048,1,128]{2,0,1:T(8,128)(2,1)S(1)}, bf16[2048,1,128]{2,0,1:T(8,128)(2,1)}, u32[]{:S(2)}) copy-start(bf16[2048,1,128]{2,0,1:T(8,128)(2,1)} %param.8) | copy-start | bytes 1572868
  43.3 2.5 %collective-permute-start.8 = (bf16[5,256,128]{2,1,0:T(8,128)(2,1)S(1)}, bf16[5,256,128]{2,1,0:T(8,128)(2,1)S(1)}, u32[]{:S(2)}, u32[]{:S(2)}) collective-permute-start(bf16[5,256,128]{2,1,0:T(8,128)(2,1)S(1)} %bitcast_dynamic-update-slice_fusion.refs_2_), channel_id=1, source_target_pairs={{0,1},{1,0},{2,3},{3,2},{4,5},{5,4},{6,7},{7,6},{8,9},{9,8},{10,11... | collective-permute-start | bytes 983048 | tf_op jit(solution)/shard_map/ppermute | solution.py:407
  43.4 2.5 %collective-permute-start.10 = (bf16[5,256,128]{2,1,0:T(8,128)(2,1)S(1)}, bf16[5,256,128]{2,1,0:T(8,128)(2,1)S(1)}, u32[]{:S(2)}, u32[]{:S(2)}) collective-permute-start(bf16[5,256,128]{2,1,0:T(8,128)(2,1)S(1)} %collective-permute-done.9.refs_4_), channel_id=1, source_target_pairs={{0,1},{1,0},{2,3},{3,2},{4,5},{5,4},{6,7},{7,6},{8,9},{9,8},{10,11... | collective-permute-start | bytes 983048 | tf_op jit(solution)/shard_map/ppermute | solution.py:407
  43.9 1.9 %collective-permute-start.7 = (bf16[2,512,128]{2,1,0:T(8,128)(2,1)S(1)}, bf16[2,512,128]{2,1,0:T(8,128)(2,1)S(1)}, u32[]{:S(2)}, u32[]{:S(2)}) collective-permute-start(bf16[2,512,128]{2,1,0:T(8,128)(2,1)S(1)} %pad_maximum_fusion.refs_0_), channel_id=1, source_target_pairs={{0,1},{1,0},{2,3},{3,2},{4,5},{5,4},{6,7},{7,6},{8,9},{9,8},{10,11... | collective-permute-start | bytes 786440 | tf_op jit(solution)/shard_map/ppermute | solution.py:407
  47.5 2.5 %collective-permute-start.11 = (bf16[7,512,128]{2,1,0:T(8,128)(2,1)S(1)}, bf16[7,512,128]{2,1,0:T(8,128)(2,1)S(1)}, u32[]{:S(2)}, u32[]{:S(2)}) collective-permute-start(bf16[7,512,128]{2,1,0:T(8,128)(2,1)S(1)} %get-tuple-element.63), channel_id=1, source_target_pairs={{0,1},{1,0},{2,3},{3,2},{4,5},{5,4},{6,7},{7,6},{8,9},{9,8},{10,11... | collective-permute-start | bytes 2752520 | tf_op jit(solution)/shard_map/ppermute | solution.py:407
  50.2 13.9 %collective-permute-start.13 = (bf16[512,128]{1,0:T(8,128)(2,1)S(1)}, bf16[512,128]{1,0:T(8,128)(2,1)S(1)}, u32[]{:S(2)}, u32[]{:S(2)}) collective-permute-start(bf16[512,128]{1,0:T(8,128)(2,1)S(1)} %get-tuple-element.76), channel_id=1, source_target_pairs={{4,0},{8,4},{12,8},{16,12},{20,16},{24,20},{28,24},{5,1},{9,5},{13... | collective-permute-start | bytes 393224 | tf_op jit(solution)/shard_map/ppermute | solution.py:413
  51.5 15.6 %collective-permute-start.14 = (bf16[512,128]{1,0:T(8,128)(2,1)S(1)}, bf16[512,128]{1,0:T(8,128)(2,1)S(1)}, u32[]{:S(2)}, u32[]{:S(2)}) collective-permute-start(bf16[512,128]{1,0:T(8,128)(2,1)S(1)} %get-tuple-element.77), channel_id=1, source_target_pairs={{8,0},{12,4},{16,8},{20,12},{24,16},{28,20},{9,1},{13,5},{17,9},{2... | collective-permute-start | bytes 393224 | tf_op jit(solution)/shard_map/ppermute | solution.py:413
  52.8 19.1 %collective-permute-start.15 = (bf16[512,128]{1,0:T(8,128)(2,1)S(1)}, bf16[512,128]{1,0:T(8,128)(2,1)S(1)}, u32[]{:S(2)}, u32[]{:S(2)}) collective-permute-start(bf16[512,128]{1,0:T(8,128)(2,1)S(1)} %get-tuple-element.78), channel_id=1, source_target_pairs={{12,0},{16,4},{20,8},{24,12},{28,16},{13,1},{17,5},{21,9},{25,13},... | collective-permute-start | bytes 393224 | tf_op jit(solution)/shard_map/ppermute | solution.py:413
  54.1 17.8 %collective-permute-start.12 = (bf16[4,256,128]{2,1,0:T(8,128)(2,1)S(1)}, bf16[4,256,128]{2,1,0:T(8,128)(2,1)S(1)}, u32[]{:S(2)}, u32[]{:S(2)}) collective-permute-start(bf16[4,256,128]{2,1,0:T(8,128)(2,1)S(1)} %get-tuple-element.75), channel_id=1, source_target_pairs={{0,2},{1,3},{2,0},{3,1},{4,6},{5,7},{6,4},{7,5},{8,10},{9,11},{10,... | collective-permute-start | bytes 786440 | tf_op jit(solution)/shard_map/ppermute | solution.py:410
  71.9 5.3 %collective-permute-start.20 = (bf16[4,512,128]{2,1,0:T(8,128)(2,1)S(1)}, bf16[4,512,128]{2,1,0:T(8,128)(2,1)S(1)}, u32[]{:S(2)}, u32[]{:S(2)}) collective-permute-start(bf16[4,512,128]{2,1,0:T(8,128)(2,1)S(1)} %get-tuple-element.87), channel_id=1, source_target_pairs={{0,1},{1,0},{2,3},{3,2},{4,5},{5,4},{6,7},{7,6},{8,9},{9,8},{10,11... | collective-permute-start | bytes 1572872 | tf_op jit(solution)/shard_map/ppermute | solution.py:407
  72.0 10.6 %collective-permute-start.16 = (bf16[256,128]{1,0:T(8,128)(2,1)S(1)}, bf16[256,128]{1,0:T(8,128)(2,1)S(1)}, u32[]{:S(2)}, u32[]{:S(2)}) collective-permute-start(bf16[256,128]{1,0:T(8,128)(2,1)S(1)} %get-tuple-element.82), channel_id=1, source_target_pairs={{16,0},{20,4},{24,8},{28,12},{17,1},{21,5},{25,9},{29,13},{18,2},{... | collective-permute-start | bytes 196616 | tf_op jit(solution)/shard_map/ppermute | solution.py:413
  73.3 18.6 %collective-permute-start.17 = (bf16[256,128]{1,0:T(8,128)(2,1)S(1)}, bf16[256,128]{1,0:T(8,128)(2,1)S(1)}, u32[]{:S(2)}, u32[]{:S(2)}) collective-permute-start(bf16[256,128]{1,0:T(8,128)(2,1)S(1)} %get-tuple-element.83), channel_id=1, source_target_pairs={{20,0},{24,4},{28,8},{21,1},{25,5},{29,9},{22,2},{26,6},{30,10},{2... | collective-permute-start | bytes 196616 | tf_op jit(solution)/shard_map/ppermute | solution.py:413
  74.6 17.3 %collective-permute-start.18 = (bf16[256,128]{1,0:T(8,128)(2,1)S(1)}, bf16[256,128]{1,0:T(8,128)(2,1)S(1)}, u32[]{:S(2)}, u32[]{:S(2)}) collective-permute-start(bf16[256,128]{1,0:T(8,128)(2,1)S(1)} %get-tuple-element.84), channel_id=1, source_target_pairs={{24,0},{28,4},{25,1},{29,5},{26,2},{30,6},{27,3},{31,7}} | collective-permute-start | bytes 196616 | tf_op jit(solution)/shard_map/ppermute | solution.py:413
  75.9 1.3 %copy-start.3 = (s32[7]{0:T(128)S(1)}, s32[7]{0:T(128)}, u32[]{:S(2)}) copy-start(s32[7]{0:T(128)} %get-tuple-element.73.asked) | copy-start | bytes 88
  75.9 16.0 %collective-permute-start.19 = (bf16[256,128]{1,0:T(8,128)(2,1)S(1)}, bf16[256,128]{1,0:T(8,128)(2,1)S(1)}, u32[]{:S(2)}, u32[]{:S(2)}) collective-permute-start(bf16[256,128]{1,0:T(8,128)(2,1)S(1)} %get-tuple-element.85), channel_id=1, source_target_pairs={{28,0},{29,1},{30,2},{31,3}} | collective-permute-start | bytes 196616 | tf_op jit(solution)/shard_map/ppermute | solution.py:413
  78.0 14.6 %collective-permute-start.21 = (bf16[4,256,128]{2,1,0:T(8,128)(2,1)S(1)}, bf16[4,256,128]{2,1,0:T(8,128)(2,1)S(1)}, u32[]{:S(2)}, u32[]{:S(2)}) collective-permute-start(bf16[4,256,128]{2,1,0:T(8,128)(2,1)S(1)} %get-tuple-element.92), channel_id=1, source_target_pairs={{0,2},{1,3},{2,0},{3,1},{4,6},{5,7},{6,4},{7,5},{8,10},{9,11},{10,... | collective-permute-start | bytes 786440 | tf_op jit(solution)/shard_map/ppermute | solution.py:410
  92.7 8.3 %collective-permute-start.23 = (bf16[4,256,128]{2,1,0:T(8,128)(2,1)S(1)}, bf16[4,256,128]{2,1,0:T(8,128)(2,1)S(1)}, u32[]{:S(2)}, u32[]{:S(2)}) collective-permute-start(bf16[4,256,128]{2,1,0:T(8,128)(2,1)S(1)} %owner_sum.1.refs_0_), channel_id=1, source_target_pairs={{0,2},{1,3},{2,0},{3,1},{4,6},{5,7},{6,4},{7,5},{8,10},{9,11},{10,... | collective-permute-start | bytes 786440 | tf_op jit(solution)/shard_map/ppermute | solution.py:410
  93.3 7.8 %collective-permute-start.22 = (bf16[4,256,128]{2,1,0:T(8,128)(2,1)S(1)}, bf16[4,256,128]{2,1,0:T(8,128)(2,1)S(1)}, u32[]{:S(2)}, u32[]{:S(2)}) collective-permute-start(bf16[4,256,128]{2,1,0:T(8,128)(2,1)S(1)} %owner_sum.1.refs_0_), channel_id=1, source_target_pairs={{0,1},{1,0},{2,3},{3,2},{4,5},{5,4},{6,7},{7,6},{8,9},{9,8},{10,11... | collective-permute-start | bytes 786440 | tf_op jit(solution)/shard_map/ppermute | solution.py:407
  101.0 1.5 %collective-permute-start.24 = (bf16[4,256,128]{2,1,0:T(8,128)(2,1)S(1)}, bf16[4,256,128]{2,1,0:T(8,128)(2,1)S(1)}, u32[]{:S(2)}, u32[]{:S(2)}) collective-permute-start(bf16[4,256,128]{2,1,0:T(8,128)(2,1)S(1)} %collective-permute-done.23.refs_2_), channel_id=1, source_target_pairs={{0,1},{1,0},{2,3},{3,2},{4,5},{5,4},{6,7},{7,6},{8,9},{9,8},{10,11... | collective-permute-start | bytes 786440 | tf_op jit(solution)/shard_map/ppermute | solution.py:407

commit v3 on v1

--- a/solution.py
+++ b/solution.py
@@ -370,8 +370,8 @@
     scaling = 1.0 / math.sqrt(feature)
     factor = scaling * math.log2(math.e)
     shifts = ctx_count - 1
-    far = [s for s in range(shifts) if 2 * (s + 1) >= ctx_count]
-    near = [s for s in range(shifts) if 2 * (s + 1) < ctx_count]
+    far = [s for s in range(shifts - 1) if 2 * (s + 2) >= ctx_count]
+    near = [s for s in range(shifts) if s not in far]
 
     q2 = queries.reshape(tok_rows, feature)
     do2 = dout.reshape(tok_rows, feature)
@@ -448,7 +448,9 @@
         row_sets += [part, swap(part)]
 
     keep_far, send_far, final, grad_qt = pl.pallas_call(
-        functools.partial(remote_kernel, factor, scaling, blocks_here, chips, far, near, piece),
+        functools.partial(
+            remote_kernel, factor, scaling, blocks_here, chips, far, near, piece
+        ),
         in_specs=[smem] + [whole] * (3 + len(row_sets)),
         out_specs=[whole] * 4,
         out_shape=[far_type, far_type, stat_type, qt_type],

time: 99.1 us -> 96.1 us (0.970); the launches traced: 98 us -> 96.4 us
  waiting for transfers between devices: 31.6 us -> 26.9 us
  starting transfers between devices: 27.4 us -> 30.5 us
    ppermute x7, waiting for transfers between devices: 19.3 us -> 14.1 us  [to_owner(): lax.ppermute(array, 'ctx', [(c, c - s - 1) for c in range(s + 1, ctx_coun...]
    ppermute x7, starting transfers between devices: 13.1 us -> 16.6 us  [to_reader(): lax.ppermute(array, 'ctx', [(c - s - 1, c) for c in range(s + 1, ctx_coun...]
  transfers between devices with their start and end apart: 25 -> 25, of which waited for: 12 -> 9; matrix products, arithmetic and copies ran while one was open for 0% -> 0% of each run, Pallas kernels for 17% -> 17%
where the time goes in v3:
time: 96.1 us; the launch traced here: 96.4 us
  starting transfers between devices  30.5 us (32%)
  waiting for transfers between devices  26.9 us (28%)
  Pallas kernels  22.5 us (23%)
  blocking collectives  13.6 us (14%)
  local copies, waits for them, and re-layouts  1.84 us (2%)
    ppermute x7, starting transfers between devices, to_reader(): lax.ppermute(array, 'ctx', [(c - s - 1, c) for c in range(s + 1, ctx_coun...  16.6 us
    ppermute x7, waiting for transfers between devices, to_owner(): lax.ppermute(array, 'ctx', [(c, c - s - 1) for c in range(s + 1, ctx_coun...  14.1 us
    all_to_all x1, blocking collectives, body(): lax.all_to_all(jnp.broadcast_to(selected.reshape(1, 3 * blocks_here), (ct...  13.6 us
    pallas_call x1, Pallas kernels, body(): pl.pallas_call(functools.partial(local_kernel, factor, scaling, blocks_he...  9.44 us
    ppermute x7, starting transfers between devices, to_owner(): lax.ppermute(array, 'ctx', [(c, c - s - 1) for c in range(s + 1, ctx_coun...  9.04 us
    ppermute x4, waiting for transfers between devices, to_chip(): lax.ppermute(array, 'head', [(h, (h + 2 * d) % heads) for h in range(head...  7.11 us
    ppermute x7, waiting for transfers between devices, swap(): return lax.ppermute(array, 'head', [(h, h ^ 1) for h in range(heads)])  5.75 us
    pallas_call x1, Pallas kernels, body(): pl.pallas_call(functools.partial(local_stats_kernel, factor, blocks_here)...  5.73 us
  transfers between devices with their start and end apart: 25, of which 9 were waited for; matrix products, arithmetic and copies ran while one was open for 0% of the time, Pallas kernels for 17%

profile of v3, /device:TPU:0, one launch (start us, length us, event | category | flops | bytes accessed | tf_op | source)
XLA Modules:
  0.0 96.4 jit_solution(17071023342491942108)
XLA Ops:
  0.6 0.8 broadcast_in_dim.7
  1.4 13.6 %all_to_all.8 = s32[8,1,12]{2,1,0:T(1,128)} all-to-all(s32[8,1,12]{2,1,0:T(1,128)S(1)} %broadcast_in_dim.8), channel_id=1, replica_groups=mesh['ctx'=8,'head'=4] {'ctx'}, dimensions={0} | all-to-all | bytes 768 | tf_op jit(solution)/shard_map/all_to_all | solution.py:416
  15.0 3.0 %pick_rows.1 = (s32[7]{0:T(128)}, bf16[512,128]{1,0:T(8,128)(2,1)}, bf16[512,128]{1,0:T(8,128)(2,1)}, bf16[256,128]{1,0:T(8,128)(2,1)}, bf16[256,128]{1,0:T(8,12...) custom-call(s32[8,12]{1,0:T(8,128)} %bitcast.34, ...), custom_call_target="tpu_custom_call" | custom-call | tf_op jit(solution)/shard_map/pick_rows/pallas_call | solution.py:420
  18.1 0.0 copy-start
  18.1 2.6 %collective-permute-start = (bf16[256,128]{1,0:T(8,128)(2,1)}, bf16[256,128]{1,0:T(8,128)(2,1)S(1)}, u32[]{:S(2)}, u32[]{:S(2)}) collective-permute-start(bf16[256,128]{1,0:T(8,128)(2,1)} %get-tuple-element.50), channel_id=1, source_target_pairs={{0,12},{4,16},{8,20},{12,24},{16,28},{1,13},{5,17},{9,21},{13,25},... | collective-permute-start | bytes 196616 | tf_op jit(solution)/shard_map/ppermute | solution.py:414
  20.7 2.5 %collective-permute-start.1 = (bf16[256,128]{1,0:T(8,128)(2,1)}, bf16[256,128]{1,0:T(8,128)(2,1)S(1)}, u32[]{:S(2)}, u32[]{:S(2)}) collective-permute-start(bf16[256,128]{1,0:T(8,128)(2,1)} %get-tuple-element.51), channel_id=1, source_target_pairs={{0,16},{4,20},{8,24},{12,28},{1,17},{5,21},{9,25},{13,29},{2,18},{... | collective-permute-start | bytes 196616 | tf_op jit(solution)/shard_map/ppermute | solution.py:414
  23.2 1.3 %collective-permute-start.2 = (bf16[256,128]{1,0:T(8,128)(2,1)}, bf16[256,128]{1,0:T(8,128)(2,1)S(1)}, u32[]{:S(2)}, u32[]{:S(2)}) collective-permute-start(bf16[256,128]{1,0:T(8,128)(2,1)} %get-tuple-element.52), channel_id=1, source_target_pairs={{0,20},{4,24},{8,28},{1,21},{5,25},{9,29},{2,22},{6,26},{10,30},{3... | collective-permute-start | bytes 196616 | tf_op jit(solution)/shard_map/ppermute | solution.py:414
  24.5 1.3 %collective-permute-start.3 = (bf16[256,128]{1,0:T(8,128)(2,1)}, bf16[256,128]{1,0:T(8,128)(2,1)S(1)}, u32[]{:S(2)}, u32[]{:S(2)}) collective-permute-start(bf16[256,128]{1,0:T(8,128)(2,1)} %get-tuple-element.53), channel_id=1, source_target_pairs={{0,24},{4,28},{1,25},{5,29},{2,26},{6,30},{3,27},{7,31}} | collective-permute-start | bytes 196616 | tf_op jit(solution)/shard_map/ppermute | solution.py:414
  25.8 2.2 %collective-permute-start.4 = (bf16[512,128]{1,0:T(8,128)(2,1)}, bf16[512,128]{1,0:T(8,128)(2,1)S(1)}, u32[]{:S(2)}, u32[]{:S(2)}) collective-permute-start(bf16[512,128]{1,0:T(8,128)(2,1)} %get-tuple-element.55), channel_id=1, source_target_pairs={{0,4},{4,8},{8,12},{12,16},{16,20},{20,24},{24,28},{1,5},{5,9},{9,... | collective-permute-start | bytes 393224 | tf_op jit(solution)/shard_map/ppermute | solution.py:414
  28.0 0.0 collective-permute-done
  28.0 1.3 %collective-permute-start.5 = (bf16[512,128]{1,0:T(8,128)(2,1)}, bf16[512,128]{1,0:T(8,128)(2,1)S(1)}, u32[]{:S(2)}, u32[]{:S(2)}) collective-permute-start(bf16[512,128]{1,0:T(8,128)(2,1)} %get-tuple-element.56), channel_id=1, source_target_pairs={{0,8},{4,12},{8,16},{12,20},{16,24},{20,28},{1,9},{5,13},{9,17},{1... | collective-permute-start | bytes 393224 | tf_op jit(solution)/shard_map/ppermute | solution.py:414
  29.3 0.0 collective-permute-done.1
  29.3 5.3 %collective-permute-start.6 = (bf16[512,128]{1,0:T(8,128)(2,1)}, bf16[512,128]{1,0:T(8,128)(2,1)S(1)}, u32[]{:S(2)}, u32[]{:S(2)}) collective-permute-start(bf16[512,128]{1,0:T(8,128)(2,1)} %get-tuple-element.57), channel_id=1, source_target_pairs={{0,28},{1,29},{2,30},{3,31}} | collective-permute-start | bytes 393224 | tf_op jit(solution)/shard_map/ppermute | solution.py:414
  34.7 0.0 collective-permute-done.2
  34.7 0.0 collective-permute-done.3
  34.8 0.0 copy-start.2
  34.8 1.6 %collective-permute-start.9 = (bf16[4,256,128]{2,1,0:T(8,128)(2,1)S(1)}, bf16[4,256,128]{2,1,0:T(8,128)(2,1)S(1)}, u32[]{:S(2)}, u32[]{:S(2)}) collective-permute-start(bf16[4,256,128]{2,1,0:T(8,128)(2,1)S(1)} %pad_maximum_fusion.1.refs_2_), channel_id=1, source_target_pairs={{0,2},{1,3},{2,0},{3,1},{4,6},{5,7},{6,4},{7,5},{8,10},{9,11},{10,... | collective-permute-start | bytes 786440 | tf_op jit(solution)/shard_map/ppermute | solution.py:408
  36.4 0.0 copy-start.5
  36.4 1.0 %copy-done.5 = bf16[2048,1,128]{2,0,1:T(8,128)(2,1)S(1)} copy-done((bf16[2048,1,128]{2,0,1:T(8,128)(2,1)S(1)}, bf16[2048,1,128]{2,0,1:T(8,128)(2,1)}, u32[]{:S(2)}) %copy-start.5) | copy-done | bytes 524312
  37.4 5.7 %local_stats.1.stats = f32[4,8,512]{2,1,0:T(8,128)S(1)} custom-call(s32[4,3]{1,0:T(4,128)S(1)} %copy-done.2, bf16[2048,128]{1,0:T(8,128)(2,1)S(1)} %bitcast.21, bf16[2048,128]{1,0:T(8,128)(2,1)S(1)} %bitcast.24, bf16[4,512,128]{2,1,0:T(8,128)(2,1)S(1)} %bitcast.16, bf16[4,512,128]{2,1,0:T(8,128)(2,1)S(1)} %bitcast.19), custom_call_target="tpu_custom_call" | custom-call | flops 2013265920 | bytes 2097152 | tf_op jit(solution)/shard_map/local_stats/pallas_call | solution.py:434
  43.1 0.0 copy-start.6
  43.1 0.0 collective-permute-done.4
  43.2 0.0 collective-permute-done.5
  43.2 0.0 collective-permute-done.6
  43.2 0.1 collective-permute-start.7
  43.3 0.5 collective-permute-start.8
  43.8 0.0 collective-permute-done.9.refs_4_
  43.8 0.1 collective-permute-start.10
  43.9 1.5 %collective-permute-done.8.refs_3_ = bf16[4,256,128]{2,1,0:T(8,128)(2,1)S(1)} collective-permute-done((bf16[4,256,128]{2,1,0:T(8,128)(2,1)S(1)}, bf16[4,256,128]{2,1,0:T(8,128)(2,1)S(1)}, u32[]{:S(2)}, u32[]{:S(2)}) %collective-permute-start.8) | collective-permute-done | bytes 262176 | tf_op jit(solution)/shard_map/ppermute | solution.py:405
  45.4 0.0 collective-permute-done.7.refs_1_
  45.4 0.4 collective-permute-done.10.refs_5_
  45.8 1.6 %remote_pairs.1 = (bf16[7,512,128]{2,1,0:T(8,128)(2,1)S(1)}, bf16[7,512,128]{2,1,0:T(8,128)(2,1)S(1)}, f32[4,8,512]{2,1,0:T(8,128)S(1)}, f32[4,128,512]{2,1,0:T(8,128)S(1)}) custom-call(s32[4,3]{1,0:T(4,128)S(1)} %copy-done.2, bf16[2048,128]{1,0:T(8,128)(2,1)S(1)} %bitcast.22, bf16[2048,128]{1,0:T(8,128)(2,1)S(1)} %bitcast.25, ...), custom_call_target="tpu_custom_call" | custom-call | flops 4026531840 | bytes 4194304 | tf_op jit(solution)/shard_map/remote_pairs/pallas_call | solution.py:450
  47.3 0.2 collective-permute-start.11
  47.5 2.3 %collective-permute-done.11.theirs = bf16[7,512,128]{2,1,0:T(8,128)(2,1)S(1)} collective-permute-done((bf16[7,512,128]{2,1,0:T(8,128)(2,1)S(1)}, bf16[7,512,128]{2,1,0:T(8,128)(2,1)S(1)}, u32[]{:S(2)}, u32[]{:S(2)}) %collective-permute-start.11) | collective-permute-done | bytes 917536 | tf_op jit(solution)/shard_map/ppermute | solution.py:405
  49.9 0.2 chip_sum.1
  50.1 1.3 %collective-permute-start.13 = (bf16[512,128]{1,0:T(8,128)(2,1)S(1)}, bf16[512,128]{1,0:T(8,128)(2,1)S(1)}, u32[]{:S(2)}, u32[]{:S(2)}) collective-permute-start(bf16[512,128]{1,0:T(8,128)(2,1)S(1)} %get-tuple-element.78), channel_id=1, source_target_pairs={{4,0},{8,4},{12,8},{16,12},{20,16},{24,20},{28,24},{5,1},{9,5},{13... | collective-permute-start | bytes 393224 | tf_op jit(solution)/shard_map/ppermute | solution.py:411
  51.4 1.3 %collective-permute-start.14 = (bf16[512,128]{1,0:T(8,128)(2,1)S(1)}, bf16[512,128]{1,0:T(8,128)(2,1)S(1)}, u32[]{:S(2)}, u32[]{:S(2)}) collective-permute-start(bf16[512,128]{1,0:T(8,128)(2,1)S(1)} %get-tuple-element.79), channel_id=1, source_target_pairs={{8,0},{12,4},{16,8},{20,12},{24,16},{28,20},{9,1},{13,5},{17,9},{2... | collective-permute-start | bytes 393224 | tf_op jit(solution)/shard_map/ppermute | solution.py:411
  52.7 1.3 %collective-permute-start.15 = (bf16[512,128]{1,0:T(8,128)(2,1)S(1)}, bf16[512,128]{1,0:T(8,128)(2,1)S(1)}, u32[]{:S(2)}, u32[]{:S(2)}) collective-permute-start(bf16[512,128]{1,0:T(8,128)(2,1)S(1)} %get-tuple-element.80), channel_id=1, source_target_pairs={{28,0},{29,1},{30,2},{31,3}} | collective-permute-start | bytes 393224 | tf_op jit(solution)/shard_map/ppermute | solution.py:411
  54.0 0.7 collective-permute-start.12
  54.6 9.4 %local_pairs.1 = (bf16[4,512,128]{2,1,0:T(8,128)(2,1)S(1)}, bf16[4,512,128]{2,1,0:T(8,128)(2,1)S(1)}, bf16[2048,128]{1,0:T(8,128)(2,1)}) custom-call(s32[4,3]{1,0:T(4,128)S(1)} %copy-done.2, bf16[2048,128]{1,0:T(8,128)(2,1)S(1)} %bitcast.23, bf16[2048,128]{1,0:T(8,128)(2,1)S(1)} %bitcast.26, bf16[4,512,128]{2,1,0:T(8,128)(2,1)S(1)} %bitcast.17, ...), custom_call_target="tpu_custom_call" | custom-call | flops 4026531840 | bytes 4194304 | tf_op jit(solution)/shard_map/local_pairs/pallas_call | solution.py:493
  64.1 0.0 collective-permute-done.13.refs_0_
  64.1 0.0 collective-permute-done.14.refs_1_
  64.1 6.0 %collective-permute-done.15.refs_2_ = bf16[512,128]{1,0:T(8,128)(2,1)S(1)} collective-permute-done((bf16[512,128]{1,0:T(8,128)(2,1)S(1)}, bf16[512,128]{1,0:T(8,128)(2,1)S(1)}, u32[]{:S(2)}, u32[]{:S(2)}) %collective-permute-start.15) | collective-permute-done | bytes 131104 | tf_op jit(solution)/shard_map/ppermute | solution.py:411
  70.1 0.0 collective-permute-done.12.refs_0_
  70.1 0.0 collective-permute-start.20
  70.1 1.3 %collective-permute-start.16 = (bf16[256,128]{1,0:T(8,128)(2,1)S(1)}, bf16[256,128]{1,0:T(8,128)(2,1)S(1)}, u32[]{:S(2)}, u32[]{:S(2)}) collective-permute-start(bf16[256,128]{1,0:T(8,128)(2,1)S(1)} %get-tuple-element.84), channel_id=1, source_target_pairs={{12,0},{16,4},{20,8},{24,12},{28,16},{13,1},{17,5},{21,9},{25,13},... | collective-permute-start | bytes 196616 | tf_op jit(solution)/shard_map/ppermute | solution.py:411
  71.4 1.3 %collective-permute-start.17 = (bf16[256,128]{1,0:T(8,128)(2,1)S(1)}, bf16[256,128]{1,0:T(8,128)(2,1)S(1)}, u32[]{:S(2)}, u32[]{:S(2)}) collective-permute-start(bf16[256,128]{1,0:T(8,128)(2,1)S(1)} %get-tuple-element.85), channel_id=1, source_target_pairs={{16,0},{20,4},{24,8},{28,12},{17,1},{21,5},{25,9},{29,13},{18,2},{... | collective-permute-start | bytes 196616 | tf_op jit(solution)/shard_map/ppermute | solution.py:411
  72.7 1.3 %collective-permute-start.18 = (bf16[256,128]{1,0:T(8,128)(2,1)S(1)}, bf16[256,128]{1,0:T(8,128)(2,1)S(1)}, u32[]{:S(2)}, u32[]{:S(2)}) collective-permute-start(bf16[256,128]{1,0:T(8,128)(2,1)S(1)} %get-tuple-element.86), channel_id=1, source_target_pairs={{20,0},{24,4},{28,8},{21,1},{25,5},{29,9},{22,2},{26,6},{30,10},{2... | collective-permute-start | bytes 196616 | tf_op jit(solution)/shard_map/ppermute | solution.py:411
  74.0 1.3 %collective-permute-start.19 = (bf16[256,128]{1,0:T(8,128)(2,1)S(1)}, bf16[256,128]{1,0:T(8,128)(2,1)S(1)}, u32[]{:S(2)}, u32[]{:S(2)}) collective-permute-start(bf16[256,128]{1,0:T(8,128)(2,1)S(1)} %get-tuple-element.87), channel_id=1, source_target_pairs={{24,0},{28,4},{25,1},{29,5},{26,2},{30,6},{27,3},{31,7}} | collective-permute-start | bytes 196616 | tf_op jit(solution)/shard_map/ppermute | solution.py:411
  75.3 0.0 collective-permute-done.20.theirs
  75.3 0.8 own_sum.1
  76.1 0.9 collective-permute-start.21
  77.0 1.3 %collective-permute-done.16.refs_0_ = bf16[256,128]{1,0:T(8,128)(2,1)S(1)} collective-permute-done((bf16[256,128]{1,0:T(8,128)(2,1)S(1)}, bf16[256,128]{1,0:T(8,128)(2,1)S(1)}, u32[]{:S(2)}, u32[]{:S(2)}) %collective-permute-start.16) | collective-permute-done | bytes 65568 | tf_op jit(solution)/shard_map/ppermute | solution.py:411
  78.3 2.3 %collective-permute-done.17.refs_1_ = bf16[256,128]{1,0:T(8,128)(2,1)S(1)} collective-permute-done((bf16[256,128]{1,0:T(8,128)(2,1)S(1)}, bf16[256,128]{1,0:T(8,128)(2,1)S(1)}, u32[]{:S(2)}, u32[]{:S(2)}) %collective-permute-start.17) | collective-permute-done | bytes 65568 | tf_op jit(solution)/shard_map/ppermute | solution.py:411
  80.6 4.6 %collective-permute-done.18.refs_2_ = bf16[256,128]{1,0:T(8,128)(2,1)S(1)} collective-permute-done((bf16[256,128]{1,0:T(8,128)(2,1)S(1)}, bf16[256,128]{1,0:T(8,128)(2,1)S(1)}, u32[]{:S(2)}, u32[]{:S(2)}) %collective-permute-start.18) | collective-permute-done | bytes 65568 | tf_op jit(solution)/shard_map/ppermute | solution.py:411
  85.1 0.0 collective-permute-done.19.refs_3_
  85.1 0.6 far_returns.1.returned
  85.8 0.1 owner_sum.1.refs_0_
  85.9 0.9 collective-permute-start.23
  86.8 7.1 %collective-permute-done.23.refs_2_ = bf16[4,256,128]{2,1,0:T(8,128)(2,1)S(1)} collective-permute-done((bf16[4,256,128]{2,1,0:T(8,128)(2,1)S(1)}, bf16[4,256,128]{2,1,0:T(8,128)(2,1)S(1)}, u32[]{:S(2)}, u32[]{:S(2)}) %collective-permute-start.23) | collective-permute-done | bytes 262176 | tf_op jit(solution)/shard_map/ppermute | solution.py:408
  93.9 0.0 collective-permute-start.24
  93.9 0.0 collective-permute-done.22.refs_1_
  93.9 1.5 %collective-permute-done.24.refs_3_ = bf16[4,256,128]{2,1,0:T(8,128)(2,1)S(1)} collective-permute-done((bf16[4,256,128]{2,1,0:T(8,128)(2,1)S(1)}, bf16[4,256,128]{2,1,0:T(8,128)(2,1)S(1)}, u32[]{:S(2)}, u32[]{:S(2)}) %collective-permute-start.24) | collective-permute-done | bytes 262176 | tf_op jit(solution)/shard_map/ppermute | solution.py:405
  95.4 1.0 %spread.1 = (bf16[4,512,128]{2,1,0:T(8,128)(2,1)}, bf16[4,512,128]{2,1,0:T(8,128)(2,1)}) custom-call(bf16[4,256,128]{2,1,0:T(8,128)(2,1)S(1)} %owner_sum.1.refs_0_, bf16[4,256,128]{2,1,0:T(8,128)(2,1)S(1)} %collective-permute-done.22.refs_1_, bf16[4,256,128]{2,1,0:T(8,128)(2,1)S(1)} %collective-permute-done.23.refs_2_, ...), custom_call_target="tpu_custom_call" | custom-call | tf_op jit(solution)/shard_map/spread/pallas_call | solution.py:543
  (15 shorter events, 0.2 us)
Async XLA Ops:
  15.0 21.3 %copy-start.1 = (bf16[2048,128]{1,0:T(8,128)(2,1)S(1)}, bf16[2048,128]{1,0:T(8,128)(2,1)}, u32[]{:S(2)}) copy-start(bf16[2048,128]{1,0:T(8,128)(2,1)} %param.7) | copy-start | bytes 1572868
  15.0 21.3 %copy-start.4 = (bf16[2048,1,128]{2,0,1:T(8,128)(2,1)S(1)}, bf16[2048,1,128]{2,0,1:T(8,128)(2,1)}, u32[]{:S(2)}) copy-start(bf16[2048,1,128]{2,0,1:T(8,128)(2,1)} %param.5) | copy-start | bytes 1572868
  18.1 18.3 %copy-start = (bf16[2048,128]{1,0:T(8,128)(2,1)S(1)}, bf16[2048,128]{1,0:T(8,128)(2,1)}, u32[]{:S(2)}) copy-start(bf16[2048,128]{1,0:T(8,128)(2,1)} %param.6) | copy-start | bytes 1572868
  18.1 10.0 %collective-permute-start = (bf16[256,128]{1,0:T(8,128)(2,1)}, bf16[256,128]{1,0:T(8,128)(2,1)S(1)}, u32[]{:S(2)}, u32[]{:S(2)}) collective-permute-start(bf16[256,128]{1,0:T(8,128)(2,1)} %get-tuple-element.50), channel_id=1, source_target_pairs={{0,12},{4,16},{8,20},{12,24},{16,28},{1,13},{5,17},{9,21},{13,25},... | collective-permute-start | bytes 196616 | tf_op jit(solution)/shard_map/ppermute | solution.py:414
  20.7 8.7 %collective-permute-start.1 = (bf16[256,128]{1,0:T(8,128)(2,1)}, bf16[256,128]{1,0:T(8,128)(2,1)S(1)}, u32[]{:S(2)}, u32[]{:S(2)}) collective-permute-start(bf16[256,128]{1,0:T(8,128)(2,1)} %get-tuple-element.51), channel_id=1, source_target_pairs={{0,16},{4,20},{8,24},{12,28},{1,17},{5,21},{9,25},{13,29},{2,18},{... | collective-permute-start | bytes 196616 | tf_op jit(solution)/shard_map/ppermute | solution.py:414
  23.2 11.5 %collective-permute-start.2 = (bf16[256,128]{1,0:T(8,128)(2,1)}, bf16[256,128]{1,0:T(8,128)(2,1)S(1)}, u32[]{:S(2)}, u32[]{:S(2)}) collective-permute-start(bf16[256,128]{1,0:T(8,128)(2,1)} %get-tuple-element.52), channel_id=1, source_target_pairs={{0,20},{4,24},{8,28},{1,21},{5,25},{9,29},{2,22},{6,26},{10,30},{3... | collective-permute-start | bytes 196616 | tf_op jit(solution)/shard_map/ppermute | solution.py:414
  24.5 10.2 %collective-permute-start.3 = (bf16[256,128]{1,0:T(8,128)(2,1)}, bf16[256,128]{1,0:T(8,128)(2,1)S(1)}, u32[]{:S(2)}, u32[]{:S(2)}) collective-permute-start(bf16[256,128]{1,0:T(8,128)(2,1)} %get-tuple-element.53), channel_id=1, source_target_pairs={{0,24},{4,28},{1,25},{5,29},{2,26},{6,30},{3,27},{7,31}} | collective-permute-start | bytes 196616 | tf_op jit(solution)/shard_map/ppermute | solution.py:414
  25.8 17.3 %collective-permute-start.4 = (bf16[512,128]{1,0:T(8,128)(2,1)}, bf16[512,128]{1,0:T(8,128)(2,1)S(1)}, u32[]{:S(2)}, u32[]{:S(2)}) collective-permute-start(bf16[512,128]{1,0:T(8,128)(2,1)} %get-tuple-element.55), channel_id=1, source_target_pairs={{0,4},{4,8},{8,12},{12,16},{16,20},{20,24},{24,28},{1,5},{5,9},{9,... | collective-permute-start | bytes 393224 | tf_op jit(solution)/shard_map/ppermute | solution.py:414
  28.0 15.1 %collective-permute-start.5 = (bf16[512,128]{1,0:T(8,128)(2,1)}, bf16[512,128]{1,0:T(8,128)(2,1)S(1)}, u32[]{:S(2)}, u32[]{:S(2)}) collective-permute-start(bf16[512,128]{1,0:T(8,128)(2,1)} %get-tuple-element.56), channel_id=1, source_target_pairs={{0,8},{4,12},{8,16},{12,20},{16,24},{20,28},{1,9},{5,13},{9,17},{1... | collective-permute-start | bytes 393224 | tf_op jit(solution)/shard_map/ppermute | solution.py:414
  29.3 13.8 %collective-permute-start.6 = (bf16[512,128]{1,0:T(8,128)(2,1)}, bf16[512,128]{1,0:T(8,128)(2,1)S(1)}, u32[]{:S(2)}, u32[]{:S(2)}) collective-permute-start(bf16[512,128]{1,0:T(8,128)(2,1)} %get-tuple-element.57), channel_id=1, source_target_pairs={{0,28},{1,29},{2,30},{3,31}} | collective-permute-start | bytes 393224 | tf_op jit(solution)/shard_map/ppermute | solution.py:414
  34.8 1.6 %copy-start.2 = (s32[4,3]{1,0:T(4,128)S(1)}, s32[4,3]{1,0:T(4,128)}, u32[]{:S(2)}) copy-start(s32[4,3]{1,0:T(4,128)} %chosen.2) | copy-start | bytes 148
  34.8 9.0 %collective-permute-start.9 = (bf16[4,256,128]{2,1,0:T(8,128)(2,1)S(1)}, bf16[4,256,128]{2,1,0:T(8,128)(2,1)S(1)}, u32[]{:S(2)}, u32[]{:S(2)}) collective-permute-start(bf16[4,256,128]{2,1,0:T(8,128)(2,1)S(1)} %pad_maximum_fusion.1.refs_2_), channel_id=1, source_target_pairs={{0,2},{1,3},{2,0},{3,1},{4,6},{5,7},{6,4},{7,5},{8,10},{9,11},{10,... | collective-permute-start | bytes 786440 | tf_op jit(solution)/shard_map/ppermute | solution.py:408
  36.4 1.0 %copy-start.5 = (bf16[2048,1,128]{2,0,1:T(8,128)(2,1)S(1)}, bf16[2048,1,128]{2,0,1:T(8,128)(2,1)}, u32[]{:S(2)}) copy-start(bf16[2048,1,128]{2,0,1:T(8,128)(2,1)} %param.8) | copy-start | bytes 1572868
  43.1 2.6 %copy-start.6 = (bf16[2048,1,128]{2,0,1:T(8,128)(2,1)S(1)}, bf16[2048,1,128]{2,0,1:T(8,128)(2,1)}, u32[]{:S(2)}) copy-start(bf16[2048,1,128]{2,0,1:T(8,128)(2,1)} %param.8) | copy-start | bytes 1572868
  43.2 2.2 %collective-permute-start.7 = (bf16[3,512,128]{2,1,0:T(8,128)(2,1)S(1)}, bf16[3,512,128]{2,1,0:T(8,128)(2,1)S(1)}, u32[]{:S(2)}, u32[]{:S(2)}) collective-permute-start(bf16[3,512,128]{2,1,0:T(8,128)(2,1)S(1)} %pad_maximum_fusion.refs_0_), channel_id=1, source_target_pairs={{0,1},{1,0},{2,3},{3,2},{4,5},{5,4},{6,7},{7,6},{8,9},{9,8},{10,11... | collective-permute-start | bytes 1179656 | tf_op jit(solution)/shard_map/ppermute | solution.py:405
  43.3 2.1 %collective-permute-start.8 = (bf16[4,256,128]{2,1,0:T(8,128)(2,1)S(1)}, bf16[4,256,128]{2,1,0:T(8,128)(2,1)S(1)}, u32[]{:S(2)}, u32[]{:S(2)}) collective-permute-start(bf16[4,256,128]{2,1,0:T(8,128)(2,1)S(1)} %pad_maximum_fusion.1.refs_2_), channel_id=1, source_target_pairs={{0,1},{1,0},{2,3},{3,2},{4,5},{5,4},{6,7},{7,6},{8,9},{9,8},{10,11... | collective-permute-start | bytes 786440 | tf_op jit(solution)/shard_map/ppermute | solution.py:405
  43.8 2.0 %collective-permute-start.10 = (bf16[4,256,128]{2,1,0:T(8,128)(2,1)S(1)}, bf16[4,256,128]{2,1,0:T(8,128)(2,1)S(1)}, u32[]{:S(2)}, u32[]{:S(2)}) collective-permute-start(bf16[4,256,128]{2,1,0:T(8,128)(2,1)S(1)} %collective-permute-done.9.refs_4_), channel_id=1, source_target_pairs={{0,1},{1,0},{2,3},{3,2},{4,5},{5,4},{6,7},{7,6},{8,9},{9,8},{10,11... | collective-permute-start | bytes 786440 | tf_op jit(solution)/shard_map/ppermute | solution.py:405
  47.3 2.5 %collective-permute-start.11 = (bf16[7,512,128]{2,1,0:T(8,128)(2,1)S(1)}, bf16[7,512,128]{2,1,0:T(8,128)(2,1)S(1)}, u32[]{:S(2)}, u32[]{:S(2)}) collective-permute-start(bf16[7,512,128]{2,1,0:T(8,128)(2,1)S(1)} %get-tuple-element.65), channel_id=1, source_target_pairs={{0,1},{1,0},{2,3},{3,2},{4,5},{5,4},{6,7},{7,6},{8,9},{9,8},{10,11... | collective-permute-start | bytes 2752520 | tf_op jit(solution)/shard_map/ppermute | solution.py:405
  50.1 14.0 %collective-permute-start.13 = (bf16[512,128]{1,0:T(8,128)(2,1)S(1)}, bf16[512,128]{1,0:T(8,128)(2,1)S(1)}, u32[]{:S(2)}, u32[]{:S(2)}) collective-permute-start(bf16[512,128]{1,0:T(8,128)(2,1)S(1)} %get-tuple-element.78), channel_id=1, source_target_pairs={{4,0},{8,4},{12,8},{16,12},{20,16},{24,20},{28,24},{5,1},{9,5},{13... | collective-permute-start | bytes 393224 | tf_op jit(solution)/shard_map/ppermute | solution.py:411
  51.4 12.7 %collective-permute-start.14 = (bf16[512,128]{1,0:T(8,128)(2,1)S(1)}, bf16[512,128]{1,0:T(8,128)(2,1)S(1)}, u32[]{:S(2)}, u32[]{:S(2)}) collective-permute-start(bf16[512,128]{1,0:T(8,128)(2,1)S(1)} %get-tuple-element.79), channel_id=1, source_target_pairs={{8,0},{12,4},{16,8},{20,12},{24,16},{28,20},{9,1},{13,5},{17,9},{2... | collective-permute-start | bytes 393224 | tf_op jit(solution)/shard_map/ppermute | solution.py:411
  52.7 17.4 %collective-permute-start.15 = (bf16[512,128]{1,0:T(8,128)(2,1)S(1)}, bf16[512,128]{1,0:T(8,128)(2,1)S(1)}, u32[]{:S(2)}, u32[]{:S(2)}) collective-permute-start(bf16[512,128]{1,0:T(8,128)(2,1)S(1)} %get-tuple-element.80), channel_id=1, source_target_pairs={{28,0},{29,1},{30,2},{31,3}} | collective-permute-start | bytes 393224 | tf_op jit(solution)/shard_map/ppermute | solution.py:411
  54.0 16.1 %collective-permute-start.12 = (bf16[4,256,128]{2,1,0:T(8,128)(2,1)S(1)}, bf16[4,256,128]{2,1,0:T(8,128)(2,1)S(1)}, u32[]{:S(2)}, u32[]{:S(2)}) collective-permute-start(bf16[4,256,128]{2,1,0:T(8,128)(2,1)S(1)} %get-tuple-element.77), channel_id=1, source_target_pairs={{0,2},{1,3},{2,0},{3,1},{4,6},{5,7},{6,4},{7,5},{8,10},{9,11},{10,... | collective-permute-start | bytes 786440 | tf_op jit(solution)/shard_map/ppermute | solution.py:408
  70.1 5.3 %collective-permute-start.20 = (bf16[4,512,128]{2,1,0:T(8,128)(2,1)S(1)}, bf16[4,512,128]{2,1,0:T(8,128)(2,1)S(1)}, u32[]{:S(2)}, u32[]{:S(2)}) collective-permute-start(bf16[4,512,128]{2,1,0:T(8,128)(2,1)S(1)} %get-tuple-element.89), channel_id=1, source_target_pairs={{0,1},{1,0},{2,3},{3,2},{4,5},{5,4},{6,7},{7,6},{8,9},{9,8},{10,11... | collective-permute-start | bytes 1572872 | tf_op jit(solution)/shard_map/ppermute | solution.py:405
  70.1 8.2 %collective-permute-start.16 = (bf16[256,128]{1,0:T(8,128)(2,1)S(1)}, bf16[256,128]{1,0:T(8,128)(2,1)S(1)}, u32[]{:S(2)}, u32[]{:S(2)}) collective-permute-start(bf16[256,128]{1,0:T(8,128)(2,1)S(1)} %get-tuple-element.84), channel_id=1, source_target_pairs={{12,0},{16,4},{20,8},{24,12},{28,16},{13,1},{17,5},{21,9},{25,13},... | collective-permute-start | bytes 196616 | tf_op jit(solution)/shard_map/ppermute | solution.py:411
  71.4 9.1 %collective-permute-start.17 = (bf16[256,128]{1,0:T(8,128)(2,1)S(1)}, bf16[256,128]{1,0:T(8,128)(2,1)S(1)}, u32[]{:S(2)}, u32[]{:S(2)}) collective-permute-start(bf16[256,128]{1,0:T(8,128)(2,1)S(1)} %get-tuple-element.85), channel_id=1, source_target_pairs={{16,0},{20,4},{24,8},{28,12},{17,1},{21,5},{25,9},{29,13},{18,2},{... | collective-permute-start | bytes 196616 | tf_op jit(solution)/shard_map/ppermute | solution.py:411
  72.7 12.4 %collective-permute-start.18 = (bf16[256,128]{1,0:T(8,128)(2,1)S(1)}, bf16[256,128]{1,0:T(8,128)(2,1)S(1)}, u32[]{:S(2)}, u32[]{:S(2)}) collective-permute-start(bf16[256,128]{1,0:T(8,128)(2,1)S(1)} %get-tuple-element.86), channel_id=1, source_target_pairs={{20,0},{24,4},{28,8},{21,1},{25,5},{29,9},{22,2},{26,6},{30,10},{2... | collective-permute-start | bytes 196616 | tf_op jit(solution)/shard_map/ppermute | solution.py:411
  74.0 1.3 %copy-start.3 = (s32[7]{0:T(128)S(1)}, s32[7]{0:T(128)}, u32[]{:S(2)}) copy-start(s32[7]{0:T(128)} %get-tuple-element.75.asked) | copy-start | bytes 88
  74.0 11.1 %collective-permute-start.19 = (bf16[256,128]{1,0:T(8,128)(2,1)S(1)}, bf16[256,128]{1,0:T(8,128)(2,1)S(1)}, u32[]{:S(2)}, u32[]{:S(2)}) collective-permute-start(bf16[256,128]{1,0:T(8,128)(2,1)S(1)} %get-tuple-element.87), channel_id=1, source_target_pairs={{24,0},{28,4},{25,1},{29,5},{26,2},{30,6},{27,3},{31,7}} | collective-permute-start | bytes 196616 | tf_op jit(solution)/shard_map/ppermute | solution.py:411
  76.1 9.6 %collective-permute-start.21 = (bf16[4,256,128]{2,1,0:T(8,128)(2,1)S(1)}, bf16[4,256,128]{2,1,0:T(8,128)(2,1)S(1)}, u32[]{:S(2)}, u32[]{:S(2)}) collective-permute-start(bf16[4,256,128]{2,1,0:T(8,128)(2,1)S(1)} %get-tuple-element.94), channel_id=1, source_target_pairs={{0,2},{1,3},{2,0},{3,1},{4,6},{5,7},{6,4},{7,5},{8,10},{9,11},{10,... | collective-permute-start | bytes 786440 | tf_op jit(solution)/shard_map/ppermute | solution.py:408
  85.9 8.0 %collective-permute-start.23 = (bf16[4,256,128]{2,1,0:T(8,128)(2,1)S(1)}, bf16[4,256,128]{2,1,0:T(8,128)(2,1)S(1)}, u32[]{:S(2)}, u32[]{:S(2)}) collective-permute-start(bf16[4,256,128]{2,1,0:T(8,128)(2,1)S(1)} %owner_sum.1.refs_0_), channel_id=1, source_target_pairs={{0,2},{1,3},{2,0},{3,1},{4,6},{5,7},{6,4},{7,5},{8,10},{9,11},{10,... | collective-permute-start | bytes 786440 | tf_op jit(solution)/shard_map/ppermute | solution.py:408
  86.8 7.1 %collective-permute-start.22 = (bf16[4,256,128]{2,1,0:T(8,128)(2,1)S(1)}, bf16[4,256,128]{2,1,0:T(8,128)(2,1)S(1)}, u32[]{:S(2)}, u32[]{:S(2)}) collective-permute-start(bf16[4,256,128]{2,1,0:T(8,128)(2,1)S(1)} %owner_sum.1.refs_0_), channel_id=1, source_target_pairs={{0,1},{1,0},{2,3},{3,2},{4,5},{5,4},{6,7},{7,6},{8,9},{9,8},{10,11... | collective-permute-start | bytes 786440 | tf_op jit(solution)/shard_map/ppermute | solution.py:405
  93.9 1.5 %collective-permute-start.24 = (bf16[4,256,128]{2,1,0:T(8,128)(2,1)S(1)}, bf16[4,256,128]{2,1,0:T(8,128)(2,1)S(1)}, u32[]{:S(2)}, u32[]{:S(2)}) collective-permute-start(bf16[4,256,128]{2,1,0:T(8,128)(2,1)S(1)} %collective-permute-done.23.refs_2_), channel_id=1, source_target_pairs={{0,1},{1,0},{2,3},{3,2},{4,5},{5,4},{6,7},{7,6},{8,9},{9,8},{10,11... | collective-permute-start | bytes 786440 | tf_op jit(solution)/shard_map/ppermute | solution.py:405

commit v4 on v3

--- a/solution.py
+++ b/solution.py
@@ -370,7 +370,7 @@
     scaling = 1.0 / math.sqrt(feature)
     factor = scaling * math.log2(math.e)
     shifts = ctx_count - 1
-    far = [s for s in range(shifts - 1) if 2 * (s + 2) >= ctx_count]
+    far = [s for s in reversed(range(shifts - 1)) if 2 * (s + 2) >= ctx_count]
     near = [s for s in range(shifts) if s not in far]
 
     q2 = queries.reshape(tok_rows, feature)

time: 96.1 us -> 95.7 us (level)
  waiting for transfers between devices: 26.9 us -> 25.6 us
    ppermute x4, starting transfers between devices: 4 us -> 5.32 us  [to_chip(): lax.ppermute(array, 'head', [(h, (h + 2 * d) % heads) for h in range(head...]
    ppermute x7, starting transfers between devices: 16.6 us -> 15.3 us  [to_reader(): lax.ppermute(array, 'ctx', [(c - s - 1, c) for c in range(s + 1, ctx_coun...]
  transfers between devices with their start and end apart: 25 -> 25, of which waited for: 9 -> 11; matrix products, arithmetic and copies ran while one was open for 0% -> 0% of each run, Pallas kernels for 17% -> 18%
where the time goes in v4:
time: 95.7 us; the launch traced here: 95.1 us
  starting transfers between devices  30.5 us (32%)
  waiting for transfers between devices  25.6 us (27%)
  Pallas kernels  22.5 us (24%)
  blocking collectives  13.6 us (14%)
  local copies, waits for them, and re-layouts  1.84 us (2%)
    ppermute x7, starting transfers between devices, to_reader(): lax.ppermute(array, 'ctx', [(c - s - 1, c) for c in range(s + 1, ctx_coun...  15.3 us
    all_to_all x1, blocking collectives, body(): lax.all_to_all(jnp.broadcast_to(selected.reshape(1, 3 * blocks_here), (ct...  13.6 us
    ppermute x7, waiting for transfers between devices, to_owner(): lax.ppermute(array, 'ctx', [(c, c - s - 1) for c in range(s + 1, ctx_coun...  13.1 us
    pallas_call x1, Pallas kernels, body(): pl.pallas_call(functools.partial(local_kernel, factor, scaling, blocks_he...  9.44 us
    ppermute x7, starting transfers between devices, to_owner(): lax.ppermute(array, 'ctx', [(c, c - s - 1) for c in range(s + 1, ctx_coun...  9.04 us
    ppermute x4, waiting for transfers between devices, to_chip(): lax.ppermute(array, 'head', [(h, (h + 2 * d) % heads) for h in range(head...  6.71 us
    ppermute x7, waiting for transfers between devices, swap(): return lax.ppermute(array, 'head', [(h, h ^ 1) for h in range(heads)])  5.75 us
    pallas_call x1, Pallas kernels, body(): pl.pallas_call(functools.partial(local_stats_kernel, factor, blocks_here)...  5.74 us
  transfers between devices with their start and end apart: 25, of which 11 were waited for; matrix products, arithmetic and copies ran while one was open for 0% of the time, Pallas kernels for 18%

profile of v4, /device:TPU:0, one launch (start us, length us, event | category | flops | bytes accessed | tf_op | source)
XLA Modules:
  0.0 95.1 jit_solution(13925060360150987833)
XLA Ops:
  0.6 0.8 broadcast_in_dim.7
  1.4 13.6 %all_to_all.8 = s32[8,1,12]{2,1,0:T(1,128)} all-to-all(s32[8,1,12]{2,1,0:T(1,128)S(1)} %broadcast_in_dim.8), channel_id=1, replica_groups=mesh['ctx'=8,'head'=4] {'ctx'}, dimensions={0} | all-to-all | bytes 768 | tf_op jit(solution)/shard_map/all_to_all | solution.py:416
  15.0 3.0 %pick_rows.1 = (s32[7]{0:T(128)}, bf16[512,128]{1,0:T(8,128)(2,1)}, bf16[512,128]{1,0:T(8,128)(2,1)}, bf16[256,128]{1,0:T(8,128)(2,1)}, bf16[256,128]{1,0:T(8,12...) custom-call(s32[8,12]{1,0:T(8,128)} %bitcast.34, ...), custom_call_target="tpu_custom_call" | custom-call | tf_op jit(solution)/shard_map/pick_rows/pallas_call | solution.py:420
  18.1 0.0 copy-start
  18.1 2.7 %collective-permute-start = (bf16[256,128]{1,0:T(8,128)(2,1)}, bf16[256,128]{1,0:T(8,128)(2,1)S(1)}, u32[]{:S(2)}, u32[]{:S(2)}) collective-permute-start(bf16[256,128]{1,0:T(8,128)(2,1)} %get-tuple-element.50), channel_id=1, source_target_pairs={{0,24},{4,28},{1,25},{5,29},{2,26},{6,30},{3,27},{7,31}} | collective-permute-start | bytes 196616 | tf_op jit(solution)/shard_map/ppermute | solution.py:414
  20.7 1.3 %collective-permute-start.1 = (bf16[256,128]{1,0:T(8,128)(2,1)}, bf16[256,128]{1,0:T(8,128)(2,1)S(1)}, u32[]{:S(2)}, u32[]{:S(2)}) collective-permute-start(bf16[256,128]{1,0:T(8,128)(2,1)} %get-tuple-element.51), channel_id=1, source_target_pairs={{0,20},{4,24},{8,28},{1,21},{5,25},{9,29},{2,22},{6,26},{10,30},{3... | collective-permute-start | bytes 196616 | tf_op jit(solution)/shard_map/ppermute | solution.py:414
  22.0 1.3 %collective-permute-start.2 = (bf16[256,128]{1,0:T(8,128)(2,1)}, bf16[256,128]{1,0:T(8,128)(2,1)S(1)}, u32[]{:S(2)}, u32[]{:S(2)}) collective-permute-start(bf16[256,128]{1,0:T(8,128)(2,1)} %get-tuple-element.52), channel_id=1, source_target_pairs={{0,16},{4,20},{8,24},{12,28},{1,17},{5,21},{9,25},{13,29},{2,18},{... | collective-permute-start | bytes 196616 | tf_op jit(solution)/shard_map/ppermute | solution.py:414
  23.3 2.5 %collective-permute-start.3 = (bf16[256,128]{1,0:T(8,128)(2,1)}, bf16[256,128]{1,0:T(8,128)(2,1)S(1)}, u32[]{:S(2)}, u32[]{:S(2)}) collective-permute-start(bf16[256,128]{1,0:T(8,128)(2,1)} %get-tuple-element.53), channel_id=1, source_target_pairs={{0,12},{4,16},{8,20},{12,24},{16,28},{1,13},{5,17},{9,21},{13,25},... | collective-permute-start | bytes 196616 | tf_op jit(solution)/shard_map/ppermute | solution.py:414
  25.8 2.2 %collective-permute-start.4 = (bf16[512,128]{1,0:T(8,128)(2,1)}, bf16[512,128]{1,0:T(8,128)(2,1)S(1)}, u32[]{:S(2)}, u32[]{:S(2)}) collective-permute-start(bf16[512,128]{1,0:T(8,128)(2,1)} %get-tuple-element.55), channel_id=1, source_target_pairs={{0,4},{4,8},{8,12},{12,16},{16,20},{20,24},{24,28},{1,5},{5,9},{9,... | collective-permute-start | bytes 393224 | tf_op jit(solution)/shard_map/ppermute | solution.py:414
  28.0 0.0 collective-permute-done
  28.0 2.5 %collective-permute-start.5 = (bf16[512,128]{1,0:T(8,128)(2,1)}, bf16[512,128]{1,0:T(8,128)(2,1)S(1)}, u32[]{:S(2)}, u32[]{:S(2)}) collective-permute-start(bf16[512,128]{1,0:T(8,128)(2,1)} %get-tuple-element.56), channel_id=1, source_target_pairs={{0,8},{4,12},{8,16},{12,20},{16,24},{20,28},{1,9},{5,13},{9,17},{1... | collective-permute-start | bytes 393224 | tf_op jit(solution)/shard_map/ppermute | solution.py:414
  30.5 0.0 collective-permute-done.1
  30.5 2.9 %collective-permute-start.6 = (bf16[512,128]{1,0:T(8,128)(2,1)}, bf16[512,128]{1,0:T(8,128)(2,1)S(1)}, u32[]{:S(2)}, u32[]{:S(2)}) collective-permute-start(bf16[512,128]{1,0:T(8,128)(2,1)} %get-tuple-element.57), channel_id=1, source_target_pairs={{0,28},{1,29},{2,30},{3,31}} | collective-permute-start | bytes 393224 | tf_op jit(solution)/shard_map/ppermute | solution.py:414
  33.4 0.0 collective-permute-done.2
  33.5 0.0 collective-permute-done.3
  33.5 0.0 copy-start.2
  33.5 1.6 %collective-permute-start.9 = (bf16[4,256,128]{2,1,0:T(8,128)(2,1)S(1)}, bf16[4,256,128]{2,1,0:T(8,128)(2,1)S(1)}, u32[]{:S(2)}, u32[]{:S(2)}) collective-permute-start(bf16[4,256,128]{2,1,0:T(8,128)(2,1)S(1)} %pad_maximum_fusion.1.refs_2_), channel_id=1, source_target_pairs={{0,2},{1,3},{2,0},{3,1},{4,6},{5,7},{6,4},{7,5},{8,10},{9,11},{10,... | collective-permute-start | bytes 786440 | tf_op jit(solution)/shard_map/ppermute | solution.py:408
  35.1 0.0 copy-start.5
  35.1 1.0 %copy-done.5 = bf16[2048,1,128]{2,0,1:T(8,128)(2,1)S(1)} copy-done((bf16[2048,1,128]{2,0,1:T(8,128)(2,1)S(1)}, bf16[2048,1,128]{2,0,1:T(8,128)(2,1)}, u32[]{:S(2)}) %copy-start.5) | copy-done | bytes 524312
  36.1 5.7 %local_stats.1.stats = f32[4,8,512]{2,1,0:T(8,128)S(1)} custom-call(s32[4,3]{1,0:T(4,128)S(1)} %copy-done.2, bf16[2048,128]{1,0:T(8,128)(2,1)S(1)} %bitcast.21, bf16[2048,128]{1,0:T(8,128)(2,1)S(1)} %bitcast.24, bf16[4,512,128]{2,1,0:T(8,128)(2,1)S(1)} %bitcast.16, bf16[4,512,128]{2,1,0:T(8,128)(2,1)S(1)} %bitcast.19), custom_call_target="tpu_custom_call" | custom-call | flops 2013265920 | bytes 2097152 | tf_op jit(solution)/shard_map/local_stats/pallas_call | solution.py:434
  41.9 0.0 copy-start.6
  41.9 0.0 collective-permute-done.4
  41.9 0.0 collective-permute-done.5
  41.9 0.0 collective-permute-done.6
  42.0 0.1 collective-permute-start.7
  42.1 0.5 collective-permute-start.8
  42.6 0.0 collective-permute-done.9.refs_4_
  42.6 0.1 collective-permute-start.10
  42.6 1.5 %collective-permute-done.8.refs_3_ = bf16[4,256,128]{2,1,0:T(8,128)(2,1)S(1)} collective-permute-done((bf16[4,256,128]{2,1,0:T(8,128)(2,1)S(1)}, bf16[4,256,128]{2,1,0:T(8,128)(2,1)S(1)}, u32[]{:S(2)}, u32[]{:S(2)}) %collective-permute-start.8) | collective-permute-done | bytes 262176 | tf_op jit(solution)/shard_map/ppermute | solution.py:405
  44.1 0.0 collective-permute-done.7.refs_1_
  44.1 0.4 collective-permute-done.10.refs_5_
  44.5 1.6 %remote_pairs.1 = (bf16[7,512,128]{2,1,0:T(8,128)(2,1)S(1)}, bf16[7,512,128]{2,1,0:T(8,128)(2,1)S(1)}, f32[4,8,512]{2,1,0:T(8,128)S(1)}, f32[4,128,512]{2,1,0:T(8,128)S(1)}) custom-call(s32[4,3]{1,0:T(4,128)S(1)} %copy-done.2, bf16[2048,128]{1,0:T(8,128)(2,1)S(1)} %bitcast.22, bf16[2048,128]{1,0:T(8,128)(2,1)S(1)} %bitcast.25, ...), custom_call_target="tpu_custom_call" | custom-call | flops 4026531840 | bytes 4194304 | tf_op jit(solution)/shard_map/remote_pairs/pallas_call | solution.py:450
  46.1 0.2 collective-permute-start.11
  46.3 2.3 %collective-permute-done.11.theirs = bf16[7,512,128]{2,1,0:T(8,128)(2,1)S(1)} collective-permute-done((bf16[7,512,128]{2,1,0:T(8,128)(2,1)S(1)}, bf16[7,512,128]{2,1,0:T(8,128)(2,1)S(1)}, u32[]{:S(2)}, u32[]{:S(2)}) %collective-permute-start.11) | collective-permute-done | bytes 917536 | tf_op jit(solution)/shard_map/ppermute | solution.py:405
  48.6 0.2 chip_sum.1
  48.8 1.3 %collective-permute-start.13 = (bf16[512,128]{1,0:T(8,128)(2,1)S(1)}, bf16[512,128]{1,0:T(8,128)(2,1)S(1)}, u32[]{:S(2)}, u32[]{:S(2)}) collective-permute-start(bf16[512,128]{1,0:T(8,128)(2,1)S(1)} %get-tuple-element.78), channel_id=1, source_target_pairs={{4,0},{8,4},{12,8},{16,12},{20,16},{24,20},{28,24},{5,1},{9,5},{13... | collective-permute-start | bytes 393224 | tf_op jit(solution)/shard_map/ppermute | solution.py:411
  50.1 1.3 %collective-permute-start.14 = (bf16[512,128]{1,0:T(8,128)(2,1)S(1)}, bf16[512,128]{1,0:T(8,128)(2,1)S(1)}, u32[]{:S(2)}, u32[]{:S(2)}) collective-permute-start(bf16[512,128]{1,0:T(8,128)(2,1)S(1)} %get-tuple-element.79), channel_id=1, source_target_pairs={{8,0},{12,4},{16,8},{20,12},{24,16},{28,20},{9,1},{13,5},{17,9},{2... | collective-permute-start | bytes 393224 | tf_op jit(solution)/shard_map/ppermute | solution.py:411
  51.4 1.3 %collective-permute-start.15 = (bf16[512,128]{1,0:T(8,128)(2,1)S(1)}, bf16[512,128]{1,0:T(8,128)(2,1)S(1)}, u32[]{:S(2)}, u32[]{:S(2)}) collective-permute-start(bf16[512,128]{1,0:T(8,128)(2,1)S(1)} %get-tuple-element.80), channel_id=1, source_target_pairs={{28,0},{29,1},{30,2},{31,3}} | collective-permute-start | bytes 393224 | tf_op jit(solution)/shard_map/ppermute | solution.py:411
  52.7 0.7 collective-permute-start.12
  53.4 9.4 %local_pairs.1 = (bf16[4,512,128]{2,1,0:T(8,128)(2,1)S(1)}, bf16[4,512,128]{2,1,0:T(8,128)(2,1)S(1)}, bf16[2048,128]{1,0:T(8,128)(2,1)}) custom-call(s32[4,3]{1,0:T(4,128)S(1)} %copy-done.2, bf16[2048,128]{1,0:T(8,128)(2,1)S(1)} %bitcast.23, bf16[2048,128]{1,0:T(8,128)(2,1)S(1)} %bitcast.26, bf16[4,512,128]{2,1,0:T(8,128)(2,1)S(1)} %bitcast.17, ...), custom_call_target="tpu_custom_call" | custom-call | flops 4026531840 | bytes 4194304 | tf_op jit(solution)/shard_map/local_pairs/pallas_call | solution.py:493
  62.8 6.8 %collective-permute-done.15.refs_2_ = bf16[512,128]{1,0:T(8,128)(2,1)S(1)} collective-permute-done((bf16[512,128]{1,0:T(8,128)(2,1)S(1)}, bf16[512,128]{1,0:T(8,128)(2,1)S(1)}, u32[]{:S(2)}, u32[]{:S(2)}) %collective-permute-start.15) | collective-permute-done | bytes 131104 | tf_op jit(solution)/shard_map/ppermute | solution.py:411
  69.6 0.0 collective-permute-done.12.refs_0_
  69.6 0.0 collective-permute-start.20
  69.7 1.3 %collective-permute-start.16 = (bf16[256,128]{1,0:T(8,128)(2,1)S(1)}, bf16[256,128]{1,0:T(8,128)(2,1)S(1)}, u32[]{:S(2)}, u32[]{:S(2)}) collective-permute-start(bf16[256,128]{1,0:T(8,128)(2,1)S(1)} %get-tuple-element.84), channel_id=1, source_target_pairs={{24,0},{28,4},{25,1},{29,5},{26,2},{30,6},{27,3},{31,7}} | collective-permute-start | bytes 196616 | tf_op jit(solution)/shard_map/ppermute | solution.py:411
  71.0 1.3 %collective-permute-start.17 = (bf16[256,128]{1,0:T(8,128)(2,1)S(1)}, bf16[256,128]{1,0:T(8,128)(2,1)S(1)}, u32[]{:S(2)}, u32[]{:S(2)}) collective-permute-start(bf16[256,128]{1,0:T(8,128)(2,1)S(1)} %get-tuple-element.85), channel_id=1, source_target_pairs={{20,0},{24,4},{28,8},{21,1},{25,5},{29,9},{22,2},{26,6},{30,10},{2... | collective-permute-start | bytes 196616 | tf_op jit(solution)/shard_map/ppermute | solution.py:411
  72.3 1.3 %collective-permute-start.18 = (bf16[256,128]{1,0:T(8,128)(2,1)S(1)}, bf16[256,128]{1,0:T(8,128)(2,1)S(1)}, u32[]{:S(2)}, u32[]{:S(2)}) collective-permute-start(bf16[256,128]{1,0:T(8,128)(2,1)S(1)} %get-tuple-element.86), channel_id=1, source_target_pairs={{16,0},{20,4},{24,8},{28,12},{17,1},{21,5},{25,9},{29,13},{18,2},{... | collective-permute-start | bytes 196616 | tf_op jit(solution)/shard_map/ppermute | solution.py:411
  73.6 1.3 %collective-permute-start.19 = (bf16[256,128]{1,0:T(8,128)(2,1)S(1)}, bf16[256,128]{1,0:T(8,128)(2,1)S(1)}, u32[]{:S(2)}, u32[]{:S(2)}) collective-permute-start(bf16[256,128]{1,0:T(8,128)(2,1)S(1)} %get-tuple-element.87), channel_id=1, source_target_pairs={{12,0},{16,4},{20,8},{24,12},{28,16},{13,1},{17,5},{21,9},{25,13},... | collective-permute-start | bytes 196616 | tf_op jit(solution)/shard_map/ppermute | solution.py:411
  74.9 0.0 collective-permute-done.20.theirs
  74.9 0.8 own_sum.1
  75.7 1.6 %collective-permute-start.21 = (bf16[4,256,128]{2,1,0:T(8,128)(2,1)S(1)}, bf16[4,256,128]{2,1,0:T(8,128)(2,1)S(1)}, u32[]{:S(2)}, u32[]{:S(2)}) collective-permute-start(bf16[4,256,128]{2,1,0:T(8,128)(2,1)S(1)} %get-tuple-element.94), channel_id=1, source_target_pairs={{0,2},{1,3},{2,0},{3,1},{4,6},{5,7},{6,4},{7,5},{8,10},{9,11},{10,... | collective-permute-start | bytes 786440 | tf_op jit(solution)/shard_map/ppermute | solution.py:408
  77.2 0.7 collective-permute-done.16.refs_0_
  78.0 3.8 %collective-permute-done.17.refs_1_ = bf16[256,128]{1,0:T(8,128)(2,1)S(1)} collective-permute-done((bf16[256,128]{1,0:T(8,128)(2,1)S(1)}, bf16[256,128]{1,0:T(8,128)(2,1)S(1)}, u32[]{:S(2)}, u32[]{:S(2)}) %collective-permute-start.17) | collective-permute-done | bytes 65568 | tf_op jit(solution)/shard_map/ppermute | solution.py:411
  81.8 1.8 %collective-permute-done.18.refs_2_ = bf16[256,128]{1,0:T(8,128)(2,1)S(1)} collective-permute-done((bf16[256,128]{1,0:T(8,128)(2,1)S(1)}, bf16[256,128]{1,0:T(8,128)(2,1)S(1)}, u32[]{:S(2)}, u32[]{:S(2)}) %collective-permute-start.18) | collective-permute-done | bytes 65568 | tf_op jit(solution)/shard_map/ppermute | solution.py:411
  83.5 0.1 collective-permute-done.19.refs_3_
  83.6 0.6 far_returns.1.returned
  84.2 0.2 collective-permute-done.21.refs_0_
  84.5 0.1 owner_sum.1.refs_0_
  84.6 1.6 %collective-permute-start.23 = (bf16[4,256,128]{2,1,0:T(8,128)(2,1)S(1)}, bf16[4,256,128]{2,1,0:T(8,128)(2,1)S(1)}, u32[]{:S(2)}, u32[]{:S(2)}) collective-permute-start(bf16[4,256,128]{2,1,0:T(8,128)(2,1)S(1)} %owner_sum.1.refs_0_), channel_id=1, source_target_pairs={{0,2},{1,3},{2,0},{3,1},{4,6},{5,7},{6,4},{7,5},{8,10},{9,11},{10,... | collective-permute-start | bytes 786440 | tf_op jit(solution)/shard_map/ppermute | solution.py:408
  86.1 0.0 collective-permute-start.22
  86.1 6.5 %collective-permute-done.23.refs_2_ = bf16[4,256,128]{2,1,0:T(8,128)(2,1)S(1)} collective-permute-done((bf16[4,256,128]{2,1,0:T(8,128)(2,1)S(1)}, bf16[4,256,128]{2,1,0:T(8,128)(2,1)S(1)}, u32[]{:S(2)}, u32[]{:S(2)}) %collective-permute-start.23) | collective-permute-done | bytes 262176 | tf_op jit(solution)/shard_map/ppermute | solution.py:408
  92.6 0.0 collective-permute-start.24
  92.6 0.0 collective-permute-done.22.refs_1_
  92.6 1.5 %collective-permute-done.24.refs_3_ = bf16[4,256,128]{2,1,0:T(8,128)(2,1)S(1)} collective-permute-done((bf16[4,256,128]{2,1,0:T(8,128)(2,1)S(1)}, bf16[4,256,128]{2,1,0:T(8,128)(2,1)S(1)}, u32[]{:S(2)}, u32[]{:S(2)}) %collective-permute-start.24) | collective-permute-done | bytes 262176 | tf_op jit(solution)/shard_map/ppermute | solution.py:405
  94.1 1.0 %spread.1 = (bf16[4,512,128]{2,1,0:T(8,128)(2,1)}, bf16[4,512,128]{2,1,0:T(8,128)(2,1)}) custom-call(bf16[4,256,128]{2,1,0:T(8,128)(2,1)S(1)} %owner_sum.1.refs_0_, bf16[4,256,128]{2,1,0:T(8,128)(2,1)S(1)} %collective-permute-done.22.refs_1_, bf16[4,256,128]{2,1,0:T(8,128)(2,1)S(1)} %collective-permute-done.23.refs_2_, ...), custom_call_target="tpu_custom_call" | custom-call | tf_op jit(solution)/shard_map/spread/pallas_call | solution.py:543
  (15 shorter events, 0.2 us)
Async XLA Ops:
  15.0 20.0 %copy-start.1 = (bf16[2048,128]{1,0:T(8,128)(2,1)S(1)}, bf16[2048,128]{1,0:T(8,128)(2,1)}, u32[]{:S(2)}) copy-start(bf16[2048,128]{1,0:T(8,128)(2,1)} %param.7) | copy-start | bytes 1572868
  15.0 20.0 %copy-start.4 = (bf16[2048,1,128]{2,0,1:T(8,128)(2,1)S(1)}, bf16[2048,1,128]{2,0,1:T(8,128)(2,1)}, u32[]{:S(2)}) copy-start(bf16[2048,1,128]{2,0,1:T(8,128)(2,1)} %param.5) | copy-start | bytes 1572868
  18.1 17.0 %copy-start = (bf16[2048,128]{1,0:T(8,128)(2,1)S(1)}, bf16[2048,128]{1,0:T(8,128)(2,1)}, u32[]{:S(2)}) copy-start(bf16[2048,128]{1,0:T(8,128)(2,1)} %param.6) | copy-start | bytes 1572868
  18.1 10.0 %collective-permute-start = (bf16[256,128]{1,0:T(8,128)(2,1)}, bf16[256,128]{1,0:T(8,128)(2,1)S(1)}, u32[]{:S(2)}, u32[]{:S(2)}) collective-permute-start(bf16[256,128]{1,0:T(8,128)(2,1)} %get-tuple-element.50), channel_id=1, source_target_pairs={{0,24},{4,28},{1,25},{5,29},{2,26},{6,30},{3,27},{7,31}} | collective-permute-start | bytes 196616 | tf_op jit(solution)/shard_map/ppermute | solution.py:414
  20.7 9.8 %collective-permute-start.1 = (bf16[256,128]{1,0:T(8,128)(2,1)}, bf16[256,128]{1,0:T(8,128)(2,1)S(1)}, u32[]{:S(2)}, u32[]{:S(2)}) collective-permute-start(bf16[256,128]{1,0:T(8,128)(2,1)} %get-tuple-element.51), channel_id=1, source_target_pairs={{0,20},{4,24},{8,28},{1,21},{5,25},{9,29},{2,22},{6,26},{10,30},{3... | collective-permute-start | bytes 196616 | tf_op jit(solution)/shard_map/ppermute | solution.py:414
  22.0 11.4 %collective-permute-start.2 = (bf16[256,128]{1,0:T(8,128)(2,1)}, bf16[256,128]{1,0:T(8,128)(2,1)S(1)}, u32[]{:S(2)}, u32[]{:S(2)}) collective-permute-start(bf16[256,128]{1,0:T(8,128)(2,1)} %get-tuple-element.52), channel_id=1, source_target_pairs={{0,16},{4,20},{8,24},{12,28},{1,17},{5,21},{9,25},{13,29},{2,18},{... | collective-permute-start | bytes 196616 | tf_op jit(solution)/shard_map/ppermute | solution.py:414
  23.3 10.1 %collective-permute-start.3 = (bf16[256,128]{1,0:T(8,128)(2,1)}, bf16[256,128]{1,0:T(8,128)(2,1)S(1)}, u32[]{:S(2)}, u32[]{:S(2)}) collective-permute-start(bf16[256,128]{1,0:T(8,128)(2,1)} %get-tuple-element.53), channel_id=1, source_target_pairs={{0,12},{4,16},{8,20},{12,24},{16,28},{1,13},{5,17},{9,21},{13,25},... | collective-permute-start | bytes 196616 | tf_op jit(solution)/shard_map/ppermute | solution.py:414
  25.8 16.1 %collective-permute-start.4 = (bf16[512,128]{1,0:T(8,128)(2,1)}, bf16[512,128]{1,0:T(8,128)(2,1)S(1)}, u32[]{:S(2)}, u32[]{:S(2)}) collective-permute-start(bf16[512,128]{1,0:T(8,128)(2,1)} %get-tuple-element.55), channel_id=1, source_target_pairs={{0,4},{4,8},{8,12},{12,16},{16,20},{20,24},{24,28},{1,5},{5,9},{9,... | collective-permute-start | bytes 393224 | tf_op jit(solution)/shard_map/ppermute | solution.py:414
  28.0 13.9 %collective-permute-start.5 = (bf16[512,128]{1,0:T(8,128)(2,1)}, bf16[512,128]{1,0:T(8,128)(2,1)S(1)}, u32[]{:S(2)}, u32[]{:S(2)}) collective-permute-start(bf16[512,128]{1,0:T(8,128)(2,1)} %get-tuple-element.56), channel_id=1, source_target_pairs={{0,8},{4,12},{8,16},{12,20},{16,24},{20,28},{1,9},{5,13},{9,17},{1... | collective-permute-start | bytes 393224 | tf_op jit(solution)/shard_map/ppermute | solution.py:414
  30.5 11.4 %collective-permute-start.6 = (bf16[512,128]{1,0:T(8,128)(2,1)}, bf16[512,128]{1,0:T(8,128)(2,1)S(1)}, u32[]{:S(2)}, u32[]{:S(2)}) collective-permute-start(bf16[512,128]{1,0:T(8,128)(2,1)} %get-tuple-element.57), channel_id=1, source_target_pairs={{0,28},{1,29},{2,30},{3,31}} | collective-permute-start | bytes 393224 | tf_op jit(solution)/shard_map/ppermute | solution.py:414
  33.5 1.6 %copy-start.2 = (s32[4,3]{1,0:T(4,128)S(1)}, s32[4,3]{1,0:T(4,128)}, u32[]{:S(2)}) copy-start(s32[4,3]{1,0:T(4,128)} %chosen.2) | copy-start | bytes 148
  33.5 9.0 %collective-permute-start.9 = (bf16[4,256,128]{2,1,0:T(8,128)(2,1)S(1)}, bf16[4,256,128]{2,1,0:T(8,128)(2,1)S(1)}, u32[]{:S(2)}, u32[]{:S(2)}) collective-permute-start(bf16[4,256,128]{2,1,0:T(8,128)(2,1)S(1)} %pad_maximum_fusion.1.refs_2_), channel_id=1, source_target_pairs={{0,2},{1,3},{2,0},{3,1},{4,6},{5,7},{6,4},{7,5},{8,10},{9,11},{10,... | collective-permute-start | bytes 786440 | tf_op jit(solution)/shard_map/ppermute | solution.py:408
  35.1 1.0 %copy-start.5 = (bf16[2048,1,128]{2,0,1:T(8,128)(2,1)S(1)}, bf16[2048,1,128]{2,0,1:T(8,128)(2,1)}, u32[]{:S(2)}) copy-start(bf16[2048,1,128]{2,0,1:T(8,128)(2,1)} %param.8) | copy-start | bytes 1572868
  41.9 2.6 %copy-start.6 = (bf16[2048,1,128]{2,0,1:T(8,128)(2,1)S(1)}, bf16[2048,1,128]{2,0,1:T(8,128)(2,1)}, u32[]{:S(2)}) copy-start(bf16[2048,1,128]{2,0,1:T(8,128)(2,1)} %param.8) | copy-start | bytes 1572868
  42.0 2.2 %collective-permute-start.7 = (bf16[3,512,128]{2,1,0:T(8,128)(2,1)S(1)}, bf16[3,512,128]{2,1,0:T(8,128)(2,1)S(1)}, u32[]{:S(2)}, u32[]{:S(2)}) collective-permute-start(bf16[3,512,128]{2,1,0:T(8,128)(2,1)S(1)} %pad_maximum_fusion.refs_0_), channel_id=1, source_target_pairs={{0,1},{1,0},{2,3},{3,2},{4,5},{5,4},{6,7},{7,6},{8,9},{9,8},{10,11... | collective-permute-start | bytes 1179656 | tf_op jit(solution)/shard_map/ppermute | solution.py:405
  42.1 2.1 %collective-permute-start.8 = (bf16[4,256,128]{2,1,0:T(8,128)(2,1)S(1)}, bf16[4,256,128]{2,1,0:T(8,128)(2,1)S(1)}, u32[]{:S(2)}, u32[]{:S(2)}) collective-permute-start(bf16[4,256,128]{2,1,0:T(8,128)(2,1)S(1)} %pad_maximum_fusion.1.refs_2_), channel_id=1, source_target_pairs={{0,1},{1,0},{2,3},{3,2},{4,5},{5,4},{6,7},{7,6},{8,9},{9,8},{10,11... | collective-permute-start | bytes 786440 | tf_op jit(solution)/shard_map/ppermute | solution.py:405
  42.6 2.0 %collective-permute-start.10 = (bf16[4,256,128]{2,1,0:T(8,128)(2,1)S(1)}, bf16[4,256,128]{2,1,0:T(8,128)(2,1)S(1)}, u32[]{:S(2)}, u32[]{:S(2)}) collective-permute-start(bf16[4,256,128]{2,1,0:T(8,128)(2,1)S(1)} %collective-permute-done.9.refs_4_), channel_id=1, source_target_pairs={{0,1},{1,0},{2,3},{3,2},{4,5},{5,4},{6,7},{7,6},{8,9},{9,8},{10,11... | collective-permute-start | bytes 786440 | tf_op jit(solution)/shard_map/ppermute | solution.py:405
  46.1 2.5 %collective-permute-start.11 = (bf16[7,512,128]{2,1,0:T(8,128)(2,1)S(1)}, bf16[7,512,128]{2,1,0:T(8,128)(2,1)S(1)}, u32[]{:S(2)}, u32[]{:S(2)}) collective-permute-start(bf16[7,512,128]{2,1,0:T(8,128)(2,1)S(1)} %get-tuple-element.65), channel_id=1, source_target_pairs={{0,1},{1,0},{2,3},{3,2},{4,5},{5,4},{6,7},{7,6},{8,9},{9,8},{10,11... | collective-permute-start | bytes 2752520 | tf_op jit(solution)/shard_map/ppermute | solution.py:405
  48.8 14.0 %collective-permute-start.13 = (bf16[512,128]{1,0:T(8,128)(2,1)S(1)}, bf16[512,128]{1,0:T(8,128)(2,1)S(1)}, u32[]{:S(2)}, u32[]{:S(2)}) collective-permute-start(bf16[512,128]{1,0:T(8,128)(2,1)S(1)} %get-tuple-element.78), channel_id=1, source_target_pairs={{4,0},{8,4},{12,8},{16,12},{20,16},{24,20},{28,24},{5,1},{9,5},{13... | collective-permute-start | bytes 393224 | tf_op jit(solution)/shard_map/ppermute | solution.py:411
  50.1 12.7 %collective-permute-start.14 = (bf16[512,128]{1,0:T(8,128)(2,1)S(1)}, bf16[512,128]{1,0:T(8,128)(2,1)S(1)}, u32[]{:S(2)}, u32[]{:S(2)}) collective-permute-start(bf16[512,128]{1,0:T(8,128)(2,1)S(1)} %get-tuple-element.79), channel_id=1, source_target_pairs={{8,0},{12,4},{16,8},{20,12},{24,16},{28,20},{9,1},{13,5},{17,9},{2... | collective-permute-start | bytes 393224 | tf_op jit(solution)/shard_map/ppermute | solution.py:411
  51.4 18.2 %collective-permute-start.15 = (bf16[512,128]{1,0:T(8,128)(2,1)S(1)}, bf16[512,128]{1,0:T(8,128)(2,1)S(1)}, u32[]{:S(2)}, u32[]{:S(2)}) collective-permute-start(bf16[512,128]{1,0:T(8,128)(2,1)S(1)} %get-tuple-element.80), channel_id=1, source_target_pairs={{28,0},{29,1},{30,2},{31,3}} | collective-permute-start | bytes 393224 | tf_op jit(solution)/shard_map/ppermute | solution.py:411
  52.7 16.9 %collective-permute-start.12 = (bf16[4,256,128]{2,1,0:T(8,128)(2,1)S(1)}, bf16[4,256,128]{2,1,0:T(8,128)(2,1)S(1)}, u32[]{:S(2)}, u32[]{:S(2)}) collective-permute-start(bf16[4,256,128]{2,1,0:T(8,128)(2,1)S(1)} %get-tuple-element.77), channel_id=1, source_target_pairs={{0,2},{1,3},{2,0},{3,1},{4,6},{5,7},{6,4},{7,5},{8,10},{9,11},{10,... | collective-permute-start | bytes 786440 | tf_op jit(solution)/shard_map/ppermute | solution.py:408
  69.6 5.3 %collective-permute-start.20 = (bf16[4,512,128]{2,1,0:T(8,128)(2,1)S(1)}, bf16[4,512,128]{2,1,0:T(8,128)(2,1)S(1)}, u32[]{:S(2)}, u32[]{:S(2)}) collective-permute-start(bf16[4,512,128]{2,1,0:T(8,128)(2,1)S(1)} %get-tuple-element.89), channel_id=1, source_target_pairs={{0,1},{1,0},{2,3},{3,2},{4,5},{5,4},{6,7},{7,6},{8,9},{9,8},{10,11... | collective-permute-start | bytes 1572872 | tf_op jit(solution)/shard_map/ppermute | solution.py:405
  69.7 8.3 %collective-permute-start.16 = (bf16[256,128]{1,0:T(8,128)(2,1)S(1)}, bf16[256,128]{1,0:T(8,128)(2,1)S(1)}, u32[]{:S(2)}, u32[]{:S(2)}) collective-permute-start(bf16[256,128]{1,0:T(8,128)(2,1)S(1)} %get-tuple-element.84), channel_id=1, source_target_pairs={{24,0},{28,4},{25,1},{29,5},{26,2},{30,6},{27,3},{31,7}} | collective-permute-start | bytes 196616 | tf_op jit(solution)/shard_map/ppermute | solution.py:411
  71.0 10.8 %collective-permute-start.17 = (bf16[256,128]{1,0:T(8,128)(2,1)S(1)}, bf16[256,128]{1,0:T(8,128)(2,1)S(1)}, u32[]{:S(2)}, u32[]{:S(2)}) collective-permute-start(bf16[256,128]{1,0:T(8,128)(2,1)S(1)} %get-tuple-element.85), channel_id=1, source_target_pairs={{20,0},{24,4},{28,8},{21,1},{25,5},{29,9},{22,2},{26,6},{30,10},{2... | collective-permute-start | bytes 196616 | tf_op jit(solution)/shard_map/ppermute | solution.py:411
  72.3 11.3 %collective-permute-start.18 = (bf16[256,128]{1,0:T(8,128)(2,1)S(1)}, bf16[256,128]{1,0:T(8,128)(2,1)S(1)}, u32[]{:S(2)}, u32[]{:S(2)}) collective-permute-start(bf16[256,128]{1,0:T(8,128)(2,1)S(1)} %get-tuple-element.86), channel_id=1, source_target_pairs={{16,0},{20,4},{24,8},{28,12},{17,1},{21,5},{25,9},{29,13},{18,2},{... | collective-permute-start | bytes 196616 | tf_op jit(solution)/shard_map/ppermute | solution.py:411
  73.6 1.3 %copy-start.3 = (s32[7]{0:T(128)S(1)}, s32[7]{0:T(128)}, u32[]{:S(2)}) copy-start(s32[7]{0:T(128)} %get-tuple-element.75.asked) | copy-start | bytes 88
  73.6 10.0 %collective-permute-start.19 = (bf16[256,128]{1,0:T(8,128)(2,1)S(1)}, bf16[256,128]{1,0:T(8,128)(2,1)S(1)}, u32[]{:S(2)}, u32[]{:S(2)}) collective-permute-start(bf16[256,128]{1,0:T(8,128)(2,1)S(1)} %get-tuple-element.87), channel_id=1, source_target_pairs={{12,0},{16,4},{20,8},{24,12},{28,16},{13,1},{17,5},{21,9},{25,13},... | collective-permute-start | bytes 196616 | tf_op jit(solution)/shard_map/ppermute | solution.py:411
  75.7 8.8 %collective-permute-start.21 = (bf16[4,256,128]{2,1,0:T(8,128)(2,1)S(1)}, bf16[4,256,128]{2,1,0:T(8,128)(2,1)S(1)}, u32[]{:S(2)}, u32[]{:S(2)}) collective-permute-start(bf16[4,256,128]{2,1,0:T(8,128)(2,1)S(1)} %get-tuple-element.94), channel_id=1, source_target_pairs={{0,2},{1,3},{2,0},{3,1},{4,6},{5,7},{6,4},{7,5},{8,10},{9,11},{10,... | collective-permute-start | bytes 786440 | tf_op jit(solution)/shard_map/ppermute | solution.py:408
  84.6 8.0 %collective-permute-start.23 = (bf16[4,256,128]{2,1,0:T(8,128)(2,1)S(1)}, bf16[4,256,128]{2,1,0:T(8,128)(2,1)S(1)}, u32[]{:S(2)}, u32[]{:S(2)}) collective-permute-start(bf16[4,256,128]{2,1,0:T(8,128)(2,1)S(1)} %owner_sum.1.refs_0_), channel_id=1, source_target_pairs={{0,2},{1,3},{2,0},{3,1},{4,6},{5,7},{6,4},{7,5},{8,10},{9,11},{10,... | collective-permute-start | bytes 786440 | tf_op jit(solution)/shard_map/ppermute | solution.py:408
  86.1 6.5 %collective-permute-start.22 = (bf16[4,256,128]{2,1,0:T(8,128)(2,1)S(1)}, bf16[4,256,128]{2,1,0:T(8,128)(2,1)S(1)}, u32[]{:S(2)}, u32[]{:S(2)}) collective-permute-start(bf16[4,256,128]{2,1,0:T(8,128)(2,1)S(1)} %owner_sum.1.refs_0_), channel_id=1, source_target_pairs={{0,1},{1,0},{2,3},{3,2},{4,5},{5,4},{6,7},{7,6},{8,9},{9,8},{10,11... | collective-permute-start | bytes 786440 | tf_op jit(solution)/shard_map/ppermute | solution.py:405
  92.6 1.5 %collective-permute-start.24 = (bf16[4,256,128]{2,1,0:T(8,128)(2,1)S(1)}, bf16[4,256,128]{2,1,0:T(8,128)(2,1)S(1)}, u32[]{:S(2)}, u32[]{:S(2)}) collective-permute-start(bf16[4,256,128]{2,1,0:T(8,128)(2,1)S(1)} %collective-permute-done.23.refs_2_), channel_id=1, source_target_pairs={{0,1},{1,0},{2,3},{3,2},{4,5},{5,4},{6,7},{7,6},{8,9},{9,8},{10,11... | collective-permute-start | bytes 786440 | tf_op jit(solution)/shard_map/ppermute | solution.py:405

commit v5 on v4

--- a/solution.py
+++ b/solution.py
@@ -177,7 +177,7 @@
     factor, scaling, blocks_here, chips, far, near, piece, chosen, q, do, stats, *refs
 ):
     near_refs, far_refs, refs = refs[:2], refs[2 : 2 + 2 * chips], refs[2 + 2 * chips :]
-    keep, send, final, grad_qt, rows, acc, s_buf, dp_buf, parts = refs
+    keep, send, final, ds_far, rows, acc, s_buf, dp_buf, parts = refs
     place = lax.axis_index("head")
     core, chip = lax.rem(place, 2), lax.div(place, 2)
     block_len = rows.shape[2]
@@ -234,7 +234,6 @@
             weighted = weighted + scale * parts[t, 2:3, :]
         final[row, 0:1, :] = top + jnp.log2(total)
         final[row, 1:2, :] = weighted / total
-        grad_qt[row] = jnp.zeros_like(grad_qt[row])
         for t in range(3):
             slot = slot_of(chosen, blocks_here, row, t) - blocks_here
 
@@ -246,7 +245,7 @@
                 dscores = (weights * (dp_buf[t] - delta)).astype(BF16)
                 acc[1, slot] += dot_nn(weights.astype(BF16), do[span, :])
                 acc[0, slot] += dot_nn(dscores, q[span, :])
-                grad_qt[row] += dot_nn(rows[0, slot].T, dscores)
+                ds_far[row * 3 + t] = dscores
 
         return 0
 
@@ -258,9 +257,9 @@
 
 
 def local_kernel(
-    factor, scaling, blocks_here, chosen, q, do, keys, values, final, grad_qt,
-    keep, send, grad_q,
-    acc, total_qt,
+    factor, scaling, blocks_here, chosen, q, do, keys, values, final,
+    keep, send, ds_own,
+    acc,
 ):
     core = lax.rem(lax.axis_index("head"), 2)
     block_len = keys.shape[1]
@@ -279,7 +278,7 @@
             scores = dot_nt(keys[slot, cut, :], rows_from(q, first))
             return scores, dot_nt(values[slot, cut, :], rows_from(do, first))
 
-        def pair(slot, seconds, masked):
+        def pair(slot, t, seconds, masked):
             parts = ((0, 0), (half, seconds))
             ready = [products(slot, c, first) for c, first in parts]
             sides = []
@@ -293,18 +292,17 @@
                 cut = pl.ds(c, half)
                 acc[1, slot, cut, :] += dot_nn(weights, rows_from(do, first))
                 acc[0, slot, cut, :] += dot_nn(dscores, rows_from(q, first))
-                total_qt[:, first:] += dot_nn(keys[slot, cut, :].T, dscores)
-
-        total_qt[...] = grad_qt[row]
-        pair(row, half, True)
+                ds_own[row * 4 + t, cut, first:] = dscores
+
+        ds_own[row * 4 + 3, half:, :half] = jnp.zeros((half, half), BF16)
+        pair(row, 3, half, True)
         for t in range(3):
             slot = slot_of(chosen, blocks_here, row, t)
 
             @pl.when((slot >= 0) & (slot < blocks_here))
             def _():
-                pair(slot, 0, False)
-
-        grad_q[span, :] = (total_qt[...].T * scaling).astype(BF16)
+                pair(slot, t, 0, False)
+
         return 0
 
     lax.fori_loop(0, blocks_here, per_row, 0)
@@ -312,6 +310,29 @@
     send_scale = jnp.where(core == 0, 1.0, scaling)
     keep[...] = (acc[core] * keep_scale).astype(BF16)
     send[...] = (acc[1 - core] * send_scale).astype(BF16)
+
+
+def query_kernel(scaling, blocks_here, chosen, keys, rows, ds_far, ds_own, grad_q, total_qt):
+    block_len = keys.shape[1]
+
+    def per_row(row, _):
+        total_qt[...] = dot_nn(keys[row].T, ds_own[row * 4 + 3])
+        for t in range(3):
+            slot = slot_of(chosen, blocks_here, row, t)
+
+            @pl.when((slot >= 0) & (slot < blocks_here))
+            def _():
+                total_qt[...] += dot_nn(keys[slot].T, ds_own[row * 4 + t])
+
+            @pl.when(slot >= blocks_here)
+            def _():
+                total_qt[...] += dot_nn(rows[0, slot - blocks_here].T, ds_far[row * 3 + t])
+
+        span = pl.ds(row * block_len, block_len)
+        grad_q[span, :] = (total_qt[...].T * scaling).astype(BF16)
+        return 0
+
+    lax.fori_loop(0, blocks_here, per_row, 0)
 
 
 def far_return_kernel(far, asked, *refs):
@@ -388,7 +409,8 @@
     own_type = jax.ShapeDtypeStruct(local_shape, BF16)
     block_type = jax.ShapeDtypeStruct((block_len, feature), BF16)
     piece_type = jax.ShapeDtypeStruct((piece, feature), BF16)
-    qt_type = jax.ShapeDtypeStruct((blocks_here, feature, block_len), F32)
+    square = (block_len, block_len)
+    ds_bytes = block_len * block_len * 2
     pair_flops = 2 * block_len * block_len * feature
     block_bytes = block_len * feature * 2
     pair_bytes = block_len * block_len * 4
@@ -447,21 +469,30 @@
     for part in far_more:
         row_sets += [part, swap(part)]
 
-    keep_far, send_far, final, grad_qt = pl.pallas_call(
+    keep_far, send_far, final, ds_far, far_rows = pl.pallas_call(
         functools.partial(
             remote_kernel, factor, scaling, blocks_here, chips, far, near, piece
         ),
         in_specs=[smem] + [whole] * (3 + len(row_sets)),
-        out_specs=[whole] * 4,
-        out_shape=[far_type, far_type, stat_type, qt_type],
+        out_specs=[whole] * 5,
+        out_shape=[
+            far_type,
+            far_type,
+            stat_type,
+            jax.ShapeDtypeStruct((3 * blocks_here,) + square, BF16),
+            jax.ShapeDtypeStruct((2,) + remote_shape, BF16),
+        ],
         scratch_shapes=[
-            pltpu.VMEM((2,) + remote_shape, BF16),
             pltpu.VMEM((2,) + remote_shape, F32),
             pltpu.VMEM((3, block_len, block_len), F32),
             pltpu.VMEM((3, block_len, block_len), F32),
             pltpu.VMEM((4, 8, block_len), F32),
         ],
-        compiler_params=params((10 * shifts + 4 * blocks_here) * block_bytes + 6 * pair_bytes),
+        compiler_params=params(
+            (10 * shifts + 4 * blocks_here) * block_bytes
+            + 6 * pair_bytes
+            + 3 * blocks_here * ds_bytes
+        ),
         cost_estimate=cost(60, 8 * tok_rows * feature * 2),
         name="remote_pairs",
     )(chosen, q2, do2, stats, *row_sets)
@@ -490,19 +521,20 @@
     far_sums, near_sums = chip_far[:chips], chip_far[chips:]
     far_parts = [to_chip(far_sums[d], d) for d in range(1, chips)]
     near_back = [to_owner(near_sums[i], s) for i, s in enumerate(near)]
-    keep_own, send_own, grad_q = pl.pallas_call(
+    keep_own, send_own, ds_own = pl.pallas_call(
         functools.partial(local_kernel, factor, scaling, blocks_here),
-        in_specs=[smem] + [whole] * 6,
+        in_specs=[smem] + [whole] * 5,
         out_specs=[whole] * 3,
-        out_shape=[own_type, own_type, jax.ShapeDtypeStruct((tok_rows, feature), BF16)],
-        scratch_shapes=[
-            pltpu.VMEM((2,) + local_shape, F32),
-            pltpu.VMEM((feature, block_len), F32),
+        out_shape=[
+            own_type,
+            own_type,
+            jax.ShapeDtypeStruct((4 * blocks_here,) + square, BF16),
         ],
-        compiler_params=params(14 * blocks_here * block_bytes),
+        scratch_shapes=[pltpu.VMEM((2,) + local_shape, F32)],
+        compiler_params=params(12 * blocks_here * block_bytes + 4 * blocks_here * ds_bytes),
         cost_estimate=cost(60, 8 * tok_rows * feature * 2),
         name="local_pairs",
-    )(chosen, q2, do2, key_blocks, value_blocks, final, grad_qt)
+    )(chosen, q2, do2, key_blocks, value_blocks, final)
     far_parts, near_back, keep_own, send_own = lax.optimization_barrier(
         (far_parts, near_back, keep_own, send_own)
     )
@@ -536,9 +568,23 @@
         compiler_params=params(6 * blocks_here * block_bytes),
         name="owner_sum",
     )(returned, own_sums[0], *own_parts)
+    mine, ds_own = lax.optimization_barrier((mine, ds_own))
+    gathered = [to_chip(mine, d) for d in range(1, chips)]
+    grad_q = pl.pallas_call(
+        functools.partial(query_kernel, scaling, blocks_here),
+        in_specs=[smem] + [whole] * 4,
+        out_specs=whole,
+        out_shape=jax.ShapeDtypeStruct((tok_rows, feature), BF16),
+        scratch_shapes=[pltpu.VMEM((feature, block_len), F32)],
+        compiler_params=params(
+            (3 * blocks_here + 2 * shifts) * block_bytes + 7 * blocks_here * ds_bytes
+        ),
+        cost_estimate=cost(30, 8 * tok_rows * feature * 2),
+        name="query_grads",
+    )(chosen, key_blocks, far_rows, ds_far, ds_own)
+    gathered, grad_q = lax.optimization_barrier((gathered, grad_q))
     spread = [mine, swap(mine)]
-    for d in range(1, chips):
-        part = to_chip(mine, d)
+    for part in gathered:
         spread += [part, swap(part)]
     grad_keys, grad_values = pl.pallas_call(
         functools.partial(spread_kernel, chips, piece),

time: 95.7 us -> 98.3 us (1.027)
  local copies, waits for them, and re-layouts: 1.84 us -> 5.64 us
  Pallas kernels: 22.5 us -> 25.2 us
  waiting for transfers between devices: 25.6 us -> 23.5 us
  starting transfers between devices: 30.5 us -> 28.6 us
    pallas_call x0 -> x1, Pallas kernels: none -> 4.46 us  [body(): pl.pallas_call(functools.partial(query_kernel, scaling, blocks_here), in_...]
    unnamed x14 -> x22, local copies, waits for them, and re-layouts: 1.07 us -> 4.87 us
    ppermute x4, waiting for transfers between devices: 6.71 us -> 3.21 us  [to_chip(): lax.ppermute(array, 'head', [(h, (h + 2 * d) % heads) for h in range(head...]
    ppermute x4, starting transfers between devices: 5.32 us -> 3.36 us  [to_chip(): lax.ppermute(array, 'head', [(h, (h + 2 * d) % heads) for h in range(head...]
    pallas_call x1, Pallas kernels: 9.44 us -> 7.76 us  [body(): pl.pallas_call(functools.partial(local_kernel, factor, scaling, blocks_he...]
    ppermute x7, waiting for transfers between devices: 13.1 us -> 14.5 us  [to_owner(): lax.ppermute(array, 'ctx', [(c, c - s - 1) for c in range(s + 1, ctx_coun...]
  transfers between devices with their start and end apart: 25 -> 25, of which waited for: 11 -> 11; matrix products, arithmetic and copies ran while one was open for 0% -> 0% of each run, Pallas kernels for 18% -> 20%
where the time goes in v5:
time: 98.3 us; the launch traced here: 97.4 us
  starting transfers between devices  28.6 us (29%)
  Pallas kernels  25.2 us (26%)
  waiting for transfers between devices  23.5 us (24%)
  blocking collectives  13.5 us (14%)
  local copies, waits for them, and re-layouts  5.64 us (6%)
    ppermute x7, starting transfers between devices, to_reader(): lax.ppermute(array, 'ctx', [(c - s - 1, c) for c in range(s + 1, ctx_coun...  15.3 us
    ppermute x7, waiting for transfers between devices, to_owner(): lax.ppermute(array, 'ctx', [(c, c - s - 1) for c in range(s + 1, ctx_coun...  14.5 us
    all_to_all x1, blocking collectives, body(): lax.all_to_all(jnp.broadcast_to(selected.reshape(1, 3 * blocks_here), (ct...  13.5 us
    ppermute x7, starting transfers between devices, to_owner(): lax.ppermute(array, 'ctx', [(c, c - s - 1) for c in range(s + 1, ctx_coun...  9.04 us
    pallas_call x1, Pallas kernels, body(): pl.pallas_call(functools.partial(local_kernel, factor, scaling, blocks_he...  7.76 us
    ppermute x7, waiting for transfers between devices, swap(): return lax.ppermute(array, 'head', [(h, h ^ 1) for h in range(heads)])  5.76 us
    pallas_call x1, Pallas kernels, body(): pl.pallas_call(functools.partial(local_stats_kernel, factor, blocks_here)...  5.72 us
    unnamed x22, local copies, waits for them, and re-layouts  4.87 us
  transfers between devices with their start and end apart: 25, of which 11 were waited for; matrix products, arithmetic and copies ran while one was open for 0% of the time, Pallas kernels for 20%

profile of v5, /device:TPU:0, one launch (start us, length us, event | category | flops | bytes accessed | tf_op | source)
XLA Modules:
  0.0 97.4 jit_solution(12531751647423836874)
XLA Ops:
  0.6 0.8 broadcast_in_dim.7
  1.4 13.5 %all_to_all.8 = s32[8,1,12]{2,1,0:T(1,128)} all-to-all(s32[8,1,12]{2,1,0:T(1,128)S(1)} %broadcast_in_dim.8), channel_id=1, replica_groups=mesh['ctx'=8,'head'=4] {'ctx'}, dimensions={0} | all-to-all | bytes 768 | tf_op jit(solution)/shard_map/all_to_all | solution.py:438
  14.9 2.9 %pick_rows.1 = (s32[7]{0:T(128)}, bf16[512,128]{1,0:T(8,128)(2,1)}, bf16[512,128]{1,0:T(8,128)(2,1)}, bf16[256,128]{1,0:T(8,128)(2,1)}, bf16[256,128]{1,0:T(8,12...) custom-call(s32[8,12]{1,0:T(8,128)} %bitcast.36, ...), custom_call_target="tpu_custom_call" | custom-call | tf_op jit(solution)/shard_map/pick_rows/pallas_call | solution.py:442
  17.8 2.7 %collective-permute-start = (bf16[256,128]{1,0:T(8,128)(2,1)}, bf16[256,128]{1,0:T(8,128)(2,1)S(1)}, u32[]{:S(2)}, u32[]{:S(2)}) collective-permute-start(bf16[256,128]{1,0:T(8,128)(2,1)} %get-tuple-element.56), channel_id=1, source_target_pairs={{0,24},{4,28},{1,25},{5,29},{2,26},{6,30},{3,27},{7,31}} | collective-permute-start | bytes 196616 | tf_op jit(solution)/shard_map/ppermute | solution.py:436
  20.5 1.3 %collective-permute-start.1 = (bf16[256,128]{1,0:T(8,128)(2,1)}, bf16[256,128]{1,0:T(8,128)(2,1)S(1)}, u32[]{:S(2)}, u32[]{:S(2)}) collective-permute-start(bf16[256,128]{1,0:T(8,128)(2,1)} %get-tuple-element.57), channel_id=1, source_target_pairs={{0,20},{4,24},{8,28},{1,21},{5,25},{9,29},{2,22},{6,26},{10,30},{3... | collective-permute-start | bytes 196616 | tf_op jit(solution)/shard_map/ppermute | solution.py:436
  21.8 1.3 %collective-permute-start.2 = (bf16[256,128]{1,0:T(8,128)(2,1)}, bf16[256,128]{1,0:T(8,128)(2,1)S(1)}, u32[]{:S(2)}, u32[]{:S(2)}) collective-permute-start(bf16[256,128]{1,0:T(8,128)(2,1)} %get-tuple-element.58), channel_id=1, source_target_pairs={{0,16},{4,20},{8,24},{12,28},{1,17},{5,21},{9,25},{13,29},{2,18},{... | collective-permute-start | bytes 196616 | tf_op jit(solution)/shard_map/ppermute | solution.py:436
  23.1 2.5 %collective-permute-start.3 = (bf16[256,128]{1,0:T(8,128)(2,1)}, bf16[256,128]{1,0:T(8,128)(2,1)S(1)}, u32[]{:S(2)}, u32[]{:S(2)}) collective-permute-start(bf16[256,128]{1,0:T(8,128)(2,1)} %get-tuple-element.59), channel_id=1, source_target_pairs={{0,12},{4,16},{8,20},{12,24},{16,28},{1,13},{5,17},{9,21},{13,25},... | collective-permute-start | bytes 196616 | tf_op jit(solution)/shard_map/ppermute | solution.py:436
  25.6 2.2 %collective-permute-start.4 = (bf16[512,128]{1,0:T(8,128)(2,1)}, bf16[512,128]{1,0:T(8,128)(2,1)S(1)}, u32[]{:S(2)}, u32[]{:S(2)}) collective-permute-start(bf16[512,128]{1,0:T(8,128)(2,1)} %get-tuple-element.61), channel_id=1, source_target_pairs={{0,4},{4,8},{8,12},{12,16},{16,20},{20,24},{24,28},{1,5},{5,9},{9,... | collective-permute-start | bytes 393224 | tf_op jit(solution)/shard_map/ppermute | solution.py:436
  27.7 0.0 collective-permute-done
  27.8 2.5 %collective-permute-start.5 = (bf16[512,128]{1,0:T(8,128)(2,1)}, bf16[512,128]{1,0:T(8,128)(2,1)S(1)}, u32[]{:S(2)}, u32[]{:S(2)}) collective-permute-start(bf16[512,128]{1,0:T(8,128)(2,1)} %get-tuple-element.62), channel_id=1, source_target_pairs={{0,8},{4,12},{8,16},{12,20},{16,24},{20,28},{1,9},{5,13},{9,17},{1... | collective-permute-start | bytes 393224 | tf_op jit(solution)/shard_map/ppermute | solution.py:436
  30.2 0.0 collective-permute-done.1
  30.2 2.9 %collective-permute-start.6 = (bf16[512,128]{1,0:T(8,128)(2,1)}, bf16[512,128]{1,0:T(8,128)(2,1)S(1)}, u32[]{:S(2)}, u32[]{:S(2)}) collective-permute-start(bf16[512,128]{1,0:T(8,128)(2,1)} %get-tuple-element.63), channel_id=1, source_target_pairs={{0,28},{1,29},{2,30},{3,31}} | collective-permute-start | bytes 393224 | tf_op jit(solution)/shard_map/ppermute | solution.py:436
  33.2 0.0 collective-permute-done.2
  33.2 0.0 collective-permute-done.3
  33.2 1.6 %collective-permute-start.9 = (bf16[4,256,128]{2,1,0:T(8,128)(2,1)S(1)}, bf16[4,256,128]{2,1,0:T(8,128)(2,1)S(1)}, u32[]{:S(2)}, u32[]{:S(2)}) collective-permute-start(bf16[4,256,128]{2,1,0:T(8,128)(2,1)S(1)} %pad_maximum_fusion.1.refs_2_), channel_id=1, source_target_pairs={{0,2},{1,3},{2,0},{3,1},{4,6},{5,7},{6,4},{7,5},{8,10},{9,11},{10,... | collective-permute-start | bytes 786440 | tf_op jit(solution)/shard_map/ppermute | solution.py:430
  34.8 1.0 %copy-done = bf16[2048,128]{1,0:T(8,128)(2,1)S(1)} copy-done((bf16[2048,128]{1,0:T(8,128)(2,1)S(1)}, bf16[2048,128]{1,0:T(8,128)(2,1)}, u32[]{:S(2)}) %copy-start) | copy-done | bytes 524312
  35.8 1.0 %copy-done.2 = bf16[2048,128]{1,0:T(8,128)(2,1)S(1)} copy-done((bf16[2048,128]{1,0:T(8,128)(2,1)S(1)}, bf16[2048,128]{1,0:T(8,128)(2,1)}, u32[]{:S(2)}) %copy-start.2) | copy-done | bytes 524312
  36.9 0.7 copy-done.4
  37.6 1.0 %copy-done.7 = bf16[2048,1,128]{2,0,1:T(8,128)(2,1)S(1)} copy-done((bf16[2048,1,128]{2,0,1:T(8,128)(2,1)S(1)}, bf16[2048,1,128]{2,0,1:T(8,128)(2,1)}, u32[]{:S(2)}) %copy-start.7) | copy-done | bytes 524312
  38.6 1.0 %copy-done.9 = bf16[2048,1,128]{2,0,1:T(8,128)(2,1)S(1)} copy-done((bf16[2048,1,128]{2,0,1:T(8,128)(2,1)S(1)}, bf16[2048,1,128]{2,0,1:T(8,128)(2,1)}, u32[]{:S(2)}) %copy-start.9) | copy-done | bytes 524312
  39.7 5.7 %local_stats.1.stats = f32[4,8,512]{2,1,0:T(8,128)S(1)} custom-call(s32[4,3]{1,0:T(4,128)S(1)} %copy-done.4, bf16[2048,128]{1,0:T(8,128)(2,1)S(1)} %bitcast.22, bf16[2048,128]{1,0:T(8,128)(2,1)S(1)} %bitcast.25, bf16[4,512,128]{2,1,0:T(8,128)(2,1)S(1)} %bitcast.16, bf16[4,512,128]{2,1,0:T(8,128)(2,1)S(1)} %bitcast.20), custom_call_target="tpu_custom_call" | custom-call | flops 2013265920 | bytes 2097152 | tf_op jit(solution)/shard_map/local_stats/pallas_call | solution.py:456
  45.4 0.0 collective-permute-done.4
  45.5 0.0 copy-start.1
  45.5 0.0 copy-start.3
  45.5 0.1 collective-permute-start.7
  45.6 0.5 collective-permute-start.8
  46.1 0.0 collective-permute-done.9.refs_4_
  46.1 0.1 collective-permute-start.10
  46.1 1.5 %collective-permute-done.8.refs_3_ = bf16[4,256,128]{2,1,0:T(8,128)(2,1)S(1)} collective-permute-done((bf16[4,256,128]{2,1,0:T(8,128)(2,1)S(1)}, bf16[4,256,128]{2,1,0:T(8,128)(2,1)S(1)}, u32[]{:S(2)}, u32[]{:S(2)}) %collective-permute-start.8) | collective-permute-done | bytes 262176 | tf_op jit(solution)/shard_map/ppermute | solution.py:427
  47.7 0.4 collective-permute-done.10.refs_5_
  48.0 1.6 %remote_pairs.1 = (bf16[7,512,128]{2,1,0:T(8,128)(2,1)S(1)}, bf16[7,512,128]{2,1,0:T(8,128)(2,1)S(1)}, f32[4,8,512]{2,1,0:T(8,128)S(1)}, bf16[12,512,512]{2,1,0:T(8,128)(2,1)S(1)}, bf16[2,7,512,128]{3,2,1,0:T(8,128)(2,1)S(1)}) custom-call(s32[4,3]{1,0:T(4,128)S(1)} %copy-done.5, bf16[2048,128]{1,0:T(8,128)(2,1)S(1)} %bitcast.23, ...), custom_call_target="tpu_custom_call" | custom-call | flops 4026531840 | bytes 4194304 | tf_op jit(solution)/shard_map/remote_pairs/pallas_call | solution.py:472
  49.6 0.2 collective-permute-start.11
  49.8 2.3 %collective-permute-done.11.theirs = bf16[7,512,128]{2,1,0:T(8,128)(2,1)S(1)} collective-permute-done((bf16[7,512,128]{2,1,0:T(8,128)(2,1)S(1)}, bf16[7,512,128]{2,1,0:T(8,128)(2,1)S(1)}, u32[]{:S(2)}, u32[]{:S(2)}) %collective-permute-start.11) | collective-permute-done | bytes 917536 | tf_op jit(solution)/shard_map/ppermute | solution.py:427
  52.1 0.2 chip_sum.1
  52.4 1.3 %collective-permute-start.13 = (bf16[512,128]{1,0:T(8,128)(2,1)S(1)}, bf16[512,128]{1,0:T(8,128)(2,1)S(1)}, u32[]{:S(2)}, u32[]{:S(2)}) collective-permute-start(bf16[512,128]{1,0:T(8,128)(2,1)S(1)} %get-tuple-element.80), channel_id=1, source_target_pairs={{4,0},{8,4},{12,8},{16,12},{20,16},{24,20},{28,24},{5,1},{9,5},{13... | collective-permute-start | bytes 393224 | tf_op jit(solution)/shard_map/ppermute | solution.py:433
  53.7 1.3 %collective-permute-start.14 = (bf16[512,128]{1,0:T(8,128)(2,1)S(1)}, bf16[512,128]{1,0:T(8,128)(2,1)S(1)}, u32[]{:S(2)}, u32[]{:S(2)}) collective-permute-start(bf16[512,128]{1,0:T(8,128)(2,1)S(1)} %get-tuple-element.81), channel_id=1, source_target_pairs={{8,0},{12,4},{16,8},{20,12},{24,16},{28,20},{9,1},{13,5},{17,9},{2... | collective-permute-start | bytes 393224 | tf_op jit(solution)/shard_map/ppermute | solution.py:433
  55.0 1.3 %collective-permute-start.15 = (bf16[512,128]{1,0:T(8,128)(2,1)S(1)}, bf16[512,128]{1,0:T(8,128)(2,1)S(1)}, u32[]{:S(2)}, u32[]{:S(2)}) collective-permute-start(bf16[512,128]{1,0:T(8,128)(2,1)S(1)} %get-tuple-element.82), channel_id=1, source_target_pairs={{28,0},{29,1},{30,2},{31,3}} | collective-permute-start | bytes 393224 | tf_op jit(solution)/shard_map/ppermute | solution.py:433
  56.3 0.6 collective-permute-start.12
  56.9 7.8 %local_pairs.1 = (bf16[4,512,128]{2,1,0:T(8,128)(2,1)S(1)}, bf16[4,512,128]{2,1,0:T(8,128)(2,1)S(1)}, bf16[16,512,512]{2,1,0:T(8,128)(2,1)S(1)}) custom-call(s32[4,3]{1,0:T(4,128)S(1)} %copy-done.5, bf16[2048,128]{1,0:T(8,128)(2,1)S(1)} %bitcast.24, bf16[2048,128]{1,0:T(8,128)(2,1)S(1)} %bitcast.27, bf16[4,512,128]{2,1,0:T(8,128)(2,1)S(1)} %bitcast.17, ...), custom_call_target="tpu_custom_call" | custom-call | flops 4026531840 | bytes 4194304 | tf_op jit(solution)/shard_map/local_pairs/pallas_call | solution.py:524
  64.6 0.0 collective-permute-done.13.refs_0_
  64.7 7.2 %collective-permute-done.15.refs_2_ = bf16[512,128]{1,0:T(8,128)(2,1)S(1)} collective-permute-done((bf16[512,128]{1,0:T(8,128)(2,1)S(1)}, bf16[512,128]{1,0:T(8,128)(2,1)S(1)}, u32[]{:S(2)}, u32[]{:S(2)}) %collective-permute-start.15) | collective-permute-done | bytes 131104 | tf_op jit(solution)/shard_map/ppermute | solution.py:433
  71.8 0.0 collective-permute-done.12.refs_0_
  71.8 0.0 collective-permute-start.20
  71.9 1.3 %collective-permute-start.16 = (bf16[256,128]{1,0:T(8,128)(2,1)S(1)}, bf16[256,128]{1,0:T(8,128)(2,1)S(1)}, u32[]{:S(2)}, u32[]{:S(2)}) collective-permute-start(bf16[256,128]{1,0:T(8,128)(2,1)S(1)} %get-tuple-element.87), channel_id=1, source_target_pairs={{24,0},{28,4},{25,1},{29,5},{26,2},{30,6},{27,3},{31,7}} | collective-permute-start | bytes 196616 | tf_op jit(solution)/shard_map/ppermute | solution.py:433
  73.2 1.3 %collective-permute-start.17 = (bf16[256,128]{1,0:T(8,128)(2,1)S(1)}, bf16[256,128]{1,0:T(8,128)(2,1)S(1)}, u32[]{:S(2)}, u32[]{:S(2)}) collective-permute-start(bf16[256,128]{1,0:T(8,128)(2,1)S(1)} %get-tuple-element.88), channel_id=1, source_target_pairs={{20,0},{24,4},{28,8},{21,1},{25,5},{29,9},{22,2},{26,6},{30,10},{2... | collective-permute-start | bytes 196616 | tf_op jit(solution)/shard_map/ppermute | solution.py:433
  74.5 1.3 %collective-permute-start.18 = (bf16[256,128]{1,0:T(8,128)(2,1)S(1)}, bf16[256,128]{1,0:T(8,128)(2,1)S(1)}, u32[]{:S(2)}, u32[]{:S(2)}) collective-permute-start(bf16[256,128]{1,0:T(8,128)(2,1)S(1)} %get-tuple-element.89), channel_id=1, source_target_pairs={{16,0},{20,4},{24,8},{28,12},{17,1},{21,5},{25,9},{29,13},{18,2},{... | collective-permute-start | bytes 196616 | tf_op jit(solution)/shard_map/ppermute | solution.py:433
  75.8 1.3 %collective-permute-start.19 = (bf16[256,128]{1,0:T(8,128)(2,1)S(1)}, bf16[256,128]{1,0:T(8,128)(2,1)S(1)}, u32[]{:S(2)}, u32[]{:S(2)}) collective-permute-start(bf16[256,128]{1,0:T(8,128)(2,1)S(1)} %get-tuple-element.90), channel_id=1, source_target_pairs={{12,0},{16,4},{20,8},{24,12},{28,16},{13,1},{17,5},{21,9},{25,13},... | collective-permute-start | bytes 196616 | tf_op jit(solution)/shard_map/ppermute | solution.py:433
  77.1 0.8 own_sum.1
  77.9 0.6 collective-permute-start.21
  78.5 1.7 %collective-permute-done.16.refs_0_ = bf16[256,128]{1,0:T(8,128)(2,1)S(1)} collective-permute-done((bf16[256,128]{1,0:T(8,128)(2,1)S(1)}, bf16[256,128]{1,0:T(8,128)(2,1)S(1)}, u32[]{:S(2)}, u32[]{:S(2)}) %collective-permute-start.16) | collective-permute-done | bytes 65568 | tf_op jit(solution)/shard_map/ppermute | solution.py:433
  80.2 3.2 %collective-permute-done.17.refs_1_ = bf16[256,128]{1,0:T(8,128)(2,1)S(1)} collective-permute-done((bf16[256,128]{1,0:T(8,128)(2,1)S(1)}, bf16[256,128]{1,0:T(8,128)(2,1)S(1)}, u32[]{:S(2)}, u32[]{:S(2)}) %collective-permute-start.17) | collective-permute-done | bytes 65568 | tf_op jit(solution)/shard_map/ppermute | solution.py:433
  83.4 2.3 %collective-permute-done.18.refs_2_ = bf16[256,128]{1,0:T(8,128)(2,1)S(1)} collective-permute-done((bf16[256,128]{1,0:T(8,128)(2,1)S(1)}, bf16[256,128]{1,0:T(8,128)(2,1)S(1)}, u32[]{:S(2)}, u32[]{:S(2)}) %collective-permute-start.18) | collective-permute-done | bytes 65568 | tf_op jit(solution)/shard_map/ppermute | solution.py:433
  85.7 0.1 collective-permute-done.19.refs_3_
  85.8 0.6 far_returns.1.returned
  86.4 0.2 collective-permute-done.21.refs_0_
  86.7 0.1 owner_sum.1.refs_0_
  86.8 0.6 collective-permute-start.22
  87.4 0.0 collective-permute-start.23
  87.4 4.5 %query_grads.1 = bf16[2048,128]{1,0:T(8,128)(2,1)} custom-call(s32[4,3]{1,0:T(4,128)S(1)} %copy-done.5, bf16[4,512,128]{2,1,0:T(8,128)(2,1)S(1)} %bitcast.18, bf16[2,7,512,128]{3,2,1,0:T(8,128)(2,1)S(1)} %get-tuple-element.100.rows, bf16[12,512,512]{2,1,0:T(8,128)(2,1)S(1)} %get-tuple-element.101.ds_far, bf16[16,512,512]{2,1,0:T(8,128)(2,1)S(1)} %get-tuple-element.102.ds_own), custom_call_target="tpu_custom_call" | custom-call | flops 2013265920 | bytes 4194304 | tf_op jit(solution)/shard_map/query_grads/pallas_call | solution.py:573
  91.8 3.0 %collective-permute-done.22.refs_2_ = bf16[4,256,128]{2,1,0:T(8,128)(2,1)S(1)} collective-permute-done((bf16[4,256,128]{2,1,0:T(8,128)(2,1)S(1)}, bf16[4,256,128]{2,1,0:T(8,128)(2,1)S(1)}, u32[]{:S(2)}, u32[]{:S(2)}) %collective-permute-start.22) | collective-permute-done | bytes 262176 | tf_op jit(solution)/shard_map/ppermute | solution.py:430
  94.8 0.0 collective-permute-start.24
  94.8 0.0 collective-permute-done.23.refs_1_
  94.8 1.5 %collective-permute-done.24.refs_3_ = bf16[4,256,128]{2,1,0:T(8,128)(2,1)S(1)} collective-permute-done((bf16[4,256,128]{2,1,0:T(8,128)(2,1)S(1)}, bf16[4,256,128]{2,1,0:T(8,128)(2,1)S(1)}, u32[]{:S(2)}, u32[]{:S(2)}) %collective-permute-start.24) | collective-permute-done | bytes 262176 | tf_op jit(solution)/shard_map/ppermute | solution.py:427
  96.3 1.0 %spread.1 = (bf16[4,512,128]{2,1,0:T(8,128)(2,1)}, bf16[4,512,128]{2,1,0:T(8,128)(2,1)}) custom-call(bf16[4,256,128]{2,1,0:T(8,128)(2,1)S(1)} %owner_sum.1.refs_0_, bf16[4,256,128]{2,1,0:T(8,128)(2,1)S(1)} %collective-permute-done.23.refs_1_, bf16[4,256,128]{2,1,0:T(8,128)(2,1)S(1)} %collective-permute-done.22.refs_2_, ...), custom_call_target="tpu_custom_call" | custom-call | tf_op jit(solution)/shard_map/spread/pallas_call | solution.py:589
  (24 shorter events, 0.2 us)
Async XLA Ops:
  17.8 10.0 %collective-permute-start = (bf16[256,128]{1,0:T(8,128)(2,1)}, bf16[256,128]{1,0:T(8,128)(2,1)S(1)}, u32[]{:S(2)}, u32[]{:S(2)}) collective-permute-start(bf16[256,128]{1,0:T(8,128)(2,1)} %get-tuple-element.56), channel_id=1, source_target_pairs={{0,24},{4,28},{1,25},{5,29},{2,26},{6,30},{3,27},{7,31}} | collective-permute-start | bytes 196616 | tf_op jit(solution)/shard_map/ppermute | solution.py:436
  20.5 9.8 %collective-permute-start.1 = (bf16[256,128]{1,0:T(8,128)(2,1)}, bf16[256,128]{1,0:T(8,128)(2,1)S(1)}, u32[]{:S(2)}, u32[]{:S(2)}) collective-permute-start(bf16[256,128]{1,0:T(8,128)(2,1)} %get-tuple-element.57), channel_id=1, source_target_pairs={{0,20},{4,24},{8,28},{1,21},{5,25},{9,29},{2,22},{6,26},{10,30},{3... | collective-permute-start | bytes 196616 | tf_op jit(solution)/shard_map/ppermute | solution.py:436
  21.8 11.4 %collective-permute-start.2 = (bf16[256,128]{1,0:T(8,128)(2,1)}, bf16[256,128]{1,0:T(8,128)(2,1)S(1)}, u32[]{:S(2)}, u32[]{:S(2)}) collective-permute-start(bf16[256,128]{1,0:T(8,128)(2,1)} %get-tuple-element.58), channel_id=1, source_target_pairs={{0,16},{4,20},{8,24},{12,28},{1,17},{5,21},{9,25},{13,29},{2,18},{... | collective-permute-start | bytes 196616 | tf_op jit(solution)/shard_map/ppermute | solution.py:436
  23.1 10.1 %collective-permute-start.3 = (bf16[256,128]{1,0:T(8,128)(2,1)}, bf16[256,128]{1,0:T(8,128)(2,1)S(1)}, u32[]{:S(2)}, u32[]{:S(2)}) collective-permute-start(bf16[256,128]{1,0:T(8,128)(2,1)} %get-tuple-element.59), channel_id=1, source_target_pairs={{0,12},{4,16},{8,20},{12,24},{16,28},{1,13},{5,17},{9,21},{13,25},... | collective-permute-start | bytes 196616 | tf_op jit(solution)/shard_map/ppermute | solution.py:436
  25.6 19.8 %collective-permute-start.4 = (bf16[512,128]{1,0:T(8,128)(2,1)}, bf16[512,128]{1,0:T(8,128)(2,1)S(1)}, u32[]{:S(2)}, u32[]{:S(2)}) collective-permute-start(bf16[512,128]{1,0:T(8,128)(2,1)} %get-tuple-element.61), channel_id=1, source_target_pairs={{0,4},{4,8},{8,12},{12,16},{16,20},{20,24},{24,28},{1,5},{5,9},{9,... | collective-permute-start | bytes 393224 | tf_op jit(solution)/shard_map/ppermute | solution.py:436
  27.8 17.6 %collective-permute-start.5 = (bf16[512,128]{1,0:T(8,128)(2,1)}, bf16[512,128]{1,0:T(8,128)(2,1)S(1)}, u32[]{:S(2)}, u32[]{:S(2)}) collective-permute-start(bf16[512,128]{1,0:T(8,128)(2,1)} %get-tuple-element.62), channel_id=1, source_target_pairs={{0,8},{4,12},{8,16},{12,20},{16,24},{20,28},{1,9},{5,13},{9,17},{1... | collective-permute-start | bytes 393224 | tf_op jit(solution)/shard_map/ppermute | solution.py:436
  30.2 15.2 %collective-permute-start.6 = (bf16[512,128]{1,0:T(8,128)(2,1)}, bf16[512,128]{1,0:T(8,128)(2,1)S(1)}, u32[]{:S(2)}, u32[]{:S(2)}) collective-permute-start(bf16[512,128]{1,0:T(8,128)(2,1)} %get-tuple-element.63), channel_id=1, source_target_pairs={{0,28},{1,29},{2,30},{3,31}} | collective-permute-start | bytes 393224 | tf_op jit(solution)/shard_map/ppermute | solution.py:436
  33.2 12.8 %collective-permute-start.9 = (bf16[4,256,128]{2,1,0:T(8,128)(2,1)S(1)}, bf16[4,256,128]{2,1,0:T(8,128)(2,1)S(1)}, u32[]{:S(2)}, u32[]{:S(2)}) collective-permute-start(bf16[4,256,128]{2,1,0:T(8,128)(2,1)S(1)} %pad_maximum_fusion.1.refs_2_), channel_id=1, source_target_pairs={{0,2},{1,3},{2,0},{3,1},{4,6},{5,7},{6,4},{7,5},{8,10},{9,11},{10,... | collective-permute-start | bytes 786440 | tf_op jit(solution)/shard_map/ppermute | solution.py:430
  34.8 1.0 %copy-start = (bf16[2048,128]{1,0:T(8,128)(2,1)S(1)}, bf16[2048,128]{1,0:T(8,128)(2,1)}, u32[]{:S(2)}) copy-start(bf16[2048,128]{1,0:T(8,128)(2,1)} %param.6) | copy-start | bytes 1572868
  35.8 1.0 %copy-start.2 = (bf16[2048,128]{1,0:T(8,128)(2,1)S(1)}, bf16[2048,128]{1,0:T(8,128)(2,1)}, u32[]{:S(2)}) copy-start(bf16[2048,128]{1,0:T(8,128)(2,1)} %param.7) | copy-start | bytes 1572868
  36.9 0.7 copy-start.4
  37.6 1.0 %copy-start.7 = (bf16[2048,1,128]{2,0,1:T(8,128)(2,1)S(1)}, bf16[2048,1,128]{2,0,1:T(8,128)(2,1)}, u32[]{:S(2)}) copy-start(bf16[2048,1,128]{2,0,1:T(8,128)(2,1)} %param.5) | copy-start | bytes 1572868
  38.6 1.0 %copy-start.9 = (bf16[2048,1,128]{2,0,1:T(8,128)(2,1)S(1)}, bf16[2048,1,128]{2,0,1:T(8,128)(2,1)}, u32[]{:S(2)}) copy-start(bf16[2048,1,128]{2,0,1:T(8,128)(2,1)} %param.8) | copy-start | bytes 1572868
  39.6 8.4 %copy-start.5 = (s32[4,3]{1,0:T(4,128)S(1)}, s32[4,3]{1,0:T(4,128)}, u32[]{:S(2)}) copy-start(s32[4,3]{1,0:T(4,128)} %chosen.3) | copy-start | bytes 148
  39.6 8.4 %copy-start.8 = (bf16[2048,1,128]{2,0,1:T(8,128)(2,1)S(1)}, bf16[2048,1,128]{2,0,1:T(8,128)(2,1)}, u32[]{:S(2)}) copy-start(bf16[2048,1,128]{2,0,1:T(8,128)(2,1)} %param.5) | copy-start | bytes 1572868
  39.6 8.4 %copy-start.10 = (bf16[2048,1,128]{2,0,1:T(8,128)(2,1)S(1)}, bf16[2048,1,128]{2,0,1:T(8,128)(2,1)}, u32[]{:S(2)}) copy-start(bf16[2048,1,128]{2,0,1:T(8,128)(2,1)} %param.8) | copy-start | bytes 1572868
  45.5 11.4 %copy-start.1 = (bf16[2048,128]{1,0:T(8,128)(2,1)S(1)}, bf16[2048,128]{1,0:T(8,128)(2,1)}, u32[]{:S(2)}) copy-start(bf16[2048,128]{1,0:T(8,128)(2,1)} %param.6) | copy-start | bytes 1572868
  45.5 11.4 %copy-start.3 = (bf16[2048,128]{1,0:T(8,128)(2,1)S(1)}, bf16[2048,128]{1,0:T(8,128)(2,1)}, u32[]{:S(2)}) copy-start(bf16[2048,128]{1,0:T(8,128)(2,1)} %param.7) | copy-start | bytes 1572868
  45.5 2.2 %collective-permute-start.7 = (bf16[3,512,128]{2,1,0:T(8,128)(2,1)S(1)}, bf16[3,512,128]{2,1,0:T(8,128)(2,1)S(1)}, u32[]{:S(2)}, u32[]{:S(2)}) collective-permute-start(bf16[3,512,128]{2,1,0:T(8,128)(2,1)S(1)} %pad_maximum_fusion.refs_0_), channel_id=1, source_target_pairs={{0,1},{1,0},{2,3},{3,2},{4,5},{5,4},{6,7},{7,6},{8,9},{9,8},{10,11... | collective-permute-start | bytes 1179656 | tf_op jit(solution)/shard_map/ppermute | solution.py:427
  45.6 2.1 %collective-permute-start.8 = (bf16[4,256,128]{2,1,0:T(8,128)(2,1)S(1)}, bf16[4,256,128]{2,1,0:T(8,128)(2,1)S(1)}, u32[]{:S(2)}, u32[]{:S(2)}) collective-permute-start(bf16[4,256,128]{2,1,0:T(8,128)(2,1)S(1)} %pad_maximum_fusion.1.refs_2_), channel_id=1, source_target_pairs={{0,1},{1,0},{2,3},{3,2},{4,5},{5,4},{6,7},{7,6},{8,9},{9,8},{10,11... | collective-permute-start | bytes 786440 | tf_op jit(solution)/shard_map/ppermute | solution.py:427
  46.1 2.0 %collective-permute-start.10 = (bf16[4,256,128]{2,1,0:T(8,128)(2,1)S(1)}, bf16[4,256,128]{2,1,0:T(8,128)(2,1)S(1)}, u32[]{:S(2)}, u32[]{:S(2)}) collective-permute-start(bf16[4,256,128]{2,1,0:T(8,128)(2,1)S(1)} %collective-permute-done.9.refs_4_), channel_id=1, source_target_pairs={{0,1},{1,0},{2,3},{3,2},{4,5},{5,4},{6,7},{7,6},{8,9},{9,8},{10,11... | collective-permute-start | bytes 786440 | tf_op jit(solution)/shard_map/ppermute | solution.py:427
  49.6 2.5 %collective-permute-start.11 = (bf16[7,512,128]{2,1,0:T(8,128)(2,1)S(1)}, bf16[7,512,128]{2,1,0:T(8,128)(2,1)S(1)}, u32[]{:S(2)}, u32[]{:S(2)}) collective-permute-start(bf16[7,512,128]{2,1,0:T(8,128)(2,1)S(1)} %get-tuple-element.71), channel_id=1, source_target_pairs={{0,1},{1,0},{2,3},{3,2},{4,5},{5,4},{6,7},{7,6},{8,9},{9,8},{10,11... | collective-permute-start | bytes 2752520 | tf_op jit(solution)/shard_map/ppermute | solution.py:427
  52.3 24.8 %copy-start.6 = (s32[7]{0:T(128)S(1)}, s32[7]{0:T(128)}, u32[]{:S(2)}) copy-start(s32[7]{0:T(128)} %get-tuple-element.55.asked) | copy-start | bytes 88
  52.4 12.3 %collective-permute-start.13 = (bf16[512,128]{1,0:T(8,128)(2,1)S(1)}, bf16[512,128]{1,0:T(8,128)(2,1)S(1)}, u32[]{:S(2)}, u32[]{:S(2)}) collective-permute-start(bf16[512,128]{1,0:T(8,128)(2,1)S(1)} %get-tuple-element.80), channel_id=1, source_target_pairs={{4,0},{8,4},{12,8},{16,12},{20,16},{24,20},{28,24},{5,1},{9,5},{13... | collective-permute-start | bytes 393224 | tf_op jit(solution)/shard_map/ppermute | solution.py:433
  53.7 11.0 %collective-permute-start.14 = (bf16[512,128]{1,0:T(8,128)(2,1)S(1)}, bf16[512,128]{1,0:T(8,128)(2,1)S(1)}, u32[]{:S(2)}, u32[]{:S(2)}) collective-permute-start(bf16[512,128]{1,0:T(8,128)(2,1)S(1)} %get-tuple-element.81), channel_id=1, source_target_pairs={{8,0},{12,4},{16,8},{20,12},{24,16},{28,20},{9,1},{13,5},{17,9},{2... | collective-permute-start | bytes 393224 | tf_op jit(solution)/shard_map/ppermute | solution.py:433
  55.0 16.9 %collective-permute-start.15 = (bf16[512,128]{1,0:T(8,128)(2,1)S(1)}, bf16[512,128]{1,0:T(8,128)(2,1)S(1)}, u32[]{:S(2)}, u32[]{:S(2)}) collective-permute-start(bf16[512,128]{1,0:T(8,128)(2,1)S(1)} %get-tuple-element.82), channel_id=1, source_target_pairs={{28,0},{29,1},{30,2},{31,3}} | collective-permute-start | bytes 393224 | tf_op jit(solution)/shard_map/ppermute | solution.py:433
  56.3 15.6 %collective-permute-start.12 = (bf16[4,256,128]{2,1,0:T(8,128)(2,1)S(1)}, bf16[4,256,128]{2,1,0:T(8,128)(2,1)S(1)}, u32[]{:S(2)}, u32[]{:S(2)}) collective-permute-start(bf16[4,256,128]{2,1,0:T(8,128)(2,1)S(1)} %get-tuple-element.79), channel_id=1, source_target_pairs={{0,2},{1,3},{2,0},{3,1},{4,6},{5,7},{6,4},{7,5},{8,10},{9,11},{10,... | collective-permute-start | bytes 786440 | tf_op jit(solution)/shard_map/ppermute | solution.py:430
  71.8 5.3 %collective-permute-start.20 = (bf16[4,512,128]{2,1,0:T(8,128)(2,1)S(1)}, bf16[4,512,128]{2,1,0:T(8,128)(2,1)S(1)}, u32[]{:S(2)}, u32[]{:S(2)}) collective-permute-start(bf16[4,512,128]{2,1,0:T(8,128)(2,1)S(1)} %get-tuple-element.92), channel_id=1, source_target_pairs={{0,1},{1,0},{2,3},{3,2},{4,5},{5,4},{6,7},{7,6},{8,9},{9,8},{10,11... | collective-permute-start | bytes 1572872 | tf_op jit(solution)/shard_map/ppermute | solution.py:427
  71.9 8.3 %collective-permute-start.16 = (bf16[256,128]{1,0:T(8,128)(2,1)S(1)}, bf16[256,128]{1,0:T(8,128)(2,1)S(1)}, u32[]{:S(2)}, u32[]{:S(2)}) collective-permute-start(bf16[256,128]{1,0:T(8,128)(2,1)S(1)} %get-tuple-element.87), channel_id=1, source_target_pairs={{24,0},{28,4},{25,1},{29,5},{26,2},{30,6},{27,3},{31,7}} | collective-permute-start | bytes 196616 | tf_op jit(solution)/shard_map/ppermute | solution.py:433
  73.2 10.2 %collective-permute-start.17 = (bf16[256,128]{1,0:T(8,128)(2,1)S(1)}, bf16[256,128]{1,0:T(8,128)(2,1)S(1)}, u32[]{:S(2)}, u32[]{:S(2)}) collective-permute-start(bf16[256,128]{1,0:T(8,128)(2,1)S(1)} %get-tuple-element.88), channel_id=1, source_target_pairs={{20,0},{24,4},{28,8},{21,1},{25,5},{29,9},{22,2},{26,6},{30,10},{2... | collective-permute-start | bytes 196616 | tf_op jit(solution)/shard_map/ppermute | solution.py:433
  74.5 11.3 %collective-permute-start.18 = (bf16[256,128]{1,0:T(8,128)(2,1)S(1)}, bf16[256,128]{1,0:T(8,128)(2,1)S(1)}, u32[]{:S(2)}, u32[]{:S(2)}) collective-permute-start(bf16[256,128]{1,0:T(8,128)(2,1)S(1)} %get-tuple-element.89), channel_id=1, source_target_pairs={{16,0},{20,4},{24,8},{28,12},{17,1},{21,5},{25,9},{29,13},{18,2},{... | collective-permute-start | bytes 196616 | tf_op jit(solution)/shard_map/ppermute | solution.py:433
  75.8 10.0 %collective-permute-start.19 = (bf16[256,128]{1,0:T(8,128)(2,1)S(1)}, bf16[256,128]{1,0:T(8,128)(2,1)S(1)}, u32[]{:S(2)}, u32[]{:S(2)}) collective-permute-start(bf16[256,128]{1,0:T(8,128)(2,1)S(1)} %get-tuple-element.90), channel_id=1, source_target_pairs={{12,0},{16,4},{20,8},{24,12},{28,16},{13,1},{17,5},{21,9},{25,13},... | collective-permute-start | bytes 196616 | tf_op jit(solution)/shard_map/ppermute | solution.py:433
  77.9 8.8 %collective-permute-start.21 = (bf16[4,256,128]{2,1,0:T(8,128)(2,1)S(1)}, bf16[4,256,128]{2,1,0:T(8,128)(2,1)S(1)}, u32[]{:S(2)}, u32[]{:S(2)}) collective-permute-start(bf16[4,256,128]{2,1,0:T(8,128)(2,1)S(1)} %get-tuple-element.97), channel_id=1, source_target_pairs={{0,2},{1,3},{2,0},{3,1},{4,6},{5,7},{6,4},{7,5},{8,10},{9,11},{10,... | collective-permute-start | bytes 786440 | tf_op jit(solution)/shard_map/ppermute | solution.py:430
  86.8 8.0 %collective-permute-start.22 = (bf16[4,256,128]{2,1,0:T(8,128)(2,1)S(1)}, bf16[4,256,128]{2,1,0:T(8,128)(2,1)S(1)}, u32[]{:S(2)}, u32[]{:S(2)}) collective-permute-start(bf16[4,256,128]{2,1,0:T(8,128)(2,1)S(1)} %owner_sum.1.refs_0_), channel_id=1, source_target_pairs={{0,2},{1,3},{2,0},{3,1},{4,6},{5,7},{6,4},{7,5},{8,10},{9,11},{10,... | collective-permute-start | bytes 786440 | tf_op jit(solution)/shard_map/ppermute | solution.py:430
  87.4 7.4 %collective-permute-start.23 = (bf16[4,256,128]{2,1,0:T(8,128)(2,1)S(1)}, bf16[4,256,128]{2,1,0:T(8,128)(2,1)S(1)}, u32[]{:S(2)}, u32[]{:S(2)}) collective-permute-start(bf16[4,256,128]{2,1,0:T(8,128)(2,1)S(1)} %owner_sum.1.refs_0_), channel_id=1, source_target_pairs={{0,1},{1,0},{2,3},{3,2},{4,5},{5,4},{6,7},{7,6},{8,9},{9,8},{10,11... | collective-permute-start | bytes 786440 | tf_op jit(solution)/shard_map/ppermute | solution.py:427
  94.8 1.5 %collective-permute-start.24 = (bf16[4,256,128]{2,1,0:T(8,128)(2,1)S(1)}, bf16[4,256,128]{2,1,0:T(8,128)(2,1)S(1)}, u32[]{:S(2)}, u32[]{:S(2)}) collective-permute-start(bf16[4,256,128]{2,1,0:T(8,128)(2,1)S(1)} %collective-permute-done.22.refs_2_), channel_id=1, source_target_pairs={{0,1},{1,0},{2,3},{3,2},{4,5},{5,4},{6,7},{7,6},{8,9},{9,8},{10,11... | collective-permute-start | bytes 786440 | tf_op jit(solution)/shard_map/ppermute | solution.py:427

commit v6 on v5

--- a/solution.py
+++ b/solution.py
@@ -177,7 +177,7 @@
     factor, scaling, blocks_here, chips, far, near, piece, chosen, q, do, stats, *refs
 ):
     near_refs, far_refs, refs = refs[:2], refs[2 : 2 + 2 * chips], refs[2 + 2 * chips :]
-    keep, send, final, ds_far, rows, acc, s_buf, dp_buf, parts = refs
+    keep, send, final, grad_qt, rows, acc, s_buf, dp_buf, parts = refs
     place = lax.axis_index("head")
     core, chip = lax.rem(place, 2), lax.div(place, 2)
     block_len = rows.shape[2]
@@ -234,6 +234,7 @@
             weighted = weighted + scale * parts[t, 2:3, :]
         final[row, 0:1, :] = top + jnp.log2(total)
         final[row, 1:2, :] = weighted / total
+        grad_qt[row] = jnp.zeros_like(grad_qt[row])
         for t in range(3):
             slot = slot_of(chosen, blocks_here, row, t) - blocks_here
 
@@ -245,7 +246,7 @@
                 dscores = (weights * (dp_buf[t] - delta)).astype(BF16)
                 acc[1, slot] += dot_nn(weights.astype(BF16), do[span, :])
                 acc[0, slot] += dot_nn(dscores, q[span, :])
-                ds_far[row * 3 + t] = dscores
+                grad_qt[row] += dot_nn(rows[0, slot].T, dscores)
 
         return 0
 
@@ -312,21 +313,17 @@
     send[...] = (acc[1 - core] * send_scale).astype(BF16)
 
 
-def query_kernel(scaling, blocks_here, chosen, keys, rows, ds_far, ds_own, grad_q, total_qt):
+def query_kernel(scaling, blocks_here, chosen, keys, grad_qt, ds_own, grad_q, total_qt):
     block_len = keys.shape[1]
 
     def per_row(row, _):
-        total_qt[...] = dot_nn(keys[row].T, ds_own[row * 4 + 3])
+        total_qt[...] = grad_qt[row] + dot_nn(keys[row].T, ds_own[row * 4 + 3])
         for t in range(3):
             slot = slot_of(chosen, blocks_here, row, t)
 
             @pl.when((slot >= 0) & (slot < blocks_here))
             def _():
                 total_qt[...] += dot_nn(keys[slot].T, ds_own[row * 4 + t])
-
-            @pl.when(slot >= blocks_here)
-            def _():
-                total_qt[...] += dot_nn(rows[0, slot - blocks_here].T, ds_far[row * 3 + t])
 
         span = pl.ds(row * block_len, block_len)
         grad_q[span, :] = (total_qt[...].T * scaling).astype(BF16)
@@ -409,8 +406,7 @@
     own_type = jax.ShapeDtypeStruct(local_shape, BF16)
     block_type = jax.ShapeDtypeStruct((block_len, feature), BF16)
     piece_type = jax.ShapeDtypeStruct((piece, feature), BF16)
-    square = (block_len, block_len)
-    ds_bytes = block_len * block_len * 2
+    qt_type = jax.ShapeDtypeStruct((blocks_here, feature, block_len), F32)
     pair_flops = 2 * block_len * block_len * feature
     block_bytes = block_len * feature * 2
     pair_bytes = block_len * block_len * 4
@@ -469,30 +465,21 @@
     for part in far_more:
         row_sets += [part, swap(part)]
 
-    keep_far, send_far, final, ds_far, far_rows = pl.pallas_call(
+    keep_far, send_far, final, grad_qt = pl.pallas_call(
         functools.partial(
             remote_kernel, factor, scaling, blocks_here, chips, far, near, piece
         ),
         in_specs=[smem] + [whole] * (3 + len(row_sets)),
-        out_specs=[whole] * 5,
-        out_shape=[
-            far_type,
-            far_type,
-            stat_type,
-            jax.ShapeDtypeStruct((3 * blocks_here,) + square, BF16),
-            jax.ShapeDtypeStruct((2,) + remote_shape, BF16),
-        ],
+        out_specs=[whole] * 4,
+        out_shape=[far_type, far_type, stat_type, qt_type],
         scratch_shapes=[
+            pltpu.VMEM((2,) + remote_shape, BF16),
             pltpu.VMEM((2,) + remote_shape, F32),
             pltpu.VMEM((3, block_len, block_len), F32),
             pltpu.VMEM((3, block_len, block_len), F32),
             pltpu.VMEM((4, 8, block_len), F32),
         ],
-        compiler_params=params(
-            (10 * shifts + 4 * blocks_here) * block_bytes
-            + 6 * pair_bytes
-            + 3 * blocks_here * ds_bytes
-        ),
+        compiler_params=params((10 * shifts + 4 * blocks_here) * block_bytes + 6 * pair_bytes),
         cost_estimate=cost(60, 8 * tok_rows * feature * 2),
         name="remote_pairs",
     )(chosen, q2, do2, stats, *row_sets)
@@ -521,6 +508,8 @@
     far_sums, near_sums = chip_far[:chips], chip_far[chips:]
     far_parts = [to_chip(far_sums[d], d) for d in range(1, chips)]
     near_back = [to_owner(near_sums[i], s) for i, s in enumerate(near)]
+    square = (block_len, block_len)
+    ds_bytes = block_len * block_len * 2
     keep_own, send_own, ds_own = pl.pallas_call(
         functools.partial(local_kernel, factor, scaling, blocks_here),
         in_specs=[smem] + [whole] * 5,
@@ -572,16 +561,14 @@
     gathered = [to_chip(mine, d) for d in range(1, chips)]
     grad_q = pl.pallas_call(
         functools.partial(query_kernel, scaling, blocks_here),
-        in_specs=[smem] + [whole] * 4,
+        in_specs=[smem] + [whole] * 3,
         out_specs=whole,
         out_shape=jax.ShapeDtypeStruct((tok_rows, feature), BF16),
         scratch_shapes=[pltpu.VMEM((feature, block_len), F32)],
-        compiler_params=params(
-            (3 * blocks_here + 2 * shifts) * block_bytes + 7 * blocks_here * ds_bytes
-        ),
+        compiler_params=params(5 * blocks_here * block_bytes + 4 * blocks_here * ds_bytes),
         cost_estimate=cost(30, 8 * tok_rows * feature * 2),
         name="query_grads",
-    )(chosen, key_blocks, far_rows, ds_far, ds_own)
+    )(chosen, key_blocks, grad_qt, ds_own)
     gathered, grad_q = lax.optimization_barrier((gathered, grad_q))
     spread = [mine, swap(mine)]
     for part in gathered:

time: 98.3 us -> 98.4 us (level)
  transfers between devices with their start and end apart: 25 -> 25, of which waited for: 11 -> 12; matrix products, arithmetic and copies ran while one was open for 0% -> 0% of each run, Pallas kernels for 20% -> 20%
where the time goes in v6:
time: 98.4 us; the launch traced here: 97.3 us
  starting transfers between devices  28.6 us (29%)
  Pallas kernels  25.3 us (26%)
  waiting for transfers between devices  23.2 us (24%)
  blocking collectives  13.5 us (14%)
  local copies, waits for them, and re-layouts  5.64 us (6%)
    ppermute x7, starting transfers between devices, to_reader(): lax.ppermute(array, 'ctx', [(c - s - 1, c) for c in range(s + 1, ctx_coun...  15.3 us
    ppermute x7, waiting for transfers between devices, to_owner(): lax.ppermute(array, 'ctx', [(c, c - s - 1) for c in range(s + 1, ctx_coun...  14.3 us
    all_to_all x1, blocking collectives, body(): lax.all_to_all(jnp.broadcast_to(selected.reshape(1, 3 * blocks_here), (ct...  13.5 us
    ppermute x7, starting transfers between devices, to_owner(): lax.ppermute(array, 'ctx', [(c, c - s - 1) for c in range(s + 1, ctx_coun...  9.04 us
    pallas_call x1, Pallas kernels, body(): pl.pallas_call(functools.partial(local_kernel, factor, scaling, blocks_he...  7.76 us
    ppermute x7, waiting for transfers between devices, swap(): return lax.ppermute(array, 'head', [(h, h ^ 1) for h in range(heads)])  5.76 us
    pallas_call x1, Pallas kernels, body(): pl.pallas_call(functools.partial(local_stats_kernel, factor, blocks_here)...  5.72 us
    unnamed x22, local copies, waits for them, and re-layouts  4.87 us
  transfers between devices with their start and end apart: 25, of which 12 were waited for; matrix products, arithmetic and copies ran while one was open for 0% of the time, Pallas kernels for 20%

profile of v6, /device:TPU:0, one launch (start us, length us, event | category | flops | bytes accessed | tf_op | source)
XLA Modules:
  0.0 97.3 jit_solution(1759817027338613471)
XLA Ops:
  0.6 0.8 broadcast_in_dim.7
  1.4 13.5 %all_to_all.8 = s32[8,1,12]{2,1,0:T(1,128)} all-to-all(s32[8,1,12]{2,1,0:T(1,128)S(1)} %broadcast_in_dim.8), channel_id=1, replica_groups=mesh['ctx'=8,'head'=4] {'ctx'}, dimensions={0} | all-to-all | bytes 768 | tf_op jit(solution)/shard_map/all_to_all | solution.py:434
  14.9 3.0 %pick_rows.1 = (s32[7]{0:T(128)}, bf16[512,128]{1,0:T(8,128)(2,1)}, bf16[512,128]{1,0:T(8,128)(2,1)}, bf16[256,128]{1,0:T(8,128)(2,1)}, bf16[256,128]{1,0:T(8,12...) custom-call(s32[8,12]{1,0:T(8,128)} %bitcast.35, ...), custom_call_target="tpu_custom_call" | custom-call | tf_op jit(solution)/shard_map/pick_rows/pallas_call | solution.py:438
  17.9 2.7 %collective-permute-start = (bf16[256,128]{1,0:T(8,128)(2,1)}, bf16[256,128]{1,0:T(8,128)(2,1)S(1)}, u32[]{:S(2)}, u32[]{:S(2)}) collective-permute-start(bf16[256,128]{1,0:T(8,128)(2,1)} %get-tuple-element.55), channel_id=1, source_target_pairs={{0,24},{4,28},{1,25},{5,29},{2,26},{6,30},{3,27},{7,31}} | collective-permute-start | bytes 196616 | tf_op jit(solution)/shard_map/ppermute | solution.py:432
  20.6 1.3 %collective-permute-start.1 = (bf16[256,128]{1,0:T(8,128)(2,1)}, bf16[256,128]{1,0:T(8,128)(2,1)S(1)}, u32[]{:S(2)}, u32[]{:S(2)}) collective-permute-start(bf16[256,128]{1,0:T(8,128)(2,1)} %get-tuple-element.56), channel_id=1, source_target_pairs={{0,20},{4,24},{8,28},{1,21},{5,25},{9,29},{2,22},{6,26},{10,30},{3... | collective-permute-start | bytes 196616 | tf_op jit(solution)/shard_map/ppermute | solution.py:432
  21.9 1.3 %collective-permute-start.2 = (bf16[256,128]{1,0:T(8,128)(2,1)}, bf16[256,128]{1,0:T(8,128)(2,1)S(1)}, u32[]{:S(2)}, u32[]{:S(2)}) collective-permute-start(bf16[256,128]{1,0:T(8,128)(2,1)} %get-tuple-element.57), channel_id=1, source_target_pairs={{0,16},{4,20},{8,24},{12,28},{1,17},{5,21},{9,25},{13,29},{2,18},{... | collective-permute-start | bytes 196616 | tf_op jit(solution)/shard_map/ppermute | solution.py:432
  23.2 2.5 %collective-permute-start.3 = (bf16[256,128]{1,0:T(8,128)(2,1)}, bf16[256,128]{1,0:T(8,128)(2,1)S(1)}, u32[]{:S(2)}, u32[]{:S(2)}) collective-permute-start(bf16[256,128]{1,0:T(8,128)(2,1)} %get-tuple-element.58), channel_id=1, source_target_pairs={{0,12},{4,16},{8,20},{12,24},{16,28},{1,13},{5,17},{9,21},{13,25},... | collective-permute-start | bytes 196616 | tf_op jit(solution)/shard_map/ppermute | solution.py:432
  25.7 2.1 %collective-permute-start.4 = (bf16[512,128]{1,0:T(8,128)(2,1)}, bf16[512,128]{1,0:T(8,128)(2,1)S(1)}, u32[]{:S(2)}, u32[]{:S(2)}) collective-permute-start(bf16[512,128]{1,0:T(8,128)(2,1)} %get-tuple-element.60), channel_id=1, source_target_pairs={{0,4},{4,8},{8,12},{12,16},{16,20},{20,24},{24,28},{1,5},{5,9},{9,... | collective-permute-start | bytes 393224 | tf_op jit(solution)/shard_map/ppermute | solution.py:432
  27.9 2.5 %collective-permute-start.5 = (bf16[512,128]{1,0:T(8,128)(2,1)}, bf16[512,128]{1,0:T(8,128)(2,1)S(1)}, u32[]{:S(2)}, u32[]{:S(2)}) collective-permute-start(bf16[512,128]{1,0:T(8,128)(2,1)} %get-tuple-element.61), channel_id=1, source_target_pairs={{0,8},{4,12},{8,16},{12,20},{16,24},{20,28},{1,9},{5,13},{9,17},{1... | collective-permute-start | bytes 393224 | tf_op jit(solution)/shard_map/ppermute | solution.py:432
  30.3 2.9 %collective-permute-start.6 = (bf16[512,128]{1,0:T(8,128)(2,1)}, bf16[512,128]{1,0:T(8,128)(2,1)S(1)}, u32[]{:S(2)}, u32[]{:S(2)}) collective-permute-start(bf16[512,128]{1,0:T(8,128)(2,1)} %get-tuple-element.62), channel_id=1, source_target_pairs={{0,28},{1,29},{2,30},{3,31}} | collective-permute-start | bytes 393224 | tf_op jit(solution)/shard_map/ppermute | solution.py:432
  33.3 0.0 collective-permute-done.3
  33.3 1.6 %collective-permute-start.9 = (bf16[4,256,128]{2,1,0:T(8,128)(2,1)S(1)}, bf16[4,256,128]{2,1,0:T(8,128)(2,1)S(1)}, u32[]{:S(2)}, u32[]{:S(2)}) collective-permute-start(bf16[4,256,128]{2,1,0:T(8,128)(2,1)S(1)} %pad_maximum_fusion.1.refs_2_), channel_id=1, source_target_pairs={{0,2},{1,3},{2,0},{3,1},{4,6},{5,7},{6,4},{7,5},{8,10},{9,11},{10,... | collective-permute-start | bytes 786440 | tf_op jit(solution)/shard_map/ppermute | solution.py:426
  34.9 1.0 %copy-done = bf16[2048,128]{1,0:T(8,128)(2,1)S(1)} copy-done((bf16[2048,128]{1,0:T(8,128)(2,1)S(1)}, bf16[2048,128]{1,0:T(8,128)(2,1)}, u32[]{:S(2)}) %copy-start) | copy-done | bytes 524312
  35.9 1.0 %copy-done.2 = bf16[2048,128]{1,0:T(8,128)(2,1)S(1)} copy-done((bf16[2048,128]{1,0:T(8,128)(2,1)S(1)}, bf16[2048,128]{1,0:T(8,128)(2,1)}, u32[]{:S(2)}) %copy-start.2) | copy-done | bytes 524312
  37.0 0.7 copy-done.4
  37.7 1.0 %copy-done.7 = bf16[2048,1,128]{2,0,1:T(8,128)(2,1)S(1)} copy-done((bf16[2048,1,128]{2,0,1:T(8,128)(2,1)S(1)}, bf16[2048,1,128]{2,0,1:T(8,128)(2,1)}, u32[]{:S(2)}) %copy-start.7) | copy-done | bytes 524312
  38.7 1.0 %copy-done.9 = bf16[2048,1,128]{2,0,1:T(8,128)(2,1)S(1)} copy-done((bf16[2048,1,128]{2,0,1:T(8,128)(2,1)S(1)}, bf16[2048,1,128]{2,0,1:T(8,128)(2,1)}, u32[]{:S(2)}) %copy-start.9) | copy-done | bytes 524312
  39.7 5.7 %local_stats.1.stats = f32[4,8,512]{2,1,0:T(8,128)S(1)} custom-call(s32[4,3]{1,0:T(4,128)S(1)} %copy-done.4, bf16[2048,128]{1,0:T(8,128)(2,1)S(1)} %bitcast.22, bf16[2048,128]{1,0:T(8,128)(2,1)S(1)} %bitcast.25, bf16[4,512,128]{2,1,0:T(8,128)(2,1)S(1)} %bitcast.19, bf16[4,512,128]{2,1,0:T(8,128)(2,1)S(1)} %bitcast.16), custom_call_target="tpu_custom_call" | custom-call | flops 2013265920 | bytes 2097152 | tf_op jit(solution)/shard_map/local_stats/pallas_call | solution.py:452
  45.5 0.0 collective-permute-done.4
  45.5 0.0 collective-permute-done.5
  45.6 0.0 copy-start.1
  45.6 0.0 copy-start.3
  45.6 0.1 collective-permute-start.7
  45.7 0.5 collective-permute-start.8
  46.2 0.0 collective-permute-done.9.refs_4_
  46.2 0.1 collective-permute-start.10
  46.3 1.5 %collective-permute-done.8.refs_3_ = bf16[4,256,128]{2,1,0:T(8,128)(2,1)S(1)} collective-permute-done((bf16[4,256,128]{2,1,0:T(8,128)(2,1)S(1)}, bf16[4,256,128]{2,1,0:T(8,128)(2,1)S(1)}, u32[]{:S(2)}, u32[]{:S(2)}) %collective-permute-start.8) | collective-permute-done | bytes 262176 | tf_op jit(solution)/shard_map/ppermute | solution.py:423
  47.8 0.0 collective-permute-done.7.refs_1_
  47.8 0.4 collective-permute-done.10.refs_5_
  48.1 1.6 %remote_pairs.1 = (bf16[7,512,128]{2,1,0:T(8,128)(2,1)S(1)}, bf16[7,512,128]{2,1,0:T(8,128)(2,1)S(1)}, f32[4,8,512]{2,1,0:T(8,128)S(1)}, f32[4,128,512]{2,1,0:T(8,128)S(1)}) custom-call(s32[4,3]{1,0:T(4,128)S(1)} %copy-done.5, bf16[2048,128]{1,0:T(8,128)(2,1)S(1)} %bitcast.23, bf16[2048,128]{1,0:T(8,128)(2,1)S(1)} %bitcast.26, ...), custom_call_target="tpu_custom_call" | custom-call | flops 4026531840 | bytes 4194304 | tf_op jit(solution)/shard_map/remote_pairs/pallas_call | solution.py:468
  49.7 0.2 collective-permute-start.11
  49.9 2.3 %collective-permute-done.11.theirs = bf16[7,512,128]{2,1,0:T(8,128)(2,1)S(1)} collective-permute-done((bf16[7,512,128]{2,1,0:T(8,128)(2,1)S(1)}, bf16[7,512,128]{2,1,0:T(8,128)(2,1)S(1)}, u32[]{:S(2)}, u32[]{:S(2)}) %collective-permute-start.11) | collective-permute-done | bytes 917536 | tf_op jit(solution)/shard_map/ppermute | solution.py:423
  52.3 0.2 chip_sum.1
  52.5 1.3 %collective-permute-start.13 = (bf16[512,128]{1,0:T(8,128)(2,1)S(1)}, bf16[512,128]{1,0:T(8,128)(2,1)S(1)}, u32[]{:S(2)}, u32[]{:S(2)}) collective-permute-start(bf16[512,128]{1,0:T(8,128)(2,1)S(1)} %get-tuple-element.79), channel_id=1, source_target_pairs={{4,0},{8,4},{12,8},{16,12},{20,16},{24,20},{28,24},{5,1},{9,5},{13... | collective-permute-start | bytes 393224 | tf_op jit(solution)/shard_map/ppermute | solution.py:429
  53.8 1.3 %collective-permute-start.14 = (bf16[512,128]{1,0:T(8,128)(2,1)S(1)}, bf16[512,128]{1,0:T(8,128)(2,1)S(1)}, u32[]{:S(2)}, u32[]{:S(2)}) collective-permute-start(bf16[512,128]{1,0:T(8,128)(2,1)S(1)} %get-tuple-element.80), channel_id=1, source_target_pairs={{8,0},{12,4},{16,8},{20,12},{24,16},{28,20},{9,1},{13,5},{17,9},{2... | collective-permute-start | bytes 393224 | tf_op jit(solution)/shard_map/ppermute | solution.py:429
  55.1 1.3 %collective-permute-start.15 = (bf16[512,128]{1,0:T(8,128)(2,1)S(1)}, bf16[512,128]{1,0:T(8,128)(2,1)S(1)}, u32[]{:S(2)}, u32[]{:S(2)}) collective-permute-start(bf16[512,128]{1,0:T(8,128)(2,1)S(1)} %get-tuple-element.81), channel_id=1, source_target_pairs={{28,0},{29,1},{30,2},{31,3}} | collective-permute-start | bytes 393224 | tf_op jit(solution)/shard_map/ppermute | solution.py:429
  56.4 0.6 collective-permute-start.12
  57.0 7.8 %local_pairs.1 = (bf16[4,512,128]{2,1,0:T(8,128)(2,1)S(1)}, bf16[4,512,128]{2,1,0:T(8,128)(2,1)S(1)}, bf16[16,512,512]{2,1,0:T(8,128)(2,1)S(1)}) custom-call(s32[4,3]{1,0:T(4,128)S(1)} %copy-done.5, bf16[2048,128]{1,0:T(8,128)(2,1)S(1)} %bitcast.24, bf16[2048,128]{1,0:T(8,128)(2,1)S(1)} %bitcast.27, bf16[4,512,128]{2,1,0:T(8,128)(2,1)S(1)} %bitcast.20, ...), custom_call_target="tpu_custom_call" | custom-call | flops 4026531840 | bytes 4194304 | tf_op jit(solution)/shard_map/local_pairs/pallas_call | solution.py:513
  64.7 0.0 collective-permute-done.13.refs_0_
  64.8 0.4 collective-permute-done.14.refs_1_
  65.1 6.6 %collective-permute-done.15.refs_2_ = bf16[512,128]{1,0:T(8,128)(2,1)S(1)} collective-permute-done((bf16[512,128]{1,0:T(8,128)(2,1)S(1)}, bf16[512,128]{1,0:T(8,128)(2,1)S(1)}, u32[]{:S(2)}, u32[]{:S(2)}) %collective-permute-start.15) | collective-permute-done | bytes 131104 | tf_op jit(solution)/shard_map/ppermute | solution.py:429
  71.8 0.0 collective-permute-done.12.refs_0_
  71.8 0.0 collective-permute-start.20
  71.8 1.3 %collective-permute-start.16 = (bf16[256,128]{1,0:T(8,128)(2,1)S(1)}, bf16[256,128]{1,0:T(8,128)(2,1)S(1)}, u32[]{:S(2)}, u32[]{:S(2)}) collective-permute-start(bf16[256,128]{1,0:T(8,128)(2,1)S(1)} %get-tuple-element.86), channel_id=1, source_target_pairs={{24,0},{28,4},{25,1},{29,5},{26,2},{30,6},{27,3},{31,7}} | collective-permute-start | bytes 196616 | tf_op jit(solution)/shard_map/ppermute | solution.py:429
  73.1 1.3 %collective-permute-start.17 = (bf16[256,128]{1,0:T(8,128)(2,1)S(1)}, bf16[256,128]{1,0:T(8,128)(2,1)S(1)}, u32[]{:S(2)}, u32[]{:S(2)}) collective-permute-start(bf16[256,128]{1,0:T(8,128)(2,1)S(1)} %get-tuple-element.87), channel_id=1, source_target_pairs={{20,0},{24,4},{28,8},{21,1},{25,5},{29,9},{22,2},{26,6},{30,10},{2... | collective-permute-start | bytes 196616 | tf_op jit(solution)/shard_map/ppermute | solution.py:429
  74.4 1.3 %collective-permute-start.18 = (bf16[256,128]{1,0:T(8,128)(2,1)S(1)}, bf16[256,128]{1,0:T(8,128)(2,1)S(1)}, u32[]{:S(2)}, u32[]{:S(2)}) collective-permute-start(bf16[256,128]{1,0:T(8,128)(2,1)S(1)} %get-tuple-element.88), channel_id=1, source_target_pairs={{16,0},{20,4},{24,8},{28,12},{17,1},{21,5},{25,9},{29,13},{18,2},{... | collective-permute-start | bytes 196616 | tf_op jit(solution)/shard_map/ppermute | solution.py:429
  75.7 1.3 %collective-permute-start.19 = (bf16[256,128]{1,0:T(8,128)(2,1)S(1)}, bf16[256,128]{1,0:T(8,128)(2,1)S(1)}, u32[]{:S(2)}, u32[]{:S(2)}) collective-permute-start(bf16[256,128]{1,0:T(8,128)(2,1)S(1)} %get-tuple-element.89), channel_id=1, source_target_pairs={{12,0},{16,4},{20,8},{24,12},{28,16},{13,1},{17,5},{21,9},{25,13},... | collective-permute-start | bytes 196616 | tf_op jit(solution)/shard_map/ppermute | solution.py:429
  77.0 0.8 own_sum.1
  77.8 0.6 collective-permute-start.21
  78.4 1.7 %collective-permute-done.16.refs_0_ = bf16[256,128]{1,0:T(8,128)(2,1)S(1)} collective-permute-done((bf16[256,128]{1,0:T(8,128)(2,1)S(1)}, bf16[256,128]{1,0:T(8,128)(2,1)S(1)}, u32[]{:S(2)}, u32[]{:S(2)}) %collective-permute-start.16) | collective-permute-done | bytes 65568 | tf_op jit(solution)/shard_map/ppermute | solution.py:429
  80.1 3.2 %collective-permute-done.17.refs_1_ = bf16[256,128]{1,0:T(8,128)(2,1)S(1)} collective-permute-done((bf16[256,128]{1,0:T(8,128)(2,1)S(1)}, bf16[256,128]{1,0:T(8,128)(2,1)S(1)}, u32[]{:S(2)}, u32[]{:S(2)}) %collective-permute-start.17) | collective-permute-done | bytes 65568 | tf_op jit(solution)/shard_map/ppermute | solution.py:429
  83.3 2.3 %collective-permute-done.18.refs_2_ = bf16[256,128]{1,0:T(8,128)(2,1)S(1)} collective-permute-done((bf16[256,128]{1,0:T(8,128)(2,1)S(1)}, bf16[256,128]{1,0:T(8,128)(2,1)S(1)}, u32[]{:S(2)}, u32[]{:S(2)}) %collective-permute-start.18) | collective-permute-done | bytes 65568 | tf_op jit(solution)/shard_map/ppermute | solution.py:429
  85.7 0.1 collective-permute-done.19.refs_3_
  85.7 0.6 far_returns.1.returned
  86.4 0.2 collective-permute-done.21.refs_0_
  86.6 0.1 owner_sum.1.refs_0_
  86.7 0.6 collective-permute-start.22
  87.3 0.0 collective-permute-start.23
  87.3 4.5 %query_grads.1 = bf16[2048,128]{1,0:T(8,128)(2,1)} custom-call(s32[4,3]{1,0:T(4,128)S(1)} %copy-done.5, bf16[4,512,128]{2,1,0:T(8,128)(2,1)S(1)} %bitcast.21, f32[4,128,512]{2,1,0:T(8,128)S(1)} %get-tuple-element.99.grad_qt, bf16[16,512,512]{2,1,0:T(8,128)(2,1)S(1)} %get-tuple-element.100.ds_own), custom_call_target="tpu_custom_call" | custom-call | flops 2013265920 | bytes 4194304 | tf_op jit(solution)/shard_map/query_grads/pallas_call | solution.py:562
  91.8 2.9 %collective-permute-done.22.refs_2_ = bf16[4,256,128]{2,1,0:T(8,128)(2,1)S(1)} collective-permute-done((bf16[4,256,128]{2,1,0:T(8,128)(2,1)S(1)}, bf16[4,256,128]{2,1,0:T(8,128)(2,1)S(1)}, u32[]{:S(2)}, u32[]{:S(2)}) %collective-permute-start.22) | collective-permute-done | bytes 262176 | tf_op jit(solution)/shard_map/ppermute | solution.py:426
  94.7 0.0 collective-permute-start.24
  94.7 0.0 collective-permute-done.23.refs_1_
  94.7 1.5 %collective-permute-done.24.refs_3_ = bf16[4,256,128]{2,1,0:T(8,128)(2,1)S(1)} collective-permute-done((bf16[4,256,128]{2,1,0:T(8,128)(2,1)S(1)}, bf16[4,256,128]{2,1,0:T(8,128)(2,1)S(1)}, u32[]{:S(2)}, u32[]{:S(2)}) %collective-permute-start.24) | collective-permute-done | bytes 262176 | tf_op jit(solution)/shard_map/ppermute | solution.py:423
  96.3 1.0 %spread.1 = (bf16[4,512,128]{2,1,0:T(8,128)(2,1)}, bf16[4,512,128]{2,1,0:T(8,128)(2,1)}) custom-call(bf16[4,256,128]{2,1,0:T(8,128)(2,1)S(1)} %owner_sum.1.refs_0_, bf16[4,256,128]{2,1,0:T(8,128)(2,1)S(1)} %collective-permute-done.23.refs_1_, bf16[4,256,128]{2,1,0:T(8,128)(2,1)S(1)} %collective-permute-done.22.refs_2_, ...), custom_call_target="tpu_custom_call" | custom-call | tf_op jit(solution)/shard_map/spread/pallas_call | solution.py:576
  (24 shorter events, 0.2 us)
Async XLA Ops:
  14.9 33.2 %copy-start.5 = (s32[4,3]{1,0:T(4,128)S(1)}, s32[4,3]{1,0:T(4,128)}, u32[]{:S(2)}) copy-start(s32[4,3]{1,0:T(4,128)} %chosen.3) | copy-start | bytes 148
  14.9 33.2 %copy-start.8 = (bf16[2048,1,128]{2,0,1:T(8,128)(2,1)S(1)}, bf16[2048,1,128]{2,0,1:T(8,128)(2,1)}, u32[]{:S(2)}) copy-start(bf16[2048,1,128]{2,0,1:T(8,128)(2,1)} %param.5) | copy-start | bytes 1572868
  14.9 33.2 %copy-start.10 = (bf16[2048,1,128]{2,0,1:T(8,128)(2,1)S(1)}, bf16[2048,1,128]{2,0,1:T(8,128)(2,1)}, u32[]{:S(2)}) copy-start(bf16[2048,1,128]{2,0,1:T(8,128)(2,1)} %param.8) | copy-start | bytes 1572868
  17.9 9.9 %collective-permute-start = (bf16[256,128]{1,0:T(8,128)(2,1)}, bf16[256,128]{1,0:T(8,128)(2,1)S(1)}, u32[]{:S(2)}, u32[]{:S(2)}) collective-permute-start(bf16[256,128]{1,0:T(8,128)(2,1)} %get-tuple-element.55), channel_id=1, source_target_pairs={{0,24},{4,28},{1,25},{5,29},{2,26},{6,30},{3,27},{7,31}} | collective-permute-start | bytes 196616 | tf_op jit(solution)/shard_map/ppermute | solution.py:432
  20.6 9.8 %collective-permute-start.1 = (bf16[256,128]{1,0:T(8,128)(2,1)}, bf16[256,128]{1,0:T(8,128)(2,1)S(1)}, u32[]{:S(2)}, u32[]{:S(2)}) collective-permute-start(bf16[256,128]{1,0:T(8,128)(2,1)} %get-tuple-element.56), channel_id=1, source_target_pairs={{0,20},{4,24},{8,28},{1,21},{5,25},{9,29},{2,22},{6,26},{10,30},{3... | collective-permute-start | bytes 196616 | tf_op jit(solution)/shard_map/ppermute | solution.py:432
  21.9 11.4 %collective-permute-start.2 = (bf16[256,128]{1,0:T(8,128)(2,1)}, bf16[256,128]{1,0:T(8,128)(2,1)S(1)}, u32[]{:S(2)}, u32[]{:S(2)}) collective-permute-start(bf16[256,128]{1,0:T(8,128)(2,1)} %get-tuple-element.57), channel_id=1, source_target_pairs={{0,16},{4,20},{8,24},{12,28},{1,17},{5,21},{9,25},{13,29},{2,18},{... | collective-permute-start | bytes 196616 | tf_op jit(solution)/shard_map/ppermute | solution.py:432
  23.2 10.1 %collective-permute-start.3 = (bf16[256,128]{1,0:T(8,128)(2,1)}, bf16[256,128]{1,0:T(8,128)(2,1)S(1)}, u32[]{:S(2)}, u32[]{:S(2)}) collective-permute-start(bf16[256,128]{1,0:T(8,128)(2,1)} %get-tuple-element.58), channel_id=1, source_target_pairs={{0,12},{4,16},{8,20},{12,24},{16,28},{1,13},{5,17},{9,21},{13,25},... | collective-permute-start | bytes 196616 | tf_op jit(solution)/shard_map/ppermute | solution.py:432
  25.7 19.8 %collective-permute-start.4 = (bf16[512,128]{1,0:T(8,128)(2,1)}, bf16[512,128]{1,0:T(8,128)(2,1)S(1)}, u32[]{:S(2)}, u32[]{:S(2)}) collective-permute-start(bf16[512,128]{1,0:T(8,128)(2,1)} %get-tuple-element.60), channel_id=1, source_target_pairs={{0,4},{4,8},{8,12},{12,16},{16,20},{20,24},{24,28},{1,5},{5,9},{9,... | collective-permute-start | bytes 393224 | tf_op jit(solution)/shard_map/ppermute | solution.py:432
  27.9 17.6 %collective-permute-start.5 = (bf16[512,128]{1,0:T(8,128)(2,1)}, bf16[512,128]{1,0:T(8,128)(2,1)S(1)}, u32[]{:S(2)}, u32[]{:S(2)}) collective-permute-start(bf16[512,128]{1,0:T(8,128)(2,1)} %get-tuple-element.61), channel_id=1, source_target_pairs={{0,8},{4,12},{8,16},{12,20},{16,24},{20,28},{1,9},{5,13},{9,17},{1... | collective-permute-start | bytes 393224 | tf_op jit(solution)/shard_map/ppermute | solution.py:432
  30.3 15.2 %collective-permute-start.6 = (bf16[512,128]{1,0:T(8,128)(2,1)}, bf16[512,128]{1,0:T(8,128)(2,1)S(1)}, u32[]{:S(2)}, u32[]{:S(2)}) collective-permute-start(bf16[512,128]{1,0:T(8,128)(2,1)} %get-tuple-element.62), channel_id=1, source_target_pairs={{0,28},{1,29},{2,30},{3,31}} | collective-permute-start | bytes 393224 | tf_op jit(solution)/shard_map/ppermute | solution.py:432
  33.3 12.8 %collective-permute-start.9 = (bf16[4,256,128]{2,1,0:T(8,128)(2,1)S(1)}, bf16[4,256,128]{2,1,0:T(8,128)(2,1)S(1)}, u32[]{:S(2)}, u32[]{:S(2)}) collective-permute-start(bf16[4,256,128]{2,1,0:T(8,128)(2,1)S(1)} %pad_maximum_fusion.1.refs_2_), channel_id=1, source_target_pairs={{0,2},{1,3},{2,0},{3,1},{4,6},{5,7},{6,4},{7,5},{8,10},{9,11},{10,... | collective-permute-start | bytes 786440 | tf_op jit(solution)/shard_map/ppermute | solution.py:426
  34.9 1.0 %copy-start = (bf16[2048,128]{1,0:T(8,128)(2,1)S(1)}, bf16[2048,128]{1,0:T(8,128)(2,1)}, u32[]{:S(2)}) copy-start(bf16[2048,128]{1,0:T(8,128)(2,1)} %param.7) | copy-start | bytes 1572868
  35.9 1.0 %copy-start.2 = (bf16[2048,128]{1,0:T(8,128)(2,1)S(1)}, bf16[2048,128]{1,0:T(8,128)(2,1)}, u32[]{:S(2)}) copy-start(bf16[2048,128]{1,0:T(8,128)(2,1)} %param.6) | copy-start | bytes 1572868
  37.0 0.7 copy-start.4
  37.7 1.0 %copy-start.7 = (bf16[2048,1,128]{2,0,1:T(8,128)(2,1)S(1)}, bf16[2048,1,128]{2,0,1:T(8,128)(2,1)}, u32[]{:S(2)}) copy-start(bf16[2048,1,128]{2,0,1:T(8,128)(2,1)} %param.5) | copy-start | bytes 1572868
  38.7 1.0 %copy-start.9 = (bf16[2048,1,128]{2,0,1:T(8,128)(2,1)S(1)}, bf16[2048,1,128]{2,0,1:T(8,128)(2,1)}, u32[]{:S(2)}) copy-start(bf16[2048,1,128]{2,0,1:T(8,128)(2,1)} %param.8) | copy-start | bytes 1572868
  45.6 11.4 %copy-start.1 = (bf16[2048,128]{1,0:T(8,128)(2,1)S(1)}, bf16[2048,128]{1,0:T(8,128)(2,1)}, u32[]{:S(2)}) copy-start(bf16[2048,128]{1,0:T(8,128)(2,1)} %param.7) | copy-start | bytes 1572868
  45.6 11.4 %copy-start.3 = (bf16[2048,128]{1,0:T(8,128)(2,1)S(1)}, bf16[2048,128]{1,0:T(8,128)(2,1)}, u32[]{:S(2)}) copy-start(bf16[2048,128]{1,0:T(8,128)(2,1)} %param.6) | copy-start | bytes 1572868
  45.6 2.2 %collective-permute-start.7 = (bf16[3,512,128]{2,1,0:T(8,128)(2,1)S(1)}, bf16[3,512,128]{2,1,0:T(8,128)(2,1)S(1)}, u32[]{:S(2)}, u32[]{:S(2)}) collective-permute-start(bf16[3,512,128]{2,1,0:T(8,128)(2,1)S(1)} %pad_maximum_fusion.refs_0_), channel_id=1, source_target_pairs={{0,1},{1,0},{2,3},{3,2},{4,5},{5,4},{6,7},{7,6},{8,9},{9,8},{10,11... | collective-permute-start | bytes 1179656 | tf_op jit(solution)/shard_map/ppermute | solution.py:423
  45.7 2.1 %collective-permute-start.8 = (bf16[4,256,128]{2,1,0:T(8,128)(2,1)S(1)}, bf16[4,256,128]{2,1,0:T(8,128)(2,1)S(1)}, u32[]{:S(2)}, u32[]{:S(2)}) collective-permute-start(bf16[4,256,128]{2,1,0:T(8,128)(2,1)S(1)} %pad_maximum_fusion.1.refs_2_), channel_id=1, source_target_pairs={{0,1},{1,0},{2,3},{3,2},{4,5},{5,4},{6,7},{7,6},{8,9},{9,8},{10,11... | collective-permute-start | bytes 786440 | tf_op jit(solution)/shard_map/ppermute | solution.py:423
  46.2 2.0 %collective-permute-start.10 = (bf16[4,256,128]{2,1,0:T(8,128)(2,1)S(1)}, bf16[4,256,128]{2,1,0:T(8,128)(2,1)S(1)}, u32[]{:S(2)}, u32[]{:S(2)}) collective-permute-start(bf16[4,256,128]{2,1,0:T(8,128)(2,1)S(1)} %collective-permute-done.9.refs_4_), channel_id=1, source_target_pairs={{0,1},{1,0},{2,3},{3,2},{4,5},{5,4},{6,7},{7,6},{8,9},{9,8},{10,11... | collective-permute-start | bytes 786440 | tf_op jit(solution)/shard_map/ppermute | solution.py:423
  49.7 2.5 %collective-permute-start.11 = (bf16[7,512,128]{2,1,0:T(8,128)(2,1)S(1)}, bf16[7,512,128]{2,1,0:T(8,128)(2,1)S(1)}, u32[]{:S(2)}, u32[]{:S(2)}) collective-permute-start(bf16[7,512,128]{2,1,0:T(8,128)(2,1)S(1)} %get-tuple-element.70), channel_id=1, source_target_pairs={{0,1},{1,0},{2,3},{3,2},{4,5},{5,4},{6,7},{7,6},{8,9},{9,8},{10,11... | collective-permute-start | bytes 2752520 | tf_op jit(solution)/shard_map/ppermute | solution.py:423
  52.5 24.6 %copy-start.6 = (s32[7]{0:T(128)S(1)}, s32[7]{0:T(128)}, u32[]{:S(2)}) copy-start(s32[7]{0:T(128)} %get-tuple-element.54.asked) | copy-start | bytes 88
  52.5 12.3 %collective-permute-start.13 = (bf16[512,128]{1,0:T(8,128)(2,1)S(1)}, bf16[512,128]{1,0:T(8,128)(2,1)S(1)}, u32[]{:S(2)}, u32[]{:S(2)}) collective-permute-start(bf16[512,128]{1,0:T(8,128)(2,1)S(1)} %get-tuple-element.79), channel_id=1, source_target_pairs={{4,0},{8,4},{12,8},{16,12},{20,16},{24,20},{28,24},{5,1},{9,5},{13... | collective-permute-start | bytes 393224 | tf_op jit(solution)/shard_map/ppermute | solution.py:429
  53.8 11.4 %collective-permute-start.14 = (bf16[512,128]{1,0:T(8,128)(2,1)S(1)}, bf16[512,128]{1,0:T(8,128)(2,1)S(1)}, u32[]{:S(2)}, u32[]{:S(2)}) collective-permute-start(bf16[512,128]{1,0:T(8,128)(2,1)S(1)} %get-tuple-element.80), channel_id=1, source_target_pairs={{8,0},{12,4},{16,8},{20,12},{24,16},{28,20},{9,1},{13,5},{17,9},{2... | collective-permute-start | bytes 393224 | tf_op jit(solution)/shard_map/ppermute | solution.py:429
  55.1 16.7 %collective-permute-start.15 = (bf16[512,128]{1,0:T(8,128)(2,1)S(1)}, bf16[512,128]{1,0:T(8,128)(2,1)S(1)}, u32[]{:S(2)}, u32[]{:S(2)}) collective-permute-start(bf16[512,128]{1,0:T(8,128)(2,1)S(1)} %get-tuple-element.81), channel_id=1, source_target_pairs={{28,0},{29,1},{30,2},{31,3}} | collective-permute-start | bytes 393224 | tf_op jit(solution)/shard_map/ppermute | solution.py:429
  56.4 15.4 %collective-permute-start.12 = (bf16[4,256,128]{2,1,0:T(8,128)(2,1)S(1)}, bf16[4,256,128]{2,1,0:T(8,128)(2,1)S(1)}, u32[]{:S(2)}, u32[]{:S(2)}) collective-permute-start(bf16[4,256,128]{2,1,0:T(8,128)(2,1)S(1)} %get-tuple-element.78), channel_id=1, source_target_pairs={{0,2},{1,3},{2,0},{3,1},{4,6},{5,7},{6,4},{7,5},{8,10},{9,11},{10,... | collective-permute-start | bytes 786440 | tf_op jit(solution)/shard_map/ppermute | solution.py:426
  71.8 5.3 %collective-permute-start.20 = (bf16[4,512,128]{2,1,0:T(8,128)(2,1)S(1)}, bf16[4,512,128]{2,1,0:T(8,128)(2,1)S(1)}, u32[]{:S(2)}, u32[]{:S(2)}) collective-permute-start(bf16[4,512,128]{2,1,0:T(8,128)(2,1)S(1)} %get-tuple-element.91), channel_id=1, source_target_pairs={{0,1},{1,0},{2,3},{3,2},{4,5},{5,4},{6,7},{7,6},{8,9},{9,8},{10,11... | collective-permute-start | bytes 1572872 | tf_op jit(solution)/shard_map/ppermute | solution.py:423
  71.8 8.3 %collective-permute-start.16 = (bf16[256,128]{1,0:T(8,128)(2,1)S(1)}, bf16[256,128]{1,0:T(8,128)(2,1)S(1)}, u32[]{:S(2)}, u32[]{:S(2)}) collective-permute-start(bf16[256,128]{1,0:T(8,128)(2,1)S(1)} %get-tuple-element.86), channel_id=1, source_target_pairs={{24,0},{28,4},{25,1},{29,5},{26,2},{30,6},{27,3},{31,7}} | collective-permute-start | bytes 196616 | tf_op jit(solution)/shard_map/ppermute | solution.py:429
  73.1 10.2 %collective-permute-start.17 = (bf16[256,128]{1,0:T(8,128)(2,1)S(1)}, bf16[256,128]{1,0:T(8,128)(2,1)S(1)}, u32[]{:S(2)}, u32[]{:S(2)}) collective-permute-start(bf16[256,128]{1,0:T(8,128)(2,1)S(1)} %get-tuple-element.87), channel_id=1, source_target_pairs={{20,0},{24,4},{28,8},{21,1},{25,5},{29,9},{22,2},{26,6},{30,10},{2... | collective-permute-start | bytes 196616 | tf_op jit(solution)/shard_map/ppermute | solution.py:429
  74.4 11.3 %collective-permute-start.18 = (bf16[256,128]{1,0:T(8,128)(2,1)S(1)}, bf16[256,128]{1,0:T(8,128)(2,1)S(1)}, u32[]{:S(2)}, u32[]{:S(2)}) collective-permute-start(bf16[256,128]{1,0:T(8,128)(2,1)S(1)} %get-tuple-element.88), channel_id=1, source_target_pairs={{16,0},{20,4},{24,8},{28,12},{17,1},{21,5},{25,9},{29,13},{18,2},{... | collective-permute-start | bytes 196616 | tf_op jit(solution)/shard_map/ppermute | solution.py:429
  75.7 10.0 %collective-permute-start.19 = (bf16[256,128]{1,0:T(8,128)(2,1)S(1)}, bf16[256,128]{1,0:T(8,128)(2,1)S(1)}, u32[]{:S(2)}, u32[]{:S(2)}) collective-permute-start(bf16[256,128]{1,0:T(8,128)(2,1)S(1)} %get-tuple-element.89), channel_id=1, source_target_pairs={{12,0},{16,4},{20,8},{24,12},{28,16},{13,1},{17,5},{21,9},{25,13},... | collective-permute-start | bytes 196616 | tf_op jit(solution)/shard_map/ppermute | solution.py:429
  77.8 8.8 %collective-permute-start.21 = (bf16[4,256,128]{2,1,0:T(8,128)(2,1)S(1)}, bf16[4,256,128]{2,1,0:T(8,128)(2,1)S(1)}, u32[]{:S(2)}, u32[]{:S(2)}) collective-permute-start(bf16[4,256,128]{2,1,0:T(8,128)(2,1)S(1)} %get-tuple-element.96), channel_id=1, source_target_pairs={{0,2},{1,3},{2,0},{3,1},{4,6},{5,7},{6,4},{7,5},{8,10},{9,11},{10,... | collective-permute-start | bytes 786440 | tf_op jit(solution)/shard_map/ppermute | solution.py:426
  86.7 8.0 %collective-permute-start.22 = (bf16[4,256,128]{2,1,0:T(8,128)(2,1)S(1)}, bf16[4,256,128]{2,1,0:T(8,128)(2,1)S(1)}, u32[]{:S(2)}, u32[]{:S(2)}) collective-permute-start(bf16[4,256,128]{2,1,0:T(8,128)(2,1)S(1)} %owner_sum.1.refs_0_), channel_id=1, source_target_pairs={{0,2},{1,3},{2,0},{3,1},{4,6},{5,7},{6,4},{7,5},{8,10},{9,11},{10,... | collective-permute-start | bytes 786440 | tf_op jit(solution)/shard_map/ppermute | solution.py:426
  87.3 7.4 %collective-permute-start.23 = (bf16[4,256,128]{2,1,0:T(8,128)(2,1)S(1)}, bf16[4,256,128]{2,1,0:T(8,128)(2,1)S(1)}, u32[]{:S(2)}, u32[]{:S(2)}) collective-permute-start(bf16[4,256,128]{2,1,0:T(8,128)(2,1)S(1)} %owner_sum.1.refs_0_), channel_id=1, source_target_pairs={{0,1},{1,0},{2,3},{3,2},{4,5},{5,4},{6,7},{7,6},{8,9},{9,8},{10,11... | collective-permute-start | bytes 786440 | tf_op jit(solution)/shard_map/ppermute | solution.py:423
  94.7 1.5 %collective-permute-start.24 = (bf16[4,256,128]{2,1,0:T(8,128)(2,1)S(1)}, bf16[4,256,128]{2,1,0:T(8,128)(2,1)S(1)}, u32[]{:S(2)}, u32[]{:S(2)}) collective-permute-start(bf16[4,256,128]{2,1,0:T(8,128)(2,1)S(1)} %collective-permute-done.22.refs_2_), channel_id=1, source_target_pairs={{0,1},{1,0},{2,3},{3,2},{4,5},{5,4},{6,7},{7,6},{8,9},{9,8},{10,11... | collective-permute-start | bytes 786440 | tf_op jit(solution)/shard_map/ppermute | solution.py:423

commit v7 on v4

--- a/solution.py
+++ b/solution.py
@@ -371,7 +371,7 @@
     factor = scaling * math.log2(math.e)
     shifts = ctx_count - 1
     far = [s for s in reversed(range(shifts - 1)) if 2 * (s + 2) >= ctx_count]
-    near = [s for s in range(shifts) if s not in far]
+    near = [shifts - 1] + [s for s in range(shifts - 1) if s not in far]
 
     q2 = queries.reshape(tok_rows, feature)
     do2 = dout.reshape(tok_rows, feature)

time: 95.7 us -> 95.5 us (level)
  starting transfers between devices: 30.5 us -> 26.8 us
  waiting for transfers between devices: 25.6 us -> 28.3 us
    ppermute x7, waiting for transfers between devices: 13.1 us -> 15.5 us  [to_owner(): lax.ppermute(array, 'ctx', [(c, c - s - 1) for c in range(s + 1, ctx_coun...]
    ppermute x7, starting transfers between devices: 15.3 us -> 13.1 us  [to_reader(): lax.ppermute(array, 'ctx', [(c - s - 1, c) for c in range(s + 1, ctx_coun...]
    ppermute x4, starting transfers between devices: 5.32 us -> 3.86 us  [to_chip(): lax.ppermute(array, 'head', [(h, (h + 2 * d) % heads) for h in range(head...]
  transfers between devices with their start and end apart: 25 -> 25, of which waited for: 11 -> 10; matrix products, arithmetic and copies ran while one was open for 0% -> 0% of each run, Pallas kernels for 18% -> 18%
where the time goes in v7:
time: 95.5 us; the launch traced here: 94.2 us
  waiting for transfers between devices  28.3 us (30%)
  starting transfers between devices  26.8 us (28%)
  Pallas kernels  22.5 us (24%)
  blocking collectives  13.6 us (14%)
  local copies, waits for them, and re-layouts  1.84 us (2%)
    ppermute x7, waiting for transfers between devices, to_owner(): lax.ppermute(array, 'ctx', [(c, c - s - 1) for c in range(s + 1, ctx_coun...  15.5 us
    all_to_all x1, blocking collectives, body(): lax.all_to_all(jnp.broadcast_to(selected.reshape(1, 3 * blocks_here), (ct...  13.6 us
    ppermute x7, starting transfers between devices, to_reader(): lax.ppermute(array, 'ctx', [(c - s - 1, c) for c in range(s + 1, ctx_coun...  13.1 us
    pallas_call x1, Pallas kernels, body(): pl.pallas_call(functools.partial(local_kernel, factor, scaling, blocks_he...  9.44 us
    ppermute x7, starting transfers between devices, to_owner(): lax.ppermute(array, 'ctx', [(c, c - s - 1) for c in range(s + 1, ctx_coun...  9.04 us
    ppermute x4, waiting for transfers between devices, to_chip(): lax.ppermute(array, 'head', [(h, (h + 2 * d) % heads) for h in range(head...  7.05 us
    ppermute x7, waiting for transfers between devices, swap(): return lax.ppermute(array, 'head', [(h, h ^ 1) for h in range(heads)])  5.75 us
    pallas_call x1, Pallas kernels, body(): pl.pallas_call(functools.partial(local_stats_kernel, factor, blocks_here)...  5.74 us
  transfers between devices with their start and end apart: 25, of which 10 were waited for; matrix products, arithmetic and copies ran while one was open for 0% of the time, Pallas kernels for 18%

profile of v7, /device:TPU:0, one launch (start us, length us, event | category | flops | bytes accessed | tf_op | source)
XLA Modules:
  0.0 94.2 jit_solution(1974044738970097530)
XLA Ops:
  0.6 0.8 broadcast_in_dim.7
  1.4 13.6 %all_to_all.8 = s32[8,1,12]{2,1,0:T(1,128)} all-to-all(s32[8,1,12]{2,1,0:T(1,128)S(1)} %broadcast_in_dim.8), channel_id=1, replica_groups=mesh['ctx'=8,'head'=4] {'ctx'}, dimensions={0} | all-to-all | bytes 768 | tf_op jit(solution)/shard_map/all_to_all | solution.py:416
  15.0 3.0 %pick_rows.1 = (s32[7]{0:T(128)}, bf16[512,128]{1,0:T(8,128)(2,1)}, bf16[512,128]{1,0:T(8,128)(2,1)}, bf16[256,128]{1,0:T(8,128)(2,1)}, bf16[256,128]{1,0:T(8,12...) custom-call(s32[8,12]{1,0:T(8,128)} %bitcast.34, ...), custom_call_target="tpu_custom_call" | custom-call | tf_op jit(solution)/shard_map/pick_rows/pallas_call | solution.py:420
  18.1 0.0 copy-start
  18.1 2.7 %collective-permute-start = (bf16[256,128]{1,0:T(8,128)(2,1)}, bf16[256,128]{1,0:T(8,128)(2,1)S(1)}, u32[]{:S(2)}, u32[]{:S(2)}) collective-permute-start(bf16[256,128]{1,0:T(8,128)(2,1)} %get-tuple-element.50), channel_id=1, source_target_pairs={{0,24},{4,28},{1,25},{5,29},{2,26},{6,30},{3,27},{7,31}} | collective-permute-start | bytes 196616 | tf_op jit(solution)/shard_map/ppermute | solution.py:414
  20.7 1.3 %collective-permute-start.1 = (bf16[256,128]{1,0:T(8,128)(2,1)}, bf16[256,128]{1,0:T(8,128)(2,1)S(1)}, u32[]{:S(2)}, u32[]{:S(2)}) collective-permute-start(bf16[256,128]{1,0:T(8,128)(2,1)} %get-tuple-element.51), channel_id=1, source_target_pairs={{0,20},{4,24},{8,28},{1,21},{5,25},{9,29},{2,22},{6,26},{10,30},{3... | collective-permute-start | bytes 196616 | tf_op jit(solution)/shard_map/ppermute | solution.py:414
  22.0 1.3 %collective-permute-start.2 = (bf16[256,128]{1,0:T(8,128)(2,1)}, bf16[256,128]{1,0:T(8,128)(2,1)S(1)}, u32[]{:S(2)}, u32[]{:S(2)}) collective-permute-start(bf16[256,128]{1,0:T(8,128)(2,1)} %get-tuple-element.52), channel_id=1, source_target_pairs={{0,16},{4,20},{8,24},{12,28},{1,17},{5,21},{9,25},{13,29},{2,18},{... | collective-permute-start | bytes 196616 | tf_op jit(solution)/shard_map/ppermute | solution.py:414
  23.3 2.5 %collective-permute-start.3 = (bf16[256,128]{1,0:T(8,128)(2,1)}, bf16[256,128]{1,0:T(8,128)(2,1)S(1)}, u32[]{:S(2)}, u32[]{:S(2)}) collective-permute-start(bf16[256,128]{1,0:T(8,128)(2,1)} %get-tuple-element.53), channel_id=1, source_target_pairs={{0,12},{4,16},{8,20},{12,24},{16,28},{1,13},{5,17},{9,21},{13,25},... | collective-permute-start | bytes 196616 | tf_op jit(solution)/shard_map/ppermute | solution.py:414
  25.8 1.3 %collective-permute-start.4 = (bf16[512,128]{1,0:T(8,128)(2,1)}, bf16[512,128]{1,0:T(8,128)(2,1)S(1)}, u32[]{:S(2)}, u32[]{:S(2)}) collective-permute-start(bf16[512,128]{1,0:T(8,128)(2,1)} %get-tuple-element.55), channel_id=1, source_target_pairs={{0,28},{1,29},{2,30},{3,31}} | collective-permute-start | bytes 393224 | tf_op jit(solution)/shard_map/ppermute | solution.py:414
  27.1 0.0 collective-permute-done
  27.1 1.6 %collective-permute-start.5 = (bf16[512,128]{1,0:T(8,128)(2,1)}, bf16[512,128]{1,0:T(8,128)(2,1)S(1)}, u32[]{:S(2)}, u32[]{:S(2)}) collective-permute-start(bf16[512,128]{1,0:T(8,128)(2,1)} %get-tuple-element.56), channel_id=1, source_target_pairs={{0,4},{4,8},{8,12},{12,16},{16,20},{20,24},{24,28},{1,5},{5,9},{9,... | collective-permute-start | bytes 393224 | tf_op jit(solution)/shard_map/ppermute | solution.py:414
  28.7 0.0 collective-permute-done.1
  28.7 2.5 %collective-permute-start.6 = (bf16[512,128]{1,0:T(8,128)(2,1)}, bf16[512,128]{1,0:T(8,128)(2,1)S(1)}, u32[]{:S(2)}, u32[]{:S(2)}) collective-permute-start(bf16[512,128]{1,0:T(8,128)(2,1)} %get-tuple-element.57), channel_id=1, source_target_pairs={{0,8},{4,12},{8,16},{12,20},{16,24},{20,28},{1,9},{5,13},{9,17},{1... | collective-permute-start | bytes 393224 | tf_op jit(solution)/shard_map/ppermute | solution.py:414
  31.2 0.0 collective-permute-done.2
  31.2 0.0 collective-permute-done.3
  31.3 0.0 copy-start.2
  31.3 1.6 %collective-permute-start.9 = (bf16[4,256,128]{2,1,0:T(8,128)(2,1)S(1)}, bf16[4,256,128]{2,1,0:T(8,128)(2,1)S(1)}, u32[]{:S(2)}, u32[]{:S(2)}) collective-permute-start(bf16[4,256,128]{2,1,0:T(8,128)(2,1)S(1)} %pad_maximum_fusion.1.refs_2_), channel_id=1, source_target_pairs={{0,2},{1,3},{2,0},{3,1},{4,6},{5,7},{6,4},{7,5},{8,10},{9,11},{10,... | collective-permute-start | bytes 786440 | tf_op jit(solution)/shard_map/ppermute | solution.py:408
  32.8 0.0 copy-start.5
  32.9 1.0 %copy-done.5 = bf16[2048,1,128]{2,0,1:T(8,128)(2,1)S(1)} copy-done((bf16[2048,1,128]{2,0,1:T(8,128)(2,1)S(1)}, bf16[2048,1,128]{2,0,1:T(8,128)(2,1)}, u32[]{:S(2)}) %copy-start.5) | copy-done | bytes 524312
  33.9 5.7 %local_stats.1.stats = f32[4,8,512]{2,1,0:T(8,128)S(1)} custom-call(s32[4,3]{1,0:T(4,128)S(1)} %copy-done.2, bf16[2048,128]{1,0:T(8,128)(2,1)S(1)} %bitcast.21, bf16[2048,128]{1,0:T(8,128)(2,1)S(1)} %bitcast.24, bf16[4,512,128]{2,1,0:T(8,128)(2,1)S(1)} %bitcast.16, bf16[4,512,128]{2,1,0:T(8,128)(2,1)S(1)} %bitcast.19), custom_call_target="tpu_custom_call" | custom-call | flops 2013265920 | bytes 2097152 | tf_op jit(solution)/shard_map/local_stats/pallas_call | solution.py:434
  39.6 0.0 copy-start.6
  39.7 0.0 collective-permute-done.4
  39.7 0.0 collective-permute-done.5
  39.7 0.0 collective-permute-done.6
  39.7 0.1 collective-permute-start.7
  39.8 0.5 collective-permute-start.8
  40.3 0.0 collective-permute-done.9.refs_4_
  40.3 0.1 collective-permute-start.10
  40.4 1.5 %collective-permute-done.8.refs_3_ = bf16[4,256,128]{2,1,0:T(8,128)(2,1)S(1)} collective-permute-done((bf16[4,256,128]{2,1,0:T(8,128)(2,1)S(1)}, bf16[4,256,128]{2,1,0:T(8,128)(2,1)S(1)}, u32[]{:S(2)}, u32[]{:S(2)}) %collective-permute-start.8) | collective-permute-done | bytes 262176 | tf_op jit(solution)/shard_map/ppermute | solution.py:405
  41.9 0.0 collective-permute-done.7.refs_1_
  41.9 0.4 collective-permute-done.10.refs_5_
  42.3 1.6 %remote_pairs.1 = (bf16[7,512,128]{2,1,0:T(8,128)(2,1)S(1)}, bf16[7,512,128]{2,1,0:T(8,128)(2,1)S(1)}, f32[4,8,512]{2,1,0:T(8,128)S(1)}, f32[4,128,512]{2,1,0:T(8,128)S(1)}) custom-call(s32[4,3]{1,0:T(4,128)S(1)} %copy-done.2, bf16[2048,128]{1,0:T(8,128)(2,1)S(1)} %bitcast.22, bf16[2048,128]{1,0:T(8,128)(2,1)S(1)} %bitcast.25, ...), custom_call_target="tpu_custom_call" | custom-call | flops 4026531840 | bytes 4194304 | tf_op jit(solution)/shard_map/remote_pairs/pallas_call | solution.py:450
  43.9 0.2 collective-permute-start.11
  44.1 2.3 %collective-permute-done.11.theirs = bf16[7,512,128]{2,1,0:T(8,128)(2,1)S(1)} collective-permute-done((bf16[7,512,128]{2,1,0:T(8,128)(2,1)S(1)}, bf16[7,512,128]{2,1,0:T(8,128)(2,1)S(1)}, u32[]{:S(2)}, u32[]{:S(2)}) %collective-permute-start.11) | collective-permute-done | bytes 917536 | tf_op jit(solution)/shard_map/ppermute | solution.py:405
  46.4 0.2 chip_sum.1
  46.6 1.3 %collective-permute-start.13 = (bf16[512,128]{1,0:T(8,128)(2,1)S(1)}, bf16[512,128]{1,0:T(8,128)(2,1)S(1)}, u32[]{:S(2)}, u32[]{:S(2)}) collective-permute-start(bf16[512,128]{1,0:T(8,128)(2,1)S(1)} %get-tuple-element.78), channel_id=1, source_target_pairs={{28,0},{29,1},{30,2},{31,3}} | collective-permute-start | bytes 393224 | tf_op jit(solution)/shard_map/ppermute | solution.py:411
  47.9 1.3 %collective-permute-start.14 = (bf16[512,128]{1,0:T(8,128)(2,1)S(1)}, bf16[512,128]{1,0:T(8,128)(2,1)S(1)}, u32[]{:S(2)}, u32[]{:S(2)}) collective-permute-start(bf16[512,128]{1,0:T(8,128)(2,1)S(1)} %get-tuple-element.79), channel_id=1, source_target_pairs={{4,0},{8,4},{12,8},{16,12},{20,16},{24,20},{28,24},{5,1},{9,5},{13... | collective-permute-start | bytes 393224 | tf_op jit(solution)/shard_map/ppermute | solution.py:411
  49.2 1.3 %collective-permute-start.15 = (bf16[512,128]{1,0:T(8,128)(2,1)S(1)}, bf16[512,128]{1,0:T(8,128)(2,1)S(1)}, u32[]{:S(2)}, u32[]{:S(2)}) collective-permute-start(bf16[512,128]{1,0:T(8,128)(2,1)S(1)} %get-tuple-element.80), channel_id=1, source_target_pairs={{8,0},{12,4},{16,8},{20,12},{24,16},{28,20},{9,1},{13,5},{17,9},{2... | collective-permute-start | bytes 393224 | tf_op jit(solution)/shard_map/ppermute | solution.py:411
  50.5 0.7 collective-permute-start.12
  51.2 9.4 %local_pairs.1 = (bf16[4,512,128]{2,1,0:T(8,128)(2,1)S(1)}, bf16[4,512,128]{2,1,0:T(8,128)(2,1)S(1)}, bf16[2048,128]{1,0:T(8,128)(2,1)}) custom-call(s32[4,3]{1,0:T(4,128)S(1)} %copy-done.2, bf16[2048,128]{1,0:T(8,128)(2,1)S(1)} %bitcast.23, bf16[2048,128]{1,0:T(8,128)(2,1)S(1)} %bitcast.26, bf16[4,512,128]{2,1,0:T(8,128)(2,1)S(1)} %bitcast.17, ...), custom_call_target="tpu_custom_call" | custom-call | flops 4026531840 | bytes 4194304 | tf_op jit(solution)/shard_map/local_pairs/pallas_call | solution.py:493
  60.6 2.6 %collective-permute-done.13.refs_0_ = bf16[512,128]{1,0:T(8,128)(2,1)S(1)} collective-permute-done((bf16[512,128]{1,0:T(8,128)(2,1)S(1)}, bf16[512,128]{1,0:T(8,128)(2,1)S(1)}, u32[]{:S(2)}, u32[]{:S(2)}) %collective-permute-start.13) | collective-permute-done | bytes 131104 | tf_op jit(solution)/shard_map/ppermute | solution.py:411
  63.2 0.0 collective-permute-done.14.refs_1_
  63.2 1.5 %collective-permute-done.15.refs_2_ = bf16[512,128]{1,0:T(8,128)(2,1)S(1)} collective-permute-done((bf16[512,128]{1,0:T(8,128)(2,1)S(1)}, bf16[512,128]{1,0:T(8,128)(2,1)S(1)}, u32[]{:S(2)}, u32[]{:S(2)}) %collective-permute-start.15) | collective-permute-done | bytes 131104 | tf_op jit(solution)/shard_map/ppermute | solution.py:411
  64.7 0.0 collective-permute-done.12.refs_0_
  64.7 0.0 collective-permute-start.20
  64.8 1.3 %collective-permute-start.16 = (bf16[256,128]{1,0:T(8,128)(2,1)S(1)}, bf16[256,128]{1,0:T(8,128)(2,1)S(1)}, u32[]{:S(2)}, u32[]{:S(2)}) collective-permute-start(bf16[256,128]{1,0:T(8,128)(2,1)S(1)} %get-tuple-element.84), channel_id=1, source_target_pairs={{24,0},{28,4},{25,1},{29,5},{26,2},{30,6},{27,3},{31,7}} | collective-permute-start | bytes 196616 | tf_op jit(solution)/shard_map/ppermute | solution.py:411
  66.1 1.3 %collective-permute-start.17 = (bf16[256,128]{1,0:T(8,128)(2,1)S(1)}, bf16[256,128]{1,0:T(8,128)(2,1)S(1)}, u32[]{:S(2)}, u32[]{:S(2)}) collective-permute-start(bf16[256,128]{1,0:T(8,128)(2,1)S(1)} %get-tuple-element.85), channel_id=1, source_target_pairs={{20,0},{24,4},{28,8},{21,1},{25,5},{29,9},{22,2},{26,6},{30,10},{2... | collective-permute-start | bytes 196616 | tf_op jit(solution)/shard_map/ppermute | solution.py:411
  67.4 1.3 %collective-permute-start.18 = (bf16[256,128]{1,0:T(8,128)(2,1)S(1)}, bf16[256,128]{1,0:T(8,128)(2,1)S(1)}, u32[]{:S(2)}, u32[]{:S(2)}) collective-permute-start(bf16[256,128]{1,0:T(8,128)(2,1)S(1)} %get-tuple-element.86), channel_id=1, source_target_pairs={{16,0},{20,4},{24,8},{28,12},{17,1},{21,5},{25,9},{29,13},{18,2},{... | collective-permute-start | bytes 196616 | tf_op jit(solution)/shard_map/ppermute | solution.py:411
  68.7 1.3 %collective-permute-start.19 = (bf16[256,128]{1,0:T(8,128)(2,1)S(1)}, bf16[256,128]{1,0:T(8,128)(2,1)S(1)}, u32[]{:S(2)}, u32[]{:S(2)}) collective-permute-start(bf16[256,128]{1,0:T(8,128)(2,1)S(1)} %get-tuple-element.87), channel_id=1, source_target_pairs={{12,0},{16,4},{20,8},{24,12},{28,16},{13,1},{17,5},{21,9},{25,13},... | collective-permute-start | bytes 196616 | tf_op jit(solution)/shard_map/ppermute | solution.py:411
  70.0 0.0 collective-permute-done.20.theirs
  70.0 0.8 own_sum.1
  70.8 0.7 collective-permute-start.21
  71.5 6.7 %collective-permute-done.16.refs_0_ = bf16[256,128]{1,0:T(8,128)(2,1)S(1)} collective-permute-done((bf16[256,128]{1,0:T(8,128)(2,1)S(1)}, bf16[256,128]{1,0:T(8,128)(2,1)S(1)}, u32[]{:S(2)}, u32[]{:S(2)}) %collective-permute-start.16) | collective-permute-done | bytes 65568 | tf_op jit(solution)/shard_map/ppermute | solution.py:411
  78.2 4.3 %collective-permute-done.17.refs_1_ = bf16[256,128]{1,0:T(8,128)(2,1)S(1)} collective-permute-done((bf16[256,128]{1,0:T(8,128)(2,1)S(1)}, bf16[256,128]{1,0:T(8,128)(2,1)S(1)}, u32[]{:S(2)}, u32[]{:S(2)}) %collective-permute-start.17) | collective-permute-done | bytes 65568 | tf_op jit(solution)/shard_map/ppermute | solution.py:411
  82.5 0.3 collective-permute-done.18.refs_2_
  82.9 0.0 collective-permute-done.19.refs_3_
  82.9 0.6 far_returns.1.returned
  83.5 0.1 owner_sum.1.refs_0_
  83.6 1.0 %collective-permute-start.23 = (bf16[4,256,128]{2,1,0:T(8,128)(2,1)S(1)}, bf16[4,256,128]{2,1,0:T(8,128)(2,1)S(1)}, u32[]{:S(2)}, u32[]{:S(2)}) collective-permute-start(bf16[4,256,128]{2,1,0:T(8,128)(2,1)S(1)} %owner_sum.1.refs_0_), channel_id=1, source_target_pairs={{0,2},{1,3},{2,0},{3,1},{4,6},{5,7},{6,4},{7,5},{8,10},{9,11},{10,... | collective-permute-start | bytes 786440 | tf_op jit(solution)/shard_map/ppermute | solution.py:408
  84.6 7.0 %collective-permute-done.23.refs_2_ = bf16[4,256,128]{2,1,0:T(8,128)(2,1)S(1)} collective-permute-done((bf16[4,256,128]{2,1,0:T(8,128)(2,1)S(1)}, bf16[4,256,128]{2,1,0:T(8,128)(2,1)S(1)}, u32[]{:S(2)}, u32[]{:S(2)}) %collective-permute-start.23) | collective-permute-done | bytes 262176 | tf_op jit(solution)/shard_map/ppermute | solution.py:408
  91.6 0.0 collective-permute-start.24
  91.6 0.0 collective-permute-done.22.refs_1_
  91.6 1.5 %collective-permute-done.24.refs_3_ = bf16[4,256,128]{2,1,0:T(8,128)(2,1)S(1)} collective-permute-done((bf16[4,256,128]{2,1,0:T(8,128)(2,1)S(1)}, bf16[4,256,128]{2,1,0:T(8,128)(2,1)S(1)}, u32[]{:S(2)}, u32[]{:S(2)}) %collective-permute-start.24) | collective-permute-done | bytes 262176 | tf_op jit(solution)/shard_map/ppermute | solution.py:405
  93.2 1.0 %spread.1 = (bf16[4,512,128]{2,1,0:T(8,128)(2,1)}, bf16[4,512,128]{2,1,0:T(8,128)(2,1)}) custom-call(bf16[4,256,128]{2,1,0:T(8,128)(2,1)S(1)} %owner_sum.1.refs_0_, bf16[4,256,128]{2,1,0:T(8,128)(2,1)S(1)} %collective-permute-done.22.refs_1_, bf16[4,256,128]{2,1,0:T(8,128)(2,1)S(1)} %collective-permute-done.23.refs_2_, ...), custom_call_target="tpu_custom_call" | custom-call | tf_op jit(solution)/shard_map/spread/pallas_call | solution.py:543
  (15 shorter events, 0.2 us)
Async XLA Ops:
  15.0 17.8 %copy-start.1 = (bf16[2048,128]{1,0:T(8,128)(2,1)S(1)}, bf16[2048,128]{1,0:T(8,128)(2,1)}, u32[]{:S(2)}) copy-start(bf16[2048,128]{1,0:T(8,128)(2,1)} %param.7) | copy-start | bytes 1572868
  15.0 17.8 %copy-start.4 = (bf16[2048,1,128]{2,0,1:T(8,128)(2,1)S(1)}, bf16[2048,1,128]{2,0,1:T(8,128)(2,1)}, u32[]{:S(2)}) copy-start(bf16[2048,1,128]{2,0,1:T(8,128)(2,1)} %param.5) | copy-start | bytes 1572868
  18.1 14.8 %copy-start = (bf16[2048,128]{1,0:T(8,128)(2,1)S(1)}, bf16[2048,128]{1,0:T(8,128)(2,1)}, u32[]{:S(2)}) copy-start(bf16[2048,128]{1,0:T(8,128)(2,1)} %param.6) | copy-start | bytes 1572868
  18.1 9.0 %collective-permute-start = (bf16[256,128]{1,0:T(8,128)(2,1)}, bf16[256,128]{1,0:T(8,128)(2,1)S(1)}, u32[]{:S(2)}, u32[]{:S(2)}) collective-permute-start(bf16[256,128]{1,0:T(8,128)(2,1)} %get-tuple-element.50), channel_id=1, source_target_pairs={{0,24},{4,28},{1,25},{5,29},{2,26},{6,30},{3,27},{7,31}} | collective-permute-start | bytes 196616 | tf_op jit(solution)/shard_map/ppermute | solution.py:414
  20.7 8.0 %collective-permute-start.1 = (bf16[256,128]{1,0:T(8,128)(2,1)}, bf16[256,128]{1,0:T(8,128)(2,1)S(1)}, u32[]{:S(2)}, u32[]{:S(2)}) collective-permute-start(bf16[256,128]{1,0:T(8,128)(2,1)} %get-tuple-element.51), channel_id=1, source_target_pairs={{0,20},{4,24},{8,28},{1,21},{5,25},{9,29},{2,22},{6,26},{10,30},{3... | collective-permute-start | bytes 196616 | tf_op jit(solution)/shard_map/ppermute | solution.py:414
  22.0 9.2 %collective-permute-start.2 = (bf16[256,128]{1,0:T(8,128)(2,1)}, bf16[256,128]{1,0:T(8,128)(2,1)S(1)}, u32[]{:S(2)}, u32[]{:S(2)}) collective-permute-start(bf16[256,128]{1,0:T(8,128)(2,1)} %get-tuple-element.52), channel_id=1, source_target_pairs={{0,16},{4,20},{8,24},{12,28},{1,17},{5,21},{9,25},{13,29},{2,18},{... | collective-permute-start | bytes 196616 | tf_op jit(solution)/shard_map/ppermute | solution.py:414
  23.3 7.9 %collective-permute-start.3 = (bf16[256,128]{1,0:T(8,128)(2,1)}, bf16[256,128]{1,0:T(8,128)(2,1)S(1)}, u32[]{:S(2)}, u32[]{:S(2)}) collective-permute-start(bf16[256,128]{1,0:T(8,128)(2,1)} %get-tuple-element.53), channel_id=1, source_target_pairs={{0,12},{4,16},{8,20},{12,24},{16,28},{1,13},{5,17},{9,21},{13,25},... | collective-permute-start | bytes 196616 | tf_op jit(solution)/shard_map/ppermute | solution.py:414
  25.8 13.8 %collective-permute-start.4 = (bf16[512,128]{1,0:T(8,128)(2,1)}, bf16[512,128]{1,0:T(8,128)(2,1)S(1)}, u32[]{:S(2)}, u32[]{:S(2)}) collective-permute-start(bf16[512,128]{1,0:T(8,128)(2,1)} %get-tuple-element.55), channel_id=1, source_target_pairs={{0,28},{1,29},{2,30},{3,31}} | collective-permute-start | bytes 393224 | tf_op jit(solution)/shard_map/ppermute | solution.py:414
  27.1 12.5 %collective-permute-start.5 = (bf16[512,128]{1,0:T(8,128)(2,1)}, bf16[512,128]{1,0:T(8,128)(2,1)S(1)}, u32[]{:S(2)}, u32[]{:S(2)}) collective-permute-start(bf16[512,128]{1,0:T(8,128)(2,1)} %get-tuple-element.56), channel_id=1, source_target_pairs={{0,4},{4,8},{8,12},{12,16},{16,20},{20,24},{24,28},{1,5},{5,9},{9,... | collective-permute-start | bytes 393224 | tf_op jit(solution)/shard_map/ppermute | solution.py:414
  28.7 11.0 %collective-permute-start.6 = (bf16[512,128]{1,0:T(8,128)(2,1)}, bf16[512,128]{1,0:T(8,128)(2,1)S(1)}, u32[]{:S(2)}, u32[]{:S(2)}) collective-permute-start(bf16[512,128]{1,0:T(8,128)(2,1)} %get-tuple-element.57), channel_id=1, source_target_pairs={{0,8},{4,12},{8,16},{12,20},{16,24},{20,28},{1,9},{5,13},{9,17},{1... | collective-permute-start | bytes 393224 | tf_op jit(solution)/shard_map/ppermute | solution.py:414
  31.3 1.6 %copy-start.2 = (s32[4,3]{1,0:T(4,128)S(1)}, s32[4,3]{1,0:T(4,128)}, u32[]{:S(2)}) copy-start(s32[4,3]{1,0:T(4,128)} %chosen.2) | copy-start | bytes 148
  31.3 9.0 %collective-permute-start.9 = (bf16[4,256,128]{2,1,0:T(8,128)(2,1)S(1)}, bf16[4,256,128]{2,1,0:T(8,128)(2,1)S(1)}, u32[]{:S(2)}, u32[]{:S(2)}) collective-permute-start(bf16[4,256,128]{2,1,0:T(8,128)(2,1)S(1)} %pad_maximum_fusion.1.refs_2_), channel_id=1, source_target_pairs={{0,2},{1,3},{2,0},{3,1},{4,6},{5,7},{6,4},{7,5},{8,10},{9,11},{10,... | collective-permute-start | bytes 786440 | tf_op jit(solution)/shard_map/ppermute | solution.py:408
  32.8 1.0 %copy-start.5 = (bf16[2048,1,128]{2,0,1:T(8,128)(2,1)S(1)}, bf16[2048,1,128]{2,0,1:T(8,128)(2,1)}, u32[]{:S(2)}) copy-start(bf16[2048,1,128]{2,0,1:T(8,128)(2,1)} %param.8) | copy-start | bytes 1572868
  39.6 2.6 %copy-start.6 = (bf16[2048,1,128]{2,0,1:T(8,128)(2,1)S(1)}, bf16[2048,1,128]{2,0,1:T(8,128)(2,1)}, u32[]{:S(2)}) copy-start(bf16[2048,1,128]{2,0,1:T(8,128)(2,1)} %param.8) | copy-start | bytes 1572868
  39.7 2.2 %collective-permute-start.7 = (bf16[3,512,128]{2,1,0:T(8,128)(2,1)S(1)}, bf16[3,512,128]{2,1,0:T(8,128)(2,1)S(1)}, u32[]{:S(2)}, u32[]{:S(2)}) collective-permute-start(bf16[3,512,128]{2,1,0:T(8,128)(2,1)S(1)} %pad_maximum_fusion.refs_0_), channel_id=1, source_target_pairs={{0,1},{1,0},{2,3},{3,2},{4,5},{5,4},{6,7},{7,6},{8,9},{9,8},{10,11... | collective-permute-start | bytes 1179656 | tf_op jit(solution)/shard_map/ppermute | solution.py:405
  39.8 2.1 %collective-permute-start.8 = (bf16[4,256,128]{2,1,0:T(8,128)(2,1)S(1)}, bf16[4,256,128]{2,1,0:T(8,128)(2,1)S(1)}, u32[]{:S(2)}, u32[]{:S(2)}) collective-permute-start(bf16[4,256,128]{2,1,0:T(8,128)(2,1)S(1)} %pad_maximum_fusion.1.refs_2_), channel_id=1, source_target_pairs={{0,1},{1,0},{2,3},{3,2},{4,5},{5,4},{6,7},{7,6},{8,9},{9,8},{10,11... | collective-permute-start | bytes 786440 | tf_op jit(solution)/shard_map/ppermute | solution.py:405
  40.3 2.0 %collective-permute-start.10 = (bf16[4,256,128]{2,1,0:T(8,128)(2,1)S(1)}, bf16[4,256,128]{2,1,0:T(8,128)(2,1)S(1)}, u32[]{:S(2)}, u32[]{:S(2)}) collective-permute-start(bf16[4,256,128]{2,1,0:T(8,128)(2,1)S(1)} %collective-permute-done.9.refs_4_), channel_id=1, source_target_pairs={{0,1},{1,0},{2,3},{3,2},{4,5},{5,4},{6,7},{7,6},{8,9},{9,8},{10,11... | collective-permute-start | bytes 786440 | tf_op jit(solution)/shard_map/ppermute | solution.py:405
  43.9 2.5 %collective-permute-start.11 = (bf16[7,512,128]{2,1,0:T(8,128)(2,1)S(1)}, bf16[7,512,128]{2,1,0:T(8,128)(2,1)S(1)}, u32[]{:S(2)}, u32[]{:S(2)}) collective-permute-start(bf16[7,512,128]{2,1,0:T(8,128)(2,1)S(1)} %get-tuple-element.65), channel_id=1, source_target_pairs={{0,1},{1,0},{2,3},{3,2},{4,5},{5,4},{6,7},{7,6},{8,9},{9,8},{10,11... | collective-permute-start | bytes 2752520 | tf_op jit(solution)/shard_map/ppermute | solution.py:405
  46.6 16.6 %collective-permute-start.13 = (bf16[512,128]{1,0:T(8,128)(2,1)S(1)}, bf16[512,128]{1,0:T(8,128)(2,1)S(1)}, u32[]{:S(2)}, u32[]{:S(2)}) collective-permute-start(bf16[512,128]{1,0:T(8,128)(2,1)S(1)} %get-tuple-element.78), channel_id=1, source_target_pairs={{28,0},{29,1},{30,2},{31,3}} | collective-permute-start | bytes 393224 | tf_op jit(solution)/shard_map/ppermute | solution.py:411
  47.9 15.3 %collective-permute-start.14 = (bf16[512,128]{1,0:T(8,128)(2,1)S(1)}, bf16[512,128]{1,0:T(8,128)(2,1)S(1)}, u32[]{:S(2)}, u32[]{:S(2)}) collective-permute-start(bf16[512,128]{1,0:T(8,128)(2,1)S(1)} %get-tuple-element.79), channel_id=1, source_target_pairs={{4,0},{8,4},{12,8},{16,12},{20,16},{24,20},{28,24},{5,1},{9,5},{13... | collective-permute-start | bytes 393224 | tf_op jit(solution)/shard_map/ppermute | solution.py:411
  49.2 15.5 %collective-permute-start.15 = (bf16[512,128]{1,0:T(8,128)(2,1)S(1)}, bf16[512,128]{1,0:T(8,128)(2,1)S(1)}, u32[]{:S(2)}, u32[]{:S(2)}) collective-permute-start(bf16[512,128]{1,0:T(8,128)(2,1)S(1)} %get-tuple-element.80), channel_id=1, source_target_pairs={{8,0},{12,4},{16,8},{20,12},{24,16},{28,20},{9,1},{13,5},{17,9},{2... | collective-permute-start | bytes 393224 | tf_op jit(solution)/shard_map/ppermute | solution.py:411
  50.5 14.3 %collective-permute-start.12 = (bf16[4,256,128]{2,1,0:T(8,128)(2,1)S(1)}, bf16[4,256,128]{2,1,0:T(8,128)(2,1)S(1)}, u32[]{:S(2)}, u32[]{:S(2)}) collective-permute-start(bf16[4,256,128]{2,1,0:T(8,128)(2,1)S(1)} %get-tuple-element.77), channel_id=1, source_target_pairs={{0,2},{1,3},{2,0},{3,1},{4,6},{5,7},{6,4},{7,5},{8,10},{9,11},{10,... | collective-permute-start | bytes 786440 | tf_op jit(solution)/shard_map/ppermute | solution.py:408
  64.7 5.3 %collective-permute-start.20 = (bf16[4,512,128]{2,1,0:T(8,128)(2,1)S(1)}, bf16[4,512,128]{2,1,0:T(8,128)(2,1)S(1)}, u32[]{:S(2)}, u32[]{:S(2)}) collective-permute-start(bf16[4,512,128]{2,1,0:T(8,128)(2,1)S(1)} %get-tuple-element.89), channel_id=1, source_target_pairs={{0,1},{1,0},{2,3},{3,2},{4,5},{5,4},{6,7},{7,6},{8,9},{9,8},{10,11... | collective-permute-start | bytes 1572872 | tf_op jit(solution)/shard_map/ppermute | solution.py:405
  64.8 13.4 %collective-permute-start.16 = (bf16[256,128]{1,0:T(8,128)(2,1)S(1)}, bf16[256,128]{1,0:T(8,128)(2,1)S(1)}, u32[]{:S(2)}, u32[]{:S(2)}) collective-permute-start(bf16[256,128]{1,0:T(8,128)(2,1)S(1)} %get-tuple-element.84), channel_id=1, source_target_pairs={{24,0},{28,4},{25,1},{29,5},{26,2},{30,6},{27,3},{31,7}} | collective-permute-start | bytes 196616 | tf_op jit(solution)/shard_map/ppermute | solution.py:411
  66.1 16.4 %collective-permute-start.17 = (bf16[256,128]{1,0:T(8,128)(2,1)S(1)}, bf16[256,128]{1,0:T(8,128)(2,1)S(1)}, u32[]{:S(2)}, u32[]{:S(2)}) collective-permute-start(bf16[256,128]{1,0:T(8,128)(2,1)S(1)} %get-tuple-element.85), channel_id=1, source_target_pairs={{20,0},{24,4},{28,8},{21,1},{25,5},{29,9},{22,2},{26,6},{30,10},{2... | collective-permute-start | bytes 196616 | tf_op jit(solution)/shard_map/ppermute | solution.py:411
  67.4 15.5 %collective-permute-start.18 = (bf16[256,128]{1,0:T(8,128)(2,1)S(1)}, bf16[256,128]{1,0:T(8,128)(2,1)S(1)}, u32[]{:S(2)}, u32[]{:S(2)}) collective-permute-start(bf16[256,128]{1,0:T(8,128)(2,1)S(1)} %get-tuple-element.86), channel_id=1, source_target_pairs={{16,0},{20,4},{24,8},{28,12},{17,1},{21,5},{25,9},{29,13},{18,2},{... | collective-permute-start | bytes 196616 | tf_op jit(solution)/shard_map/ppermute | solution.py:411
  68.7 1.3 %copy-start.3 = (s32[7]{0:T(128)S(1)}, s32[7]{0:T(128)}, u32[]{:S(2)}) copy-start(s32[7]{0:T(128)} %get-tuple-element.75.asked) | copy-start | bytes 88
  68.7 14.2 %collective-permute-start.19 = (bf16[256,128]{1,0:T(8,128)(2,1)S(1)}, bf16[256,128]{1,0:T(8,128)(2,1)S(1)}, u32[]{:S(2)}, u32[]{:S(2)}) collective-permute-start(bf16[256,128]{1,0:T(8,128)(2,1)S(1)} %get-tuple-element.87), channel_id=1, source_target_pairs={{12,0},{16,4},{20,8},{24,12},{28,16},{13,1},{17,5},{21,9},{25,13},... | collective-permute-start | bytes 196616 | tf_op jit(solution)/shard_map/ppermute | solution.py:411
  70.8 12.7 %collective-permute-start.21 = (bf16[4,256,128]{2,1,0:T(8,128)(2,1)S(1)}, bf16[4,256,128]{2,1,0:T(8,128)(2,1)S(1)}, u32[]{:S(2)}, u32[]{:S(2)}) collective-permute-start(bf16[4,256,128]{2,1,0:T(8,128)(2,1)S(1)} %get-tuple-element.94), channel_id=1, source_target_pairs={{0,2},{1,3},{2,0},{3,1},{4,6},{5,7},{6,4},{7,5},{8,10},{9,11},{10,... | collective-permute-start | bytes 786440 | tf_op jit(solution)/shard_map/ppermute | solution.py:408
  83.6 8.0 %collective-permute-start.23 = (bf16[4,256,128]{2,1,0:T(8,128)(2,1)S(1)}, bf16[4,256,128]{2,1,0:T(8,128)(2,1)S(1)}, u32[]{:S(2)}, u32[]{:S(2)}) collective-permute-start(bf16[4,256,128]{2,1,0:T(8,128)(2,1)S(1)} %owner_sum.1.refs_0_), channel_id=1, source_target_pairs={{0,2},{1,3},{2,0},{3,1},{4,6},{5,7},{6,4},{7,5},{8,10},{9,11},{10,... | collective-permute-start | bytes 786440 | tf_op jit(solution)/shard_map/ppermute | solution.py:408
  84.6 7.0 %collective-permute-start.22 = (bf16[4,256,128]{2,1,0:T(8,128)(2,1)S(1)}, bf16[4,256,128]{2,1,0:T(8,128)(2,1)S(1)}, u32[]{:S(2)}, u32[]{:S(2)}) collective-permute-start(bf16[4,256,128]{2,1,0:T(8,128)(2,1)S(1)} %owner_sum.1.refs_0_), channel_id=1, source_target_pairs={{0,1},{1,0},{2,3},{3,2},{4,5},{5,4},{6,7},{7,6},{8,9},{9,8},{10,11... | collective-permute-start | bytes 786440 | tf_op jit(solution)/shard_map/ppermute | solution.py:405
  91.6 1.5 %collective-permute-start.24 = (bf16[4,256,128]{2,1,0:T(8,128)(2,1)S(1)}, bf16[4,256,128]{2,1,0:T(8,128)(2,1)S(1)}, u32[]{:S(2)}, u32[]{:S(2)}) collective-permute-start(bf16[4,256,128]{2,1,0:T(8,128)(2,1)S(1)} %collective-permute-done.23.refs_2_), channel_id=1, source_target_pairs={{0,1},{1,0},{2,3},{3,2},{4,5},{5,4},{6,7},{7,6},{8,9},{9,8},{10,11... | collective-permute-start | bytes 786440 | tf_op jit(solution)/shard_map/ppermute | solution.py:405
